TPU v7x, 32 devices: a whole 2x2x4 slice. The times are simulated.
32 devices in a mesh: tp: 2 (over core), ep: 16 (over z, y, x).
Axes of the slice: x: 2, y: 2, z: 4, core: 2. Of those that a mesh axis runs over, the one named last changes fastest.
Arguments:
- hidden_in: bfloat16 [2048, 7168], P('ep', 'tp'), may hold values from -6 to 6
- query: bfloat16 [2048, 2048], P('ep', 'tp'), may hold values from -6 to 6
- key_in: bfloat16 [2048, 2048], P('ep', 'tp'), may hold values from -6 to 6
- value_in: bfloat16 [2048, 2048], P('ep', 'tp'), may hold values from -6 to 6
- out_weight: bfloat16 [2048, 7168], P(None, ('tp', 'ep')), may hold values from -0.125 to 0.125
- norm_gain: bfloat16 [7168], P('tp'), may hold values from 0.5 to 1.5
- router: bfloat16 [7168, 16], P('tp'), may hold values from -0.0625 to 0.0625
- routes: int32 [2048, 8], P('ep'), may hold values from 0 to 15, all different within a row; in each aligned block of 128 rows (0 to 127, 128 to 255, ...) at most 80 rows name the same one
- w_gate: bfloat16 [16, 7168, 1024], P('ep', 'tp'), may hold values from -0.0625 to 0.0625
- w_up: bfloat16 [16, 7168, 1024], P('ep', 'tp'), may hold values from -0.0625 to 0.0625
- w_down: bfloat16 [16, 1024, 7168], P('ep', None, 'tp'), may hold values from -0.1875 to 0.1875
- grad_out: bfloat16 [2048, 7168], P('ep', 'tp'), may hold values from -6 to 6
Outputs:
- grad_in: bfloat16 [2048, 7168], P('ep', 'tp')
- grad_query: bfloat16 [2048, 2048], P('ep', 'tp')
- grad_key: bfloat16 [2048, 2048], P('ep', 'tp')
- grad_value: bfloat16 [2048, 2048], P('ep', 'tp')
Inputs may be any that keep to these rules, and one draw needn't show every extreme that they name: `routes`: each row names 8 different experts. Among the 128 rows of one sequence at most 80 name the same expert, and in every draw some expert is named by exactly 80 rows of some sequence.
All inputs are finite; a program needn't handle non-finite values.
Results may differ from a plain program's by a relative error of at most 0.025.
Values may be sent and summed in bfloat16 or wider, within the bound.
No kernel may reach another device: no remote copies, remote signals or barrier semaphores. Data moves between devices by JAX's collectives and lax.ppermute only.
A program may use at most 192 MiB of HBM per device.

v0:
```python
import math

import jax
import jax.numpy as jnp
from jax import lax
from jax.sharding import PartitionSpec as P

D = 7168
HDIM = 128
TOP = 8


route_scale = 2.5
norm_eps = 1e-06
masked_score = -1e30


def split_heads(values):
    return values.reshape(values.shape[0], values.shape[1] // HDIM, HDIM)


def softmax_rows(query_h, key_h):
    length = query_h.shape[0]
    scores = jnp.einsum("qhd,khd->hqk", query_h, key_h, preferred_element_type=jnp.float32) * (
        1.0 / math.sqrt(HDIM)
    )
    causal = jnp.arange(length)[None, :] <= jnp.arange(length)[:, None]
    scores = jnp.where(causal[None], scores, masked_score)
    highest = jnp.max(scores, axis=2, keepdims=True)
    weights_exp = jnp.exp(scores - highest)
    return weights_exp / jnp.sum(weights_exp, axis=2, keepdims=True)


def on_device(
    hidden_in,
    query,
    key_in,
    value_in,
    out_weight,
    norm_gain,
    router,
    routes,
    w_gate,
    w_up,
    w_down,
    grad_out,
):
    n_ep = lax.axis_size("ep")
    length = hidden_in.shape[0]
    slice_width = hidden_in.shape[1]
    capacity = min(length, (5 * length * TOP + 4 * n_ep - 1) // (4 * n_ep))
    query_h = split_heads(query)
    key_h = split_heads(key_in)
    value_h = split_heads(value_in)
    probabilities = softmax_rows(query_h, key_h)
    prob_rounded = probabilities.astype(jnp.bfloat16)
    attended = jnp.einsum("hqk,khd->qhd", prob_rounded, value_h, preferred_element_type=jnp.float32)
    attended = attended.reshape(length, -1).astype(jnp.bfloat16)
    all_heads = lax.all_gather(attended, "tp", axis=1, tiled=True)
    slab = lax.all_gather(out_weight, "ep", axis=1, tiled=True)
    proj = jnp.dot(all_heads, slab, preferred_element_type=jnp.float32)
    residual = (hidden_in.astype(jnp.float32) + proj).astype(jnp.bfloat16)
    resid_f = residual.astype(jnp.float32)
    gain_f = norm_gain.astype(jnp.float32)
    router_f = router.astype(jnp.float32)
    scaled = resid_f * gain_f
    squares = lax.psum(jnp.sum(resid_f * resid_f, axis=1), "tp")
    inv_rms = lax.rsqrt(squares[:, None] / D + norm_eps)
    normed_f = scaled * inv_rms
    logits = lax.psum(jnp.dot(normed_f, router_f, precision=lax.Precision.HIGHEST), "tp")
    normed = normed_f.astype(jnp.bfloat16)
    expert_ids = jnp.arange(n_ep, dtype=jnp.int32)
    one_hot = routes[:, :, None] == expert_ids[None, None, :]
    sigmoids = jax.nn.sigmoid(logits)
    picked = jnp.sum(jnp.where(one_hot, sigmoids[:, None, :], 0.0), axis=2)
    totals = jnp.sum(picked, axis=1, keepdims=True)
    weights = route_scale * picked / totals
    hot_int = one_hot.reshape(length * TOP, n_ep).astype(jnp.int32)
    earlier = jnp.cumsum(hot_int, axis=0) - hot_int
    slots = jnp.sum(earlier * hot_int, axis=1)
    destination = routes.reshape(-1) * capacity + slots
    send_rows = (
        jnp.zeros((n_ep * capacity, slice_width), jnp.bfloat16)
        .at[destination]
        .set(jnp.repeat(normed, TOP, axis=0))
    )
    send_grads = (
        jnp.zeros((n_ep * capacity, slice_width), jnp.bfloat16)
        .at[destination]
        .set(jnp.repeat(grad_out, TOP, axis=0))
    )
    recv_rows, recv_grads = (
        lax.all_to_all(
            send_rows.reshape(n_ep, capacity, slice_width),
            "ep",
            split_axis=0,
            concat_axis=0,
            tiled=True,
        ),
        lax.all_to_all(
            send_grads.reshape(n_ep, capacity, slice_width),
            "ep",
            split_axis=0,
            concat_axis=0,
            tiled=True,
        ),
    )
    routed_in = recv_rows.reshape(-1, slice_width)
    routed_grad = recv_grads.reshape(-1, slice_width)
    row_count = routed_in.shape[0]
    gate_local = w_gate[0]
    up_local = w_up[0]
    down_local = w_down[0]
    gate_cols = gate_local
    up_cols = up_local
    gate_part = jnp.einsum("dh,rd->hr", gate_cols, routed_in, preferred_element_type=jnp.float32)
    up_part = jnp.einsum("dh,rd->hr", up_cols, routed_in, preferred_element_type=jnp.float32)
    pre_sums = lax.psum_scatter(
        jnp.concatenate([gate_part, up_part], axis=1).astype(jnp.bfloat16),
        "tp",
        scatter_dimension=0,
        tiled=True,
    ).astype(jnp.float32)
    gate_pre = pre_sums[:, :row_count]
    up_pre = pre_sums[:, row_count:]
    back_pre = lax.psum_scatter(
        jnp.einsum("hd,rd->hr", down_local, routed_grad, preferred_element_type=jnp.float32).astype(
            jnp.bfloat16
        ),
        "tp",
        scatter_dimension=0,
        tiled=True,
    ).astype(jnp.float32)
    gate_sigmoid = jax.nn.sigmoid(gate_pre)
    gate_silu = gate_pre * gate_sigmoid
    hidden_b = lax.optimization_barrier((gate_silu * up_pre).astype(jnp.bfloat16)).astype(
        jnp.float32
    )
    score_total = lax.psum(jnp.sum(hidden_b * back_pre, axis=0), "tp")
    grad_gate = (back_pre * up_pre * gate_sigmoid * (1.0 + gate_pre * (1.0 - gate_sigmoid))).astype(
        jnp.bfloat16
    )
    grad_up = (back_pre * gate_silu).astype(jnp.bfloat16)
    gate_cols = gate_local
    up_cols = up_local
    acc_rows = jnp.einsum(
        "hr,dh->rd",
        lax.all_gather(grad_gate, "tp", axis=0, tiled=True),
        gate_cols,
        preferred_element_type=jnp.float32,
    )
    expert_grad = acc_rows + jnp.einsum(
        "hr,dh->rd",
        lax.all_gather(grad_up, "tp", axis=0, tiled=True),
        up_cols,
        preferred_element_type=jnp.float32,
    )
    back_rows = expert_grad.astype(jnp.bfloat16).reshape(n_ep, capacity, slice_width)
    score_b = score_total.astype(jnp.bfloat16).reshape(n_ep, capacity)
    ret_rows, ret_scores = (
        lax.all_to_all(back_rows, "ep", split_axis=0, concat_axis=0, tiled=True),
        lax.all_to_all(score_b, "ep", split_axis=0, concat_axis=0, tiled=True),
    )
    token_grads = ret_rows.reshape(-1, slice_width)[destination].reshape(length, TOP, slice_width)
    dnormed = jnp.einsum("tk,tkd->td", weights, token_grads.astype(jnp.float32))
    dweight = ret_scores.reshape(-1)[destination].astype(jnp.float32).reshape(length, TOP)
    dpicked = (
        route_scale / totals * (dweight - jnp.sum(dweight * picked, axis=1, keepdims=True) / totals)
    )
    dlogits = jnp.sum(
        jnp.where(one_hot, (dpicked * picked * (1.0 - picked))[:, :, None], 0.0), axis=1
    )
    dnorm_f = dnormed + jnp.dot(dlogits, router_f.T, precision=lax.Precision.HIGHEST)
    gained = gain_f * dnorm_f
    inner_sum = lax.psum(jnp.sum(gained * resid_f, axis=1), "tp")[:, None]
    dresid = inv_rms * gained - resid_f * (inv_rms * inv_rms * inv_rms) * inner_sum / D
    grad_in = (grad_out.astype(jnp.float32) + dresid).astype(jnp.bfloat16)
    partial_heads = jnp.einsum("td,hd->th", grad_in, slab, preferred_element_type=jnp.float32)
    grad_attn = lax.psum_scatter(
        partial_heads.astype(jnp.bfloat16), "tp", scatter_dimension=1, tiled=True
    )
    grad_h = split_heads(grad_attn)
    grad_value = jnp.einsum(
        "hqk,qhd->khd", prob_rounded, grad_h, preferred_element_type=jnp.float32
    )
    grad_prob = jnp.einsum("qhd,khd->hqk", grad_h, value_h, preferred_element_type=jnp.float32)
    centre = jnp.sum(probabilities * grad_prob, axis=2, keepdims=True)
    grad_score = (probabilities * (grad_prob - centre)).astype(jnp.bfloat16)
    grad_query = jnp.einsum(
        "hqk,khd->qhd", grad_score, key_h, preferred_element_type=jnp.float32
    ) * (1.0 / math.sqrt(HDIM))
    grad_key = jnp.einsum(
        "hqk,qhd->khd", grad_score, query_h, preferred_element_type=jnp.float32
    ) * (1.0 / math.sqrt(HDIM))
    return (
        grad_in,
        grad_query.reshape(length, -1).astype(jnp.bfloat16),
        grad_key.reshape(length, -1).astype(jnp.bfloat16),
        grad_value.reshape(length, -1).astype(jnp.bfloat16),
    )


def solution(mesh):
    in_specs = (
        P("ep", "tp"),
        P("ep", "tp"),
        P("ep", "tp"),
        P("ep", "tp"),
        P(None, ("tp", "ep")),
        P("tp"),
        P("tp", None),
        P("ep", None),
        P("ep", "tp", None),
        P("ep", "tp", None),
        P("ep", None, "tp"),
        P("ep", "tp"),
    )
    out_specs = (P("ep", "tp"), P("ep", "tp"), P("ep", "tp"), P("ep", "tp"))
    return jax.shard_map(
        on_device, mesh=mesh, in_specs=in_specs, out_specs=out_specs, check_vma=False
    )
```

profile of v0, /device:TPU:0, one launch (start us, length us, event | category | flops | bytes accessed | tf_op | source)
XLA Modules:
  0.0 999.3 jit_solution(14279088805155533214)
XLA Ops:
  22.3 163.1 %all-gather.4.cloned.1.call-done = bf16[2048,3584]{0,1:T(8,128)(2,1)} async-done(((bf16[2048,224]{0,1:T(8,128)(2,1)}), bf16[2048,3584]{0,1:T(8,128)(2,1)}) %all-gather.4.cloned.1.call-update) | async-done | bytes 14680080 | tf_op jit(solution)/shard_map/all_gather | solution.py:60
  185.4 10.7 %multiply_reduce_fusion.1 = (f32[128]{0:T(128)}, f32[128,3584]{1,0:T(8,128)S(1)}) fusion(bf16[128,2048]{0,1:T(8,128)(2,1)S(1)} %all_gather.12, bf16[2048,3584]{0,1:T(8,128)(2,1)} %all-gather.4.cloned.1.call-done, bf16[128,3584]{1,0:T(8,128)(2,1)S(1)} %copy-done.11), kind=kOutput, calls=%fused_computation.52 | convolution fusion | flops 1881800576 | bytes 17957376 | tf_op jit(solution)/shard_map/dot_general | solution.py:61
  199.7 15.3 %scatter_custom_fusion.1 = bf16[1280,3584]{1,0:T(8,128)(2,1)} fusion(s32[1024]{0:T(1024)} %bitcast.141, bf16[]{:T(256)} %constant.6.clone.1, bf16[128,3584]{1,0:T(8,128)(2,1)S(1)} %fusion.47), kind=kCustom, calls=%fused_computation.15 | custom fusion | bytes 10093056 | tf_op jit(solution)/shard_map/scatter | solution.py:85
  215.0 5.1 all-to-all-start.1
  220.1 15.4 %scatter_custom_fusion = bf16[1280,3584]{1,0:T(8,128)(2,1)} fusion(s32[1024]{0:T(1024)} %bitcast.142, bf16[]{:T(256)} %constant.6.clone.1, bf16[128,3584]{1,0:T(8,128)(2,1)S(1)} %copy-done.4), kind=kCustom, calls=%fused_computation.19 | custom fusion | bytes 10093056 | tf_op jit(solution)/shard_map/scatter | solution.py:90
  235.5 158.6 %all-to-all-done.1 = bf16[16,80,3584]{2,1,0:T(8,128)(2,1)} async-done(((bf16[16,80,3584]{2,1,0:T(8,128)(2,1)}), bf16[16,80,3584]{2,1,0:T(8,128)(2,1)}, u32[]{:S(2)}, u32[]{:S(2)}) %all-to-all-start.1) | async-done | bytes 9175072 | tf_op jit(solution)/shard_map/all_to_all | solution.py:93
  394.1 41.2 %all-to-all-start = ((bf16[16,80,3584]{2,1,0:T(8,128)(2,1)}), bf16[16,80,3584]{2,1,0:T(8,128)(2,1)}, u32[]{:S(2)}, u32[]{:S(2)}) async-start(bf16[16,80,3584]{2,1,0:T(8,128)(2,1)} %bitcast.125), calls=%async_computation | async-start | bytes 18350080 | tf_op jit(solution)/shard_map/all_to_all | solution.py:100
  435.7 14.3 %fusion.32 = bf16[1024,1280]{0,1:T(8,128)(2,1)S(1)} fusion(bf16[1280,3584]{1,0:T(8,128)(2,1)} %bitcast.14, bf16[1,3584,1024]{2,1,0:T(8,128)(2,1)} %param.21), kind=kOutput, calls=%fused_computation.37 | convolution fusion | flops 9396551680 | bytes 19136512 | tf_op jit(solution)/shard_map/dh,rd->hr/dot_general | solution.py:117
  450.0 14.3 %fusion.35 = bf16[1024,1280]{0,1:T(8,128)(2,1)S(1)} fusion(bf16[1280,3584]{1,0:T(8,128)(2,1)} %bitcast.14, bf16[1,3584,1024]{2,1,0:T(8,128)(2,1)} %param.20), kind=kOutput, calls=%fused_computation.38 | convolution fusion | flops 9396551680 | bytes 19136512 | tf_op jit(solution)/shard_map/dh,rd->hr/dot_general | solution.py:116
  467.4 139.4 %all-to-all-done = bf16[16,80,3584]{2,1,0:T(8,128)(2,1)} async-done(((bf16[16,80,3584]{2,1,0:T(8,128)(2,1)}), bf16[16,80,3584]{2,1,0:T(8,128)(2,1)}, u32[]{:S(2)}, u32[]{:S(2)}) %all-to-all-start) | async-done | bytes 9175072 | tf_op jit(solution)/shard_map/all_to_all | solution.py:100
  606.8 15.4 %fusion.38 = bf16[1024,1280]{0,1:T(8,128)(2,1)} fusion(bf16[1280,3584]{1,0:T(8,128)(2,1)} %bitcast.9, bf16[1,1024,3584]{2,1,0:T(8,128)(2,1)} %param.22), kind=kOutput, calls=%fused_computation.39 | convolution fusion | flops 9396551680 | bytes 19136512 | tf_op jit(solution)/shard_map/hd,rd->hr/dot_general | solution.py:127
  622.5 4.8 convert_element_type.132
  627.3 41.2 %reduce-scatter.4.cloned.1.call-done = bf16[512,1280]{0,1:T(8,128)(2,1)} async-done(((bf16[1024,1280]{0,1:T(8,128)(2,1)}), bf16[512,1280]{0,1:T(8,128)(2,1)}) %reduce-scatter.4.cloned.1.call-update) | async-done | bytes 1310736 | tf_op jit(solution)/shard_map/reduce_scatter | solution.py:126
  668.5 6.9 fusion.44
  682.2 6.8 all-to-all-start.3
  689.0 16.4 %fusion.6 = f32[1280,3584]{1,0:T(8,128)} fusion(bf16[1024,1280]{0,1:T(8,128)(2,1)} %all-gather.6.cloned.1.call-done, bf16[1,3584,1024]{2,1,0:T(8,128)(2,1)} %param.20), kind=kOutput, calls=%fused_computation.11 | convolution fusion | flops 9395240960 | bytes 28311552 | tf_op jit(solution)/shard_map/hr,dh->rd/dot_general | solution.py:146
  705.4 17.7 %add_convert_fusion = bf16[1280,3584]{1,0:T(8,128)(2,1)} fusion(f32[1280,3584]{1,0:T(8,128)} %fusion.6, bf16[1024,1280]{0,1:T(8,128)(2,1)} %all-gather.8.cloned.1.call-done, bf16[1,3584,1024]{2,1,0:T(8,128)(2,1)} %param.21), kind=kOutput, calls=%fused_computation.5 | convolution fusion | flops 9404416000 | bytes 37486592 | tf_op jit(solution)/shard_map/hr,dh->rd/dot_general | solution.py:152
  723.1 7.1 all-to-all-start.2
  730.9 6.8 gather_fusion.1
  737.9 164.9 %all-to-all-done.2 = bf16[16,80,3584]{2,1,0:T(8,128)(2,1)} async-done(((bf16[16,80,3584]{2,1,0:T(8,128)(2,1)}), bf16[16,80,3584]{2,1,0:T(8,128)(2,1)}, u32[]{:S(2)}, u32[]{:S(2)}) %all-to-all-start.2) | async-done | bytes 9175072 | tf_op jit(solution)/shard_map/all_to_all | solution.py:161
  902.8 18.6 %gather_fusion = bf16[1024,3584]{1,0:T(8,128)(2,1)} fusion(bf16[1280,3584]{1,0:T(8,128)(2,1)} %bitcast.20, s32[1024]{0:T(1024)S(1)} %broadcast_clamp_fusion), kind=kCustom, calls=%fused_computation | custom fusion | bytes 14684160 | tf_op jit(solution)/shard_map/gather | solution.py:164
  921.4 5.1 fusion.1
  933.7 8.4 convolution_convert_fusion
  942.1 43.7 %reduce-scatter.8.cloned.1.call-done = bf16[128,1024]{1,0:T(8,128)(2,1)} async-done(((bf16[128,2048]{1,0:T(8,128)(2,1)}), bf16[128,1024]{1,0:T(8,128)(2,1)}) %reduce-scatter.8.cloned.1.call-update) | async-done | bytes 262160 | tf_op jit(solution)/shard_map/reduce_scatter | solution.py:179
  (113 shorter events, 43.4 us)
Async XLA Ops:
  7.2 12.0 %copy-start = (bf16[128,1024]{1,0:T(8,128)(2,1)S(1)}, bf16[128,1024]{1,0:T(8,128)(2,1)}, u32[]{:S(2)}) copy-start(bf16[128,1024]{1,0:T(8,128)(2,1)} %param.15) | copy-start | bytes 786436
  7.2 178.2 %all-gather.4.cloned.1.call-start = ((), (), s32[]{:S(2)}) async-start(), calls=%async_computation.7 | async-start | bytes 15597568 | tf_op jit(solution)/shard_map/all_gather | solution.py:60
  17.7 4.0 copy-start.5
  17.9 167.5 %copy-start.11 = (bf16[128,3584]{1,0:T(8,128)(2,1)S(1)}, bf16[128,3584]{1,0:T(8,128)(2,1)}, u32[]{:S(2)}) copy-start(bf16[128,3584]{1,0:T(8,128)(2,1)} %param.12) | copy-start | bytes 2752516
  18.2 4.2 copy-start.10
  19.1 3.2 copy-start.14
  199.4 476.6 %copy-start.17 = (f32[128]{0:T(128)}, f32[128]{0:T(128)S(1)}, u32[]{:S(2)}) copy-start(f32[128]{0:T(128)S(1)} %get-tuple-element.28) | copy-start | bytes 1540
  215.0 5.1 copy-start.4
  215.0 179.1 %all-to-all-start.1 = ((bf16[16,80,3584]{2,1,0:T(8,128)(2,1)}), bf16[16,80,3584]{2,1,0:T(8,128)(2,1)}, u32[]{:S(2)}, u32[]{:S(2)}) async-start(bf16[16,80,3584]{2,1,0:T(8,128)(2,1)} %bitcast.126), calls=%async_computation.2 | async-start | bytes 18350080 | tf_op jit(solution)/shard_map/all_to_all | solution.py:93
  394.1 212.7 %all-to-all-start = ((bf16[16,80,3584]{2,1,0:T(8,128)(2,1)}), bf16[16,80,3584]{2,1,0:T(8,128)(2,1)}, u32[]{:S(2)}, u32[]{:S(2)}) async-start(bf16[16,80,3584]{2,1,0:T(8,128)(2,1)} %bitcast.125), calls=%async_computation | async-start | bytes 18350080 | tf_op jit(solution)/shard_map/all_to_all | solution.py:100
  435.3 187.2 %reduce-scatter.6.cloned.1.call-start = ((), (), s32[]{:S(2)}) async-start(), calls=%async_computation.9 | async-start | bytes 7864320 | tf_op jit(solution)/shard_map/reduce_scatter | solution.py:118
  467.3 201.1 %reduce-scatter.4.cloned.1.call-start = ((), (), s32[]{:S(2)}) async-start(), calls=%async_computation.8 | async-start | bytes 3932160 | tf_op jit(solution)/shard_map/reduce_scatter | solution.py:126
  622.2 66.8 %all-gather.6.cloned.1.call-start = ((), (), s32[]{:S(2)}) async-start(), calls=%async_computation.10 | async-start | bytes 3932160 | tf_op jit(solution)/shard_map/all_gather | solution.py:148
  675.4 30.0 %all-gather.8.cloned.1.call-start = ((), (), s32[]{:S(2)}) async-start(), calls=%async_computation.11 | async-start | bytes 3932160 | tf_op jit(solution)/shard_map/all_gather | solution.py:154
  682.2 41.0 %all-to-all-start.3 = ((bf16[16,1,80]{2,1,0:T(2,128)(2,1)}), bf16[16,1,80]{2,1,0:T(2,128)(2,1)S(1)}, u32[]{:S(2)}, u32[]{:S(2)}) async-start(bf16[16,1,80]{2,1,0:T(2,128)(2,1)} %all_to_all.20), calls=%async_computation.5 | async-start | bytes 16384 | tf_op jit(solution)/shard_map/all_to_all | solution.py:162
  723.1 7.4 copy-start.16
  723.1 7.4 copy-start.13
  723.1 179.7 %all-to-all-start.2 = ((bf16[16,80,3584]{2,1,0:T(8,128)(2,1)}), bf16[16,80,3584]{2,1,0:T(8,128)(2,1)}, u32[]{:S(2)}, u32[]{:S(2)}) async-start(bf16[16,80,3584]{2,1,0:T(8,128)(2,1)} %bitcast.127), calls=%async_computation.4 | async-start | bytes 18350080 | tf_op jit(solution)/shard_map/all_to_all | solution.py:161
  730.2 255.6 %reduce-scatter.8.cloned.1.call-start = ((), (), s32[]{:S(2)}) async-start(), calls=%async_computation.12 | async-start | bytes 786432 | tf_op jit(solution)/shard_map/reduce_scatter | solution.py:179
  926.5 4.8 copy-start.18
  926.5 4.8 copy-start.19
  933.7 8.4 copy-start.1
  933.7 53.2 %copy-start.15 = (f32[8,128]{1,0:T(8,128)S(1)}, f32[8,128]{1,0:T(8,128)}, u32[]{:S(2)}) copy-start(f32[8,128]{1,0:T(8,128)} %copy-done.14) | copy-start | bytes 12292
  942.1 46.4 %copy-start.9 = (f32[8,128,128]{1,2,0:T(8,128)S(1)}, f32[8,128,128]{1,2,0:T(8,128)}, u32[]{:S(2)}) copy-start(f32[8,128,128]{1,2,0:T(8,128)} %get-tuple-element.32) | copy-start | bytes 1572868
  (6 other events, 10.2 us)
Sparse Core Ops, SparseCore 0:
  10.8 174.5 all-gather.3
  467.5 14.4 reduce-scatter.5
  622.4 46.0 reduce-scatter.3
  675.5 12.5 all-gather.5
  689.5 12.5 all-gather.7
  942.3 43.4 reduce-scatter.7
where the time goes:
time: 1000 us; the launch traced here: 999 us
  waiting for transfers between devices  712 us (71%)
  matrix products  109 us (11%)
  local copies, waits for them, and re-layouts  65.6 us (7%)
  starting transfers between devices  61.3 us (6%)
  other arithmetic  26 us (3%)
  between operations  14.8 us (1%)
  blocking collectives  10.8 us (1%)
    all_to_all x1, waiting for transfers between devices, on_device(): lax.all_to_all(back_rows, 'ep', split_axis=0, concat_axis=0, tiled=True)  165 us
    all_gather x1, waiting for transfers between devices, on_device(): slab = lax.all_gather(out_weight, 'ep', axis=1, tiled=True)  163 us
    all_to_all x1, waiting for transfers between devices, on_device(): lax.all_to_all(send_rows.reshape(n_ep, capacity, slice_width), 'ep', spli...  159 us
    all_to_all x1, waiting for transfers between devices, on_device(): lax.all_to_all(send_grads.reshape(n_ep, capacity, slice_width), 'ep', spl...  139 us
    reduce_scatter x1, waiting for transfers between devices, on_device(): lax.psum_scatter(partial_heads.astype(jnp.bfloat16), 'tp', scatter_dimens...  43.7 us
    all_to_all x1, starting transfers between devices, on_device(): lax.all_to_all(send_grads.reshape(n_ep, capacity, slice_width), 'ep', spl...  41.2 us
    reduce_scatter x1, waiting for transfers between devices, on_device(): lax.psum_scatter(jnp.einsum('hd,rd->hr', down_local, routed_grad, preferr...  41.2 us
  transfers between devices with their start and end apart: 10, of which 6 were waited for; matrix products, arithmetic and copies ran while one was open for 12% of the time, Pallas kernels for 0%

commit v1 on v0

v1 whole, which is shorter than its diff:
```python
import math

import jax
import jax.numpy as jnp
from jax import lax
from jax.sharding import PartitionSpec as P

D = 7168
HDIM = 128
TOP = 8
DEPTH = 4


route_scale = 2.5
norm_eps = 1e-06
masked_score = -1e30


def split_heads(values):
    return values.reshape(values.shape[0], values.shape[1] // HDIM, HDIM)


def softmax_rows(query_h, key_h):
    length = query_h.shape[0]
    scores = jnp.einsum("qhd,khd->hqk", query_h, key_h, preferred_element_type=jnp.float32) * (
        1.0 / math.sqrt(HDIM)
    )
    causal = jnp.arange(length)[None, :] <= jnp.arange(length)[:, None]
    scores = jnp.where(causal[None], scores, masked_score)
    highest = jnp.max(scores, axis=2, keepdims=True)
    weights_exp = jnp.exp(scores - highest)
    return weights_exp / jnp.sum(weights_exp, axis=2, keepdims=True)


def depth_permute(x, pairs, n_ep):
    plane = n_ep // DEPTH
    return lax.ppermute(
        x, "ep", [(a * plane + i, b * plane + i) for a, b in pairs for i in range(plane)]
    )


def plane_permute(x, step, n_ep):
    return lax.ppermute(x, "ep", [(i, i ^ step) for i in range(n_ep)])


SWAP = [(0, 1), (1, 0), (2, 3), (3, 2)]
MIDDLE = [(1, 2), (2, 1)]
OUTWARD = [(1, 0), (2, 3)]
INWARD = [(0, 1), (3, 2)]


def spread_depth(x, n_ep):
    partner = depth_permute(x, SWAP, n_ep)
    near = depth_permute(x, MIDDLE, n_ep)
    near = (near, depth_permute(near, OUTWARD, n_ep))
    far = depth_permute(partner, MIDDLE, n_ep)
    far = (far, depth_permute(far, OUTWARD, n_ep))
    return [x, partner, near[0] + near[1], far[0] + far[1]]


def depth_sources(z):
    return [z, z ^ 1, jnp.where(z < 2, 2, 1), jnp.where(z < 2, 3, 0)]


def exchange_plane(blocks, n_ep):
    parts = [blocks[0]]
    for step in range(1, blocks.shape[0]):
        parts.append(plane_permute(blocks[step], step, n_ep))
    return jnp.concatenate(parts, axis=0)


def tp_swap(x):
    return lax.ppermute(x, "tp", [(0, 1), (1, 0)])


def tp_sum(x):
    if lax.axis_size("tp") != 2:
        return lax.psum(x, "tp")
    return x + tp_swap(x)


def tp_reduce(x, axis):
    n_tp = lax.axis_size("tp")
    if n_tp != 2:
        return lax.psum_scatter(x, "tp", scatter_dimension=axis, tiled=True).astype(jnp.float32)
    t = lax.axis_index("tp")
    width = x.shape[axis] // 2
    mine = lax.dynamic_slice_in_dim(x, t * width, width, axis)
    other = lax.dynamic_slice_in_dim(x, (1 - t) * width, width, axis)
    return mine.astype(jnp.float32) + tp_swap(other).astype(jnp.float32)


def tp_gather(x, axis):
    n_tp = lax.axis_size("tp")
    if n_tp != 2:
        return lax.all_gather(x, "tp", axis=axis, tiled=True)
    t = lax.axis_index("tp")
    other = tp_swap(x)
    first = jnp.where(t == 0, x, other)
    second = jnp.where(t == 0, other, x)
    return jnp.concatenate([first, second], axis=axis)


def one_hot_slots(mask, capacity):
    length = mask.shape[-1]
    before = (jnp.arange(length)[:, None] < jnp.arange(length)[None, :]).astype(jnp.bfloat16)
    slots = jnp.einsum(
        "...i,ij->...j", mask.astype(jnp.bfloat16), before, preferred_element_type=jnp.float32
    )
    wanted = jnp.arange(capacity, dtype=jnp.float32)[:, None]
    return (mask[..., None, :] & (slots[..., None, :] == wanted)).astype(jnp.bfloat16)


def on_device(
    hidden_in,
    query,
    key_in,
    value_in,
    out_weight,
    norm_gain,
    router,
    routes,
    w_gate,
    w_up,
    w_down,
    grad_out,
):
    n_ep = lax.axis_size("ep")
    plane = n_ep // DEPTH
    me = lax.axis_index("ep")
    z, place = me // plane, me % plane
    length = hidden_in.shape[0]
    slice_width = hidden_in.shape[1]
    capacity = min(length, (5 * length * TOP + 4 * n_ep - 1) // (4 * n_ep))
    bf16 = jnp.bfloat16

    slab = lax.all_gather(out_weight, "ep", axis=1, tiled=True)

    routes_all = lax.all_gather(routes, "ep", axis=0)
    sources = jnp.stack(depth_sources(z))
    steps = jnp.arange(plane, dtype=jnp.int32)
    relay_seq = sources * plane + place
    relay_expert = z * plane + (place ^ steps)
    relay_mask = jnp.any(
        routes_all[relay_seq][:, None] == relay_expert[None, :, None, None], axis=-1
    )
    relay_hot = one_hot_slots(relay_mask, capacity).reshape(DEPTH, plane * capacity, length)
    expert_seq = sources[:, None] * plane + (place ^ steps)[None, :]
    expert_mask = jnp.any(routes_all[expert_seq] == me, axis=-1)
    expert_hot = one_hot_slots(expert_mask, capacity).astype(jnp.float32)

    def dispatch(x):
        rows = []
        for hot, piece in zip(relay_hot, spread_depth(x, n_ep)):
            packed = jnp.dot(hot, piece, preferred_element_type=jnp.float32).astype(bf16)
            rows.append(exchange_plane(packed.reshape(plane, capacity, slice_width), n_ep))
        return rows

    query_h = split_heads(query)
    key_h = split_heads(key_in)
    value_h = split_heads(value_in)
    probabilities = softmax_rows(query_h, key_h)
    prob_rounded = probabilities.astype(bf16)
    attended = jnp.einsum("hqk,khd->qhd", prob_rounded, value_h, preferred_element_type=jnp.float32)
    attended = attended.reshape(length, -1).astype(bf16)
    all_heads = tp_gather(attended, 1)

    grad_rows = dispatch(grad_out)

    proj = jnp.dot(all_heads, slab, preferred_element_type=jnp.float32)
    residual = (hidden_in.astype(jnp.float32) + proj).astype(bf16)
    resid_f = residual.astype(jnp.float32)
    gain_f = norm_gain.astype(jnp.float32)
    router_f = router.astype(jnp.float32)
    scaled = resid_f * gain_f
    squares = tp_sum(jnp.sum(resid_f * resid_f, axis=1))
    raw_logits = tp_sum(jnp.dot(scaled, router_f, precision=lax.Precision.HIGHEST))
    inv_rms = lax.rsqrt(squares[:, None] / D + norm_eps)
    normed = (scaled * inv_rms).astype(bf16)
    normed_rows = dispatch(normed)

    logits = raw_logits * inv_rms
    expert_ids = jnp.arange(n_ep, dtype=jnp.int32)
    one_hot = routes[:, :, None] == expert_ids[None, None, :]
    sigmoids = jax.nn.sigmoid(logits)
    picked = jnp.sum(jnp.where(one_hot, sigmoids[:, None, :], 0.0), axis=2)
    totals = jnp.sum(picked, axis=1, keepdims=True)
    weights = route_scale * picked / totals
    weight_table = jnp.sum(jnp.where(one_hot, weights[:, :, None], 0.0), axis=1)
    own_weights = lax.all_to_all(
        weight_table.T.reshape(n_ep, 1, length), "ep", split_axis=0, concat_axis=0, tiled=True
    ).reshape(n_ep, length)
    row_weights = jnp.sum(expert_hot * own_weights[expert_seq][:, :, None, :], axis=-1)
    row_weights = row_weights.reshape(DEPTH, plane * capacity, 1)

    gate_local = w_gate[0]
    up_local = w_up[0]
    down_local = w_down[0]
    row_count = plane * capacity
    back_pre = tp_reduce(
        jnp.einsum(
            "rd,hd->rh",
            jnp.concatenate(grad_rows, axis=0),
            down_local,
            preferred_element_type=jnp.float32,
        ).astype(bf16),
        1,
    )
    scores, sums = [None] * DEPTH, [None] * DEPTH
    for i in range(DEPTH):
        rows = normed_rows[i]
        gate_part = jnp.dot(rows, gate_local, preferred_element_type=jnp.float32).astype(bf16)
        up_part = jnp.dot(rows, up_local, preferred_element_type=jnp.float32).astype(bf16)
        pre_sums = tp_reduce(jnp.stack([gate_part, up_part]), 2)
        gate_pre, up_pre = pre_sums[0], pre_sums[1]
        back = back_pre[i * row_count : (i + 1) * row_count]
        gate_sigmoid = jax.nn.sigmoid(gate_pre)
        gate_silu = gate_pre * gate_sigmoid
        hidden_b = lax.optimization_barrier((gate_silu * up_pre).astype(bf16)).astype(jnp.float32)
        scores[i] = jnp.sum(hidden_b * back, axis=1)
        grad_gate = (back * up_pre * gate_sigmoid * (1.0 + gate_pre * (1.0 - gate_sigmoid))).astype(
            bf16
        )
        grad_up = (back * gate_silu).astype(bf16)
        both = tp_gather(jnp.stack([grad_gate, grad_up]), 2)
        expert_grad = jnp.einsum(
            "rh,dh->rd", both[0], gate_local, preferred_element_type=jnp.float32
        ) + jnp.einsum("rh,dh->rd", both[1], up_local, preferred_element_type=jnp.float32)
        back_rows = (expert_grad * row_weights[i]).astype(bf16)
        arrived = exchange_plane(back_rows.reshape(plane, capacity, slice_width), n_ep)
        sums[i] = jnp.einsum("ri,rd->id", relay_hot[i], arrived, preferred_element_type=jnp.float32)
    far = sums[3].astype(bf16)
    far = (sums[3] + depth_permute(far, INWARD, n_ep)).astype(bf16)
    near = sums[2].astype(bf16)
    near = (sums[2] + depth_permute(near, INWARD, n_ep)).astype(bf16)
    partner = (sums[1] + depth_permute(far, MIDDLE, n_ep)).astype(bf16)
    dnormed = (
        sums[0]
        + depth_permute(near, MIDDLE, n_ep).astype(jnp.float32)
        + depth_permute(partner, SWAP, n_ep).astype(jnp.float32)
    )

    score_rows = tp_sum(jnp.concatenate(scores)).astype(bf16).astype(jnp.float32)
    score_rows = score_rows.reshape(DEPTH, plane, capacity, 1)
    token_scores = jnp.sum(expert_hot * score_rows, axis=2).reshape(n_ep, length)
    order = jnp.argmax(expert_seq.reshape(1, n_ep) == expert_ids[:, None], axis=1)
    ret_scores = lax.all_to_all(
        token_scores[order].reshape(n_ep, 1, length), "ep", split_axis=0, concat_axis=0, tiled=True
    ).reshape(n_ep, length)
    dweight = jnp.sum(jnp.where(one_hot, ret_scores.T[:, None, :], 0.0), axis=2)

    dpicked = (
        route_scale / totals * (dweight - jnp.sum(dweight * picked, axis=1, keepdims=True) / totals)
    )
    dlogits = jnp.sum(
        jnp.where(one_hot, (dpicked * picked * (1.0 - picked))[:, :, None], 0.0), axis=1
    )
    dnorm_f = dnormed + jnp.dot(dlogits, router_f.T, precision=lax.Precision.HIGHEST)
    gained = gain_f * dnorm_f
    inner_sum = tp_sum(jnp.sum(gained * resid_f, axis=1))[:, None]
    dresid = inv_rms * gained - resid_f * (inv_rms * inv_rms * inv_rms) * inner_sum / D
    grad_in = (grad_out.astype(jnp.float32) + dresid).astype(bf16)
    partial_heads = jnp.einsum("td,hd->th", grad_in, slab, preferred_element_type=jnp.float32)
    grad_attn = tp_reduce(partial_heads.astype(bf16), 1).astype(bf16)
    grad_h = split_heads(grad_attn)
    grad_value = jnp.einsum(
        "hqk,qhd->khd", prob_rounded, grad_h, preferred_element_type=jnp.float32
    )
    grad_prob = jnp.einsum("qhd,khd->hqk", grad_h, value_h, preferred_element_type=jnp.float32)
    centre = jnp.sum(probabilities * grad_prob, axis=2, keepdims=True)
    grad_score = (probabilities * (grad_prob - centre)).astype(bf16)
    grad_query = jnp.einsum(
        "hqk,khd->qhd", grad_score, key_h, preferred_element_type=jnp.float32
    ) * (1.0 / math.sqrt(HDIM))
    grad_key = jnp.einsum(
        "hqk,qhd->khd", grad_score, query_h, preferred_element_type=jnp.float32
    ) * (1.0 / math.sqrt(HDIM))
    return (
        grad_in,
        grad_query.reshape(length, -1).astype(bf16),
        grad_key.reshape(length, -1).astype(bf16),
        grad_value.reshape(length, -1).astype(bf16),
    )


def solution(mesh):
    in_specs = (
        P("ep", "tp"),
        P("ep", "tp"),
        P("ep", "tp"),
        P("ep", "tp"),
        P(None, ("tp", "ep")),
        P("tp"),
        P("tp", None),
        P("ep", None),
        P("ep", "tp", None),
        P("ep", "tp", None),
        P("ep", None, "tp"),
        P("ep", "tp"),
    )
    out_specs = (P("ep", "tp"), P("ep", "tp"), P("ep", "tp"), P("ep", "tp"))
    return jax.shard_map(
        on_device, mesh=mesh, in_specs=in_specs, out_specs=out_specs, check_vma=False
    )
```

time: 1000 us -> 657 us (0.66)
  waiting for transfers between devices: 712 us -> 249 us
  blocking collectives: 10.8 us -> 62.1 us
  starting transfers between devices: 61.3 us -> 107 us
  matrix products: 109 us -> 143 us
  local copies, waits for them, and re-layouts: 65.6 us -> 48.2 us
    all_to_all x4 -> x2, waiting for transfers between devices: 463 us -> 0.01 us  [the longest x1 0.01 us: on_device(): lax.all_to_all(weight_table.T.reshape(n_ep, 1, length), 'ep', split_axis=...]
    ppermute x0 -> x66, waiting for transfers between devices: none -> 249 us  [the longest x36 198 us: plane_permute(): return lax.ppermute(x, 'ep', [(i, i ^ step) for i in range(n_ep)])]
    all_gather x1, waiting for transfers between devices: 163 us -> 0.01 us  [on_device(): slab = lax.all_gather(out_weight, 'ep', axis=1, tiled=True)]
    ppermute x0 -> x66, starting transfers between devices: none -> 97.2 us  [the longest x36 48.2 us: plane_permute(): return lax.ppermute(x, 'ep', [(i, i ^ step) for i in range(n_ep)])]
    reduce_scatter x3 -> x0, waiting for transfers between devices: 84.8 us -> none  [the longest x1 43.7 us: on_device(): lax.psum_scatter(partial_heads.astype(jnp.bfloat16), 'tp', scatter_dimens...]
    all_gather x1, blocking collectives: 2.26 us -> 62.1 us  [on_device(): routes_all = lax.all_gather(routes, 'ep', axis=0)]
    all_to_all x4 -> x2, starting transfers between devices: 60.2 us -> 9.41 us  [the longest x1 4.74 us: on_device(): lax.all_to_all(weight_table.T.reshape(n_ep, 1, length), 'ep', split_axis=...]
    dot_general x7 -> x32, matrix products: 84.3 us -> 121 us  [the longest x4 28.6 us: on_device(): jnp.einsum('rh,dh->rd', both[1], up_local, preferred_element_type=jnp.flo...]
  transfers between devices with their start and end apart: 10 -> 69, of which waited for: 6 -> 27; matrix products, arithmetic and copies ran while one was open for 12% -> 30% of each run, Pallas kernels for 0% -> 0%
where the time goes in v1:
time: 657 us; the launch traced here: 650 us
  waiting for transfers between devices  249 us (38%)
  matrix products  143 us (22%)
  starting transfers between devices  107 us (16%)
  blocking collectives  62.1 us (9%)
  local copies, waits for them, and re-layouts  48.2 us (7%)
  other arithmetic  24.7 us (4%)
  between operations  15.9 us (2%)
    ppermute x36, waiting for transfers between devices, plane_permute(): return lax.ppermute(x, 'ep', [(i, i ^ step) for i in range(n_ep)])  198 us
    all_gather x1, blocking collectives, on_device(): routes_all = lax.all_gather(routes, 'ep', axis=0)  62.1 us
    ppermute x36, starting transfers between devices, plane_permute(): return lax.ppermute(x, 'ep', [(i, i ^ step) for i in range(n_ep)])  48.2 us
    ppermute x15, waiting for transfers between devices, depth_permute(): lax.ppermute(x, 'ep', [(a * plane + i, b * plane + i) for a, b in pairs f...  47.9 us
    ppermute x15, starting transfers between devices, depth_permute(): lax.ppermute(x, 'ep', [(a * plane + i, b * plane + i) for a, b in pairs f...  46.8 us
    dot_general x4, matrix products, on_device(): jnp.einsum('rh,dh->rd', both[1], up_local, preferred_element_type=jnp.flo...  28.6 us
    dot_general x4, matrix products, on_device(): jnp.einsum('rh,dh->rd', both[0], gate_local, preferred_element_type=jnp.f...  21.8 us
    unnamed x140, local copies, waits for them, and re-layouts  21 us
  transfers between devices with their start and end apart: 69, of which 27 were waited for; matrix products, arithmetic and copies ran while one was open for 30% of the time, Pallas kernels for 0%

profile of v1, /device:TPU:0, one launch (start us, length us, event | category | flops | bytes accessed | tf_op | source)
XLA Modules:
  0.0 649.9 jit_solution(14568331602414496050)
XLA Ops:
  12.7 62.1 %all-gather = s32[2048,8]{0,1:T(8,128)S(1)} all-gather(s32[128,8]{0,1:T(8,128)} %param.19), channel_id=2, replica_groups=mesh['tp'=2,'ep'=16] {'ep'}, dimensions={0}, use_global_device_ids=true | all-gather | bytes 69632 | tf_op jit(solution)/shard_map/all_gather | solution.py:139
  85.7 19.2 %collective-permute-done.2 = bf16[80,3584]{1,0:T(8,128)(2,1)} collective-permute-done((bf16[80,3584]{1,0:T(8,128)(2,1)}, bf16[80,3584]{1,0:T(8,128)(2,1)}, u32[]{:S(2)}, u32[]{:S(2)}) %collective-permute-start.2) | collective-permute-done | bytes 573472 | tf_op jit(solution)/shard_map/ppermute | solution.py:43
  123.8 21.7 %collective-permute-done.6 = bf16[80,3584]{1,0:T(8,128)(2,1)} collective-permute-done((bf16[80,3584]{1,0:T(8,128)(2,1)}, bf16[80,3584]{1,0:T(8,128)(2,1)}, u32[]{:S(2)}, u32[]{:S(2)}) %collective-permute-start.6) | collective-permute-done | bytes 573472 | tf_op jit(solution)/shard_map/ppermute | solution.py:43
  148.7 8.0 %collective-permute-done.7 = bf16[80,3584]{1,0:T(8,128)(2,1)} collective-permute-done((bf16[80,3584]{1,0:T(8,128)(2,1)}, bf16[80,3584]{1,0:T(8,128)(2,1)}, u32[]{:S(2)}, u32[]{:S(2)}) %collective-permute-start.7) | collective-permute-done | bytes 573472 | tf_op jit(solution)/shard_map/ppermute | solution.py:43
  165.1 21.8 %collective-permute-done.10 = bf16[128,3584]{1,0:T(8,128)(2,1)S(1)} collective-permute-done((bf16[128,3584]{1,0:T(8,128)(2,1)}, bf16[128,3584]{1,0:T(8,128)(2,1)S(1)}, u32[]{:S(2)}, u32[]{:S(2)}) %collective-permute-start.10) | collective-permute-done | bytes 917536 | tf_op jit(solution)/shard_map/ppermute | solution.py:37
  196.5 15.9 %collective-permute-done.11 = bf16[80,3584]{1,0:T(8,128)(2,1)} collective-permute-done((bf16[80,3584]{1,0:T(8,128)(2,1)}, bf16[80,3584]{1,0:T(8,128)(2,1)}, u32[]{:S(2)}, u32[]{:S(2)}) %collective-permute-start.11) | collective-permute-done | bytes 573472 | tf_op jit(solution)/shard_map/ppermute | solution.py:43
  214.3 11.8 %collective-permute-done.12 = bf16[80,3584]{1,0:T(8,128)(2,1)S(1)} collective-permute-done((bf16[80,3584]{1,0:T(8,128)(2,1)}, bf16[80,3584]{1,0:T(8,128)(2,1)S(1)}, u32[]{:S(2)}, u32[]{:S(2)}) %collective-permute-start.12) | collective-permute-done | bytes 573472 | tf_op jit(solution)/shard_map/ppermute | solution.py:43
  240.3 9.1 %collective-permute-done.17 = bf16[80,3584]{1,0:T(8,128)(2,1)S(1)} collective-permute-done((bf16[80,3584]{1,0:T(8,128)(2,1)S(1)}, bf16[80,3584]{1,0:T(8,128)(2,1)S(1)}, u32[]{:S(2)}, u32[]{:S(2)}) %collective-permute-start.17) | collective-permute-done | bytes 573472 | tf_op jit(solution)/shard_map/ppermute | solution.py:43
  251.1 14.3 %fusion.77 = bf16[1280,1024]{1,0:T(8,128)(2,1)S(1)} fusion(bf16[1280,3584]{1,0:T(8,128)(2,1)} %constant_dynamic-update-slice_fusion, bf16[1,1024,3584]{2,1,0:T(8,128)(2,1)} %param.22), kind=kOutput, calls=%fused_computation.68 | convolution fusion | flops 9396551680 | bytes 19136512 | tf_op jit(solution)/shard_map/rd,hd->rh/dot_general | solution.py:201
  268.4 10.2 %multiply_reduce_fusion.1 = (f32[128]{0:T(128)S(1)}, f32[128,3584]{1,0:T(8,128)S(1)}) fusion(bf16[2048,3584]{0,1:T(8,128)(2,1)} %all-gather.3.cloned.1.call-done, bf16[128,1024]{0,1:T(8,128)(2,1)S(1)} %get-tuple-element.103, bf16[128,1024]{0,1:T(8,128)(2,1)S(1)} %get-tuple-element.102, bf16[128,3584]{1,0:T(8,128)(2,1)S(1)} %copy-done.16), kind=kOutput, calls=%fused_computation.110 | convolution fusion | flops 1882849152 | bytes 17957376 | tf_op jit(solution)/shard_map/dot_general | solution.py:170
  303.0 10.7 %collective-permute-done.21 = bf16[80,3584]{1,0:T(8,128)(2,1)} collective-permute-done((bf16[80,3584]{1,0:T(8,128)(2,1)}, bf16[80,3584]{1,0:T(8,128)(2,1)}, u32[]{:S(2)}, u32[]{:S(2)}) %collective-permute-start.21) | collective-permute-done | bytes 573472 | tf_op jit(solution)/shard_map/ppermute | solution.py:43
  347.1 12.2 %collective-permute-done.43 = bf16[80,3584]{1,0:T(8,128)(2,1)} collective-permute-done((bf16[80,3584]{1,0:T(8,128)(2,1)}, bf16[80,3584]{1,0:T(8,128)(2,1)}, u32[]{:S(2)}, u32[]{:S(2)}) %collective-permute-start.43) | collective-permute-done | bytes 573472 | tf_op jit(solution)/shard_map/ppermute | solution.py:43
  378.9 9.2 %collective-permute-done.31 = bf16[80,3584]{1,0:T(8,128)(2,1)S(1)} collective-permute-done((bf16[80,3584]{1,0:T(8,128)(2,1)S(1)}, bf16[80,3584]{1,0:T(8,128)(2,1)S(1)}, u32[]{:S(2)}, u32[]{:S(2)}) %collective-permute-start.31) | collective-permute-done | bytes 573472 | tf_op jit(solution)/shard_map/ppermute | solution.py:43
  388.1 13.0 %collective-permute-done.32 = bf16[80,3584]{1,0:T(8,128)(2,1)S(1)} collective-permute-done((bf16[80,3584]{1,0:T(8,128)(2,1)S(1)}, bf16[80,3584]{1,0:T(8,128)(2,1)S(1)}, u32[]{:S(2)}, u32[]{:S(2)}) %collective-permute-start.32) | collective-permute-done | bytes 573472 | tf_op jit(solution)/shard_map/ppermute | solution.py:43
  415.8 7.4 %collective-permute-done.52 = bf16[80,3584]{1,0:T(8,128)(2,1)S(1)} collective-permute-done((bf16[80,3584]{1,0:T(8,128)(2,1)S(1)}, bf16[80,3584]{1,0:T(8,128)(2,1)S(1)}, u32[]{:S(2)}, u32[]{:S(2)}) %collective-permute-start.52) | collective-permute-done | bytes 573472 | tf_op jit(solution)/shard_map/ppermute | solution.py:43
  423.2 12.3 %collective-permute-done.53 = bf16[80,3584]{1,0:T(8,128)(2,1)} collective-permute-done((bf16[80,3584]{1,0:T(8,128)(2,1)S(1)}, bf16[80,3584]{1,0:T(8,128)(2,1)}, u32[]{:S(2)}, u32[]{:S(2)}) %collective-permute-start.53) | collective-permute-done | bytes 573472 | tf_op jit(solution)/shard_map/ppermute | solution.py:43
  459.3 7.3 %fusion.68 = bf16[320,3584]{1,0:T(8,128)(2,1)S(1)} fusion(f32[320,3584]{1,0:T(8,128)} %fusion.29, bf16[1,3584,1024]{2,1,0:T(8,128)(2,1)} %param.21, f32[320]{0:T(512)} %mul.346, bf16[2,320,512]{2,1,0:T(8,128)(2,1)} %copy-done.28, bf16[2,320,512]{2,1,0:T(8,128)(2,1)} %copy-done.29), kind=kOutput, calls=%fused_computation.50 | convolution fusion | flops 2353561600 | bytes 15533312 | tf_op jit(solution)/shard_map/rh,dh->rd/dot_general | solution.py:228
  479.4 7.3 %fusion.62 = bf16[320,3584]{1,0:T(8,128)(2,1)S(1)} fusion(f32[320,3584]{1,0:T(8,128)} %fusion.21, bf16[1,3584,1024]{2,1,0:T(8,128)(2,1)} %param.21, f32[320]{0:T(512)} %mul.364, bf16[2,320,512]{2,1,0:T(8,128)(2,1)} %copy-done.26, bf16[2,320,512]{2,1,0:T(8,128)(2,1)} %copy-done.27), kind=kOutput, calls=%fused_computation.48 | convolution fusion | flops 2353561600 | bytes 15533312 | tf_op jit(solution)/shard_map/rh,dh->rd/dot_general | solution.py:228
  487.9 7.9 %fusion.17 = f32[320,3584]{1,0:T(8,128)} fusion(bf16[1,3584,1024]{2,1,0:T(8,128)(2,1)} %param.20, bf16[2,320,512]{2,1,0:T(8,128)(2,1)S(1)} %get-tuple-element.96, bf16[2,320,512]{2,1,0:T(8,128)(2,1)S(1)} %get-tuple-element.95), kind=kOutput, calls=%fused_computation.21 | convolution fusion | flops 2350120960 | bytes 13238272 | tf_op jit(solution)/shard_map/rh,dh->rd/dot_general | solution.py:226
  545.7 8.6 %collective-permute-done.37 = bf16[80,3584]{1,0:T(8,128)(2,1)} collective-permute-done((bf16[80,3584]{1,0:T(8,128)(2,1)}, bf16[80,3584]{1,0:T(8,128)(2,1)}, u32[]{:S(2)}, u32[]{:S(2)}) %collective-permute-start.37) | collective-permute-done | bytes 573472 | tf_op jit(solution)/shard_map/ppermute | solution.py:43
  565.0 15.8 %collective-permute-done.39 = bf16[128,3584]{1,0:T(8,128)(2,1)S(1)} collective-permute-done((bf16[128,3584]{1,0:T(8,128)(2,1)S(1)}, bf16[128,3584]{1,0:T(8,128)(2,1)S(1)}, u32[]{:S(2)}, u32[]{:S(2)}) %collective-permute-start.39) | collective-permute-done | bytes 917536 | tf_op jit(solution)/shard_map/ppermute | solution.py:37
  586.4 22.8 %collective-permute-start.62 = (bf16[128,3584]{1,0:T(8,128)(2,1)S(1)}, bf16[128,3584]{1,0:T(8,128)(2,1)S(1)}, u32[]{:S(2)}, u32[]{:S(2)}) collective-permute-start(bf16[128,3584]{1,0:T(8,128)(2,1)S(1)} %fusion.76), channel_id=1, source_target_pairs={{0,4},{1,5},{2,6},{3,7},{4,0},{5,1},{6,2},{7,3},{8,12},{9,13},{10,... | collective-permute-start | bytes 2752520 | tf_op jit(solution)/shard_map/ppermute | solution.py:37
  610.3 10.3 %collective-permute-done.62 = bf16[128,3584]{1,0:T(8,128)(2,1)S(1)} collective-permute-done((bf16[128,3584]{1,0:T(8,128)(2,1)S(1)}, bf16[128,3584]{1,0:T(8,128)(2,1)S(1)}, u32[]{:S(2)}, u32[]{:S(2)}) %collective-permute-start.62) | collective-permute-done | bytes 917536 | tf_op jit(solution)/shard_map/ppermute | solution.py:37
  627.3 7.9 %convolution_convert_fusion.8 = bf16[128,2048]{1,0:T(8,128)(2,1)S(1)} fusion(bf16[128,3584]{1,0:T(8,128)(2,1)S(1)} %add_convert_fusion, bf16[2048,3584]{0,1:T(8,128)(2,1)} %all-gather.3.cloned.1.call-done), kind=kOutput, calls=%fused_computation.70 | convolution fusion | flops 1879310336 | bytes 16121856 | tf_op jit(solution)/shard_map/td,hd->th/dot_general | solution.py:263
  (389 shorter events, 287.4 us)
Async XLA Ops:
  7.2 260.9 %all-gather.3.cloned.1.call-start = ((), (), s32[]{:S(2)}) async-start(), calls=%async_computation.2 | async-start | bytes 15597568 | tf_op jit(solution)/shard_map/all_gather | solution.py:137
  7.9 109.0 %collective-permute-start.5 = (bf16[128,3584]{1,0:T(8,128)(2,1)}, bf16[128,3584]{1,0:T(8,128)(2,1)S(1)}, u32[]{:S(2)}, u32[]{:S(2)}) collective-permute-start(bf16[128,3584]{1,0:T(8,128)(2,1)} %param.23), channel_id=1, source_target_pairs={{0,4},{1,5},{2,6},{3,7},{4,0},{5,1},{6,2},{7,3},{8,12},{9,13},{10,... | collective-permute-start | bytes 2752520 | tf_op jit(solution)/shard_map/ppermute | solution.py:37
  11.0 112.1 %collective-permute-start.9 = (bf16[128,3584]{1,0:T(8,128)(2,1)}, bf16[128,3584]{1,0:T(8,128)(2,1)}, u32[]{:S(2)}, u32[]{:S(2)}) collective-permute-start(bf16[128,3584]{1,0:T(8,128)(2,1)} %param.23), channel_id=1, source_target_pairs={{4,8},{5,9},{6,10},{7,11},{8,4},{9,5},{10,6},{11,7},{20,24},{21,25... | collective-permute-start | bytes 2752520 | tf_op jit(solution)/shard_map/ppermute | solution.py:37
  119.6 112.9 %collective-permute-start = (bf16[128,1024]{0,1:T(8,128)(2,1)S(1)}, bf16[128,1024]{0,1:T(8,128)(2,1)}, u32[]{:S(2)}, u32[]{:S(2)}) collective-permute-start(bf16[128,1024]{0,1:T(8,128)(2,1)S(1)} %bitcast.359), channel_id=1, source_target_pairs={{0,16},{16,0},{1,17},{17,1},{2,18},{18,2},{3,19},{19,3},{4,20},{20... | collective-permute-start | bytes 786440 | tf_op jit(solution)/shard_map/ppermute | solution.py:73
  119.9 36.8 %collective-permute-start.7 = (bf16[80,3584]{1,0:T(8,128)(2,1)}, bf16[80,3584]{1,0:T(8,128)(2,1)}, u32[]{:S(2)}, u32[]{:S(2)}) collective-permute-start(bf16[80,3584]{1,0:T(8,128)(2,1)} %get-tuple-element.81), channel_id=1, source_target_pairs={{0,2},{1,3},{2,0},{3,1},{4,6},{5,7},{6,4},{7,5},{8,10},{9,11},{10,... | collective-permute-start | bytes 1720328 | tf_op jit(solution)/shard_map/ppermute | solution.py:43
  120.5 43.8 %collective-permute-start.8 = (bf16[80,3584]{1,0:T(8,128)(2,1)S(1)}, bf16[80,3584]{1,0:T(8,128)(2,1)S(1)}, u32[]{:S(2)}, u32[]{:S(2)}) collective-permute-start(bf16[80,3584]{1,0:T(8,128)(2,1)S(1)} %get-tuple-element.80), channel_id=1, source_target_pairs={{0,3},{1,2},{2,1},{3,0},{4,7},{5,6},{6,5},{7,4},{8,11},{9,10},{10,... | collective-permute-start | bytes 1720328 | tf_op jit(solution)/shard_map/ppermute | solution.py:43
  123.1 72.0 %collective-permute-start.14 = (bf16[128,3584]{1,0:T(8,128)(2,1)S(1)}, bf16[128,3584]{1,0:T(8,128)(2,1)S(1)}, u32[]{:S(2)}, u32[]{:S(2)}) collective-permute-start(bf16[128,3584]{1,0:T(8,128)(2,1)S(1)} %collective-permute-done.5), channel_id=1, source_target_pairs={{4,8},{5,9},{6,10},{7,11},{8,4},{9,5},{10,6},{11,7},{20,24},{21,25... | collective-permute-start | bytes 2752520 | tf_op jit(solution)/shard_map/ppermute | solution.py:37
  145.5 41.4 %collective-permute-start.10 = (bf16[128,3584]{1,0:T(8,128)(2,1)}, bf16[128,3584]{1,0:T(8,128)(2,1)S(1)}, u32[]{:S(2)}, u32[]{:S(2)}) collective-permute-start(bf16[128,3584]{1,0:T(8,128)(2,1)} %collective-permute-done.9), channel_id=1, source_target_pairs={{4,0},{5,1},{6,2},{7,3},{8,12},{9,13},{10,14},{11,15},{20,16},{21,... | collective-permute-start | bytes 2752520 | tf_op jit(solution)/shard_map/ppermute | solution.py:37
  192.9 33.2 %collective-permute-start.12 = (bf16[80,3584]{1,0:T(8,128)(2,1)}, bf16[80,3584]{1,0:T(8,128)(2,1)S(1)}, u32[]{:S(2)}, u32[]{:S(2)}) collective-permute-start(bf16[80,3584]{1,0:T(8,128)(2,1)} %get-tuple-element.77), channel_id=1, source_target_pairs={{0,2},{1,3},{2,0},{3,1},{4,6},{5,7},{6,4},{7,5},{8,10},{9,11},{10,... | collective-permute-start | bytes 1720328 | tf_op jit(solution)/shard_map/ppermute | solution.py:43
  194.2 32.8 %collective-permute-start.13 = (bf16[80,3584]{1,0:T(8,128)(2,1)S(1)}, bf16[80,3584]{1,0:T(8,128)(2,1)S(1)}, u32[]{:S(2)}, u32[]{:S(2)}) collective-permute-start(bf16[80,3584]{1,0:T(8,128)(2,1)S(1)} %get-tuple-element.76), channel_id=1, source_target_pairs={{0,3},{1,2},{2,1},{3,0},{4,7},{5,6},{6,5},{7,4},{8,11},{9,10},{10,... | collective-permute-start | bytes 1720328 | tf_op jit(solution)/shard_map/ppermute | solution.py:43
  195.1 32.8 %collective-permute-start.15 = (bf16[128,3584]{1,0:T(8,128)(2,1)S(1)}, bf16[128,3584]{1,0:T(8,128)(2,1)S(1)}, u32[]{:S(2)}, u32[]{:S(2)}) collective-permute-start(bf16[128,3584]{1,0:T(8,128)(2,1)S(1)} %collective-permute-done.14), channel_id=1, source_target_pairs={{4,0},{5,1},{6,2},{7,3},{8,12},{9,13},{10,14},{11,15},{20,16},{21,... | collective-permute-start | bytes 2752520 | tf_op jit(solution)/shard_map/ppermute | solution.py:37
  268.1 64.6 %collective-permute-start.19 = (bf16[1280,512]{1,0:T(8,128)(2,1)}, bf16[1280,512]{1,0:T(8,128)(2,1)}, u32[]{:S(2)}, u32[]{:S(2)}) collective-permute-start(bf16[1280,512]{1,0:T(8,128)(2,1)} %constant_dynamic-slice_fusion.1), channel_id=1, source_target_pairs={{0,16},{16,0},{1,17},{17,1},{2,18},{18,2},{3,19},{19,3},{4,20},{20... | collective-permute-start | bytes 3932168 | tf_op jit(solution)/shard_map/ppermute | solution.py:73
  281.1 46.5 %collective-permute-start.41 = (bf16[128,3584]{1,0:T(8,128)(2,1)S(1)}, bf16[128,3584]{1,0:T(8,128)(2,1)}, u32[]{:S(2)}, u32[]{:S(2)}) collective-permute-start(bf16[128,3584]{1,0:T(8,128)(2,1)S(1)} %multiply_convert_fusion), channel_id=1, source_target_pairs={{0,4},{1,5},{2,6},{3,7},{4,0},{5,1},{6,2},{7,3},{8,12},{9,13},{10,... | collective-permute-start | bytes 2752520 | tf_op jit(solution)/shard_map/ppermute | solution.py:37
  289.3 48.6 %all-to-all-start = ((f32[16,1,128]{2,1,0:T(1,128)}), f32[16,1,128]{2,1,0:T(1,128)S(1)}, u32[]{:S(2)}, u32[]{:S(2)}) async-start(f32[16,1,128]{2,1,0:T(1,128)} %bitcast.32), calls=%async_computation | async-start | bytes 16384 | tf_op jit(solution)/shard_map/all_to_all | solution.py:190
  301.3 37.7 %collective-permute-start.29 = (bf16[128,3584]{1,0:T(8,128)(2,1)S(1)}, bf16[128,3584]{1,0:T(8,128)(2,1)}, u32[]{:S(2)}, u32[]{:S(2)}) collective-permute-start(bf16[128,3584]{1,0:T(8,128)(2,1)S(1)} %multiply_convert_fusion), channel_id=1, source_target_pairs={{4,8},{5,9},{6,10},{7,11},{8,4},{9,5},{10,6},{11,7},{20,24},{21,25... | collective-permute-start | bytes 2752520 | tf_op jit(solution)/shard_map/ppermute | solution.py:37
  339.0 36.9 %collective-permute-start.50 = (bf16[128,3584]{1,0:T(8,128)(2,1)}, bf16[128,3584]{1,0:T(8,128)(2,1)S(1)}, u32[]{:S(2)}, u32[]{:S(2)}) collective-permute-start(bf16[128,3584]{1,0:T(8,128)(2,1)} %collective-permute-done.41), channel_id=1, source_target_pairs={{4,8},{5,9},{6,10},{7,11},{8,4},{9,5},{10,6},{11,7},{20,24},{21,25... | collective-permute-start | bytes 2752520 | tf_op jit(solution)/shard_map/ppermute | solution.py:37
  406.3 41.9 %collective-permute-start.34 = (bf16[2,320,512]{2,1,0:T(8,128)(2,1)S(1)}, bf16[2,320,512]{2,1,0:T(8,128)(2,1)S(1)}, u32[]{:S(2)}, u32[]{:S(2)}) collective-permute-start(bf16[2,320,512]{2,1,0:T(8,128)(2,1)S(1)} %fusion.188), channel_id=1, source_target_pairs={{0,16},{16,0},{1,17},{17,1},{2,18},{18,2},{3,19},{19,3},{4,20},{20... | collective-permute-start | bytes 1966088 | tf_op jit(solution)/shard_map/ppermute | solution.py:73
  452.7 54.0 %collective-permute-start.35 = (bf16[2,320,512]{2,1,0:T(8,128)(2,1)}, bf16[2,320,512]{2,1,0:T(8,128)(2,1)}, u32[]{:S(2)}, u32[]{:S(2)}) collective-permute-start(bf16[2,320,512]{2,1,0:T(8,128)(2,1)} %pad_maximum_fusion.9), channel_id=1, source_target_pairs={{0,16},{16,0},{1,17},{17,1},{2,18},{18,2},{3,19},{19,3},{4,20},{20... | collective-permute-start | bytes 1966088 | tf_op jit(solution)/shard_map/ppermute | solution.py:73
  453.6 33.1 %collective-permute-start.56 = (bf16[2,320,512]{2,1,0:T(8,128)(2,1)}, bf16[2,320,512]{2,1,0:T(8,128)(2,1)}, u32[]{:S(2)}, u32[]{:S(2)}) collective-permute-start(bf16[2,320,512]{2,1,0:T(8,128)(2,1)} %pad_maximum_fusion.11), channel_id=1, source_target_pairs={{0,16},{16,0},{1,17},{17,1},{2,18},{18,2},{3,19},{19,3},{4,20},{20... | collective-permute-start | bytes 1966088 | tf_op jit(solution)/shard_map/ppermute | solution.py:73
  468.0 142.2 %collective-permute-start.26 = (bf16[80,3584]{1,0:T(8,128)(2,1)}, bf16[80,3584]{1,0:T(8,128)(2,1)}, u32[]{:S(2)}, u32[]{:S(2)}) collective-permute-start(bf16[80,3584]{1,0:T(8,128)(2,1)} %get-tuple-element.59), channel_id=1, source_target_pairs={{0,1},{1,0},{2,3},{3,2},{4,5},{5,4},{6,7},{7,6},{8,9},{9,8},{10,11... | collective-permute-start | bytes 1720328 | tf_op jit(solution)/shard_map/ppermute | solution.py:43
  474.8 65.2 %all-to-all-start.1 = ((f32[16,1,128]{2,1,0:T(1,128)}), f32[16,1,128]{2,1,0:T(1,128)}, u32[]{:S(2)}, u32[]{:S(2)}) async-start(f32[16,1,128]{2,1,0:T(1,128)} %bitcast.360), calls=%async_computation.1 | async-start | bytes 16384 | tf_op jit(solution)/shard_map/all_to_all | solution.py:247
  523.0 31.3 %collective-permute-start.37 = (bf16[80,3584]{1,0:T(8,128)(2,1)}, bf16[80,3584]{1,0:T(8,128)(2,1)}, u32[]{:S(2)}, u32[]{:S(2)}) collective-permute-start(bf16[80,3584]{1,0:T(8,128)(2,1)} %get-tuple-element.46), channel_id=1, source_target_pairs={{0,2},{1,3},{2,0},{3,1},{4,6},{5,7},{6,4},{7,5},{8,10},{9,11},{10,... | collective-permute-start | bytes 1720328 | tf_op jit(solution)/shard_map/ppermute | solution.py:43
  543.8 37.8 %collective-permute-start.47 = (bf16[80,3584]{1,0:T(8,128)(2,1)}, bf16[80,3584]{1,0:T(8,128)(2,1)S(1)}, u32[]{:S(2)}, u32[]{:S(2)}) collective-permute-start(bf16[80,3584]{1,0:T(8,128)(2,1)} %get-tuple-element.55), channel_id=1, source_target_pairs={{0,1},{1,0},{2,3},{3,2},{4,5},{5,4},{6,7},{7,6},{8,9},{9,8},{10,11... | collective-permute-start | bytes 1720328 | tf_op jit(solution)/shard_map/ppermute | solution.py:43
  586.4 34.2 %collective-permute-start.62 = (bf16[128,3584]{1,0:T(8,128)(2,1)S(1)}, bf16[128,3584]{1,0:T(8,128)(2,1)S(1)}, u32[]{:S(2)}, u32[]{:S(2)}) collective-permute-start(bf16[128,3584]{1,0:T(8,128)(2,1)S(1)} %fusion.76), channel_id=1, source_target_pairs={{0,4},{1,5},{2,6},{3,7},{4,0},{5,1},{6,2},{7,3},{8,12},{9,13},{10,... | collective-permute-start | bytes 2752520 | tf_op jit(solution)/shard_map/ppermute | solution.py:37
  (108 other events, 2198.9 us)
Sparse Core Ops, SparseCore 0:
  10.8 243.1 all-gather.2

commit v2 on v1

v2 whole, which is shorter than its diff:
```python
import math

import jax
import jax.numpy as jnp
from jax import lax
from jax.sharding import PartitionSpec as P

D = 7168
HDIM = 128
TOP = 8
DEPTH = 4


route_scale = 2.5
norm_eps = 1e-06
masked_score = -1e30


def split_heads(values):
    return values.reshape(values.shape[0], values.shape[1] // HDIM, HDIM)


def softmax_rows(query_h, key_h):
    length = query_h.shape[0]
    scores = jnp.einsum("qhd,khd->hqk", query_h, key_h, preferred_element_type=jnp.float32) * (
        1.0 / math.sqrt(HDIM)
    )
    causal = jnp.arange(length)[None, :] <= jnp.arange(length)[:, None]
    scores = jnp.where(causal[None], scores, masked_score)
    highest = jnp.max(scores, axis=2, keepdims=True)
    weights_exp = jnp.exp(scores - highest)
    return weights_exp / jnp.sum(weights_exp, axis=2, keepdims=True)


def depth_permute(x, pairs, n_ep):
    plane = n_ep // DEPTH
    return lax.ppermute(
        x, "ep", [(a * plane + i, b * plane + i) for a, b in pairs for i in range(plane)]
    )


def plane_permute(x, step, n_ep):
    return lax.ppermute(x, "ep", [(i, i ^ step) for i in range(n_ep)])


SWAP = [(0, 1), (1, 0), (2, 3), (3, 2)]
MIDDLE = [(1, 2), (2, 1)]
OUTWARD = [(1, 0), (2, 3)]
INWARD = [(0, 1), (3, 2)]


class Steps:
    def __init__(self, n_ep):
        self.n_ep = n_ep
        self.held = ()

    def run(self, moves, work=None, inputs=()):
        moving = tuple(x for x, _ in moves)
        moving, inputs, self.held = lax.optimization_barrier((moving, tuple(inputs), self.held))
        arrived = [
            plane_permute(x, way, self.n_ep)
            if isinstance(way, int)
            else depth_permute(x, way, self.n_ep)
            for x, (_, way) in zip(moving, moves)
        ]
        result = () if work is None else work(*inputs)
        arrived, result = lax.optimization_barrier((arrived, result))
        self.held = (arrived, result)
        return arrived if work is None else [*arrived, result]


def to_plane(blocks):
    return [(blocks[r], r) for r in range(1, blocks.shape[0])]


def from_plane(blocks, arrived):
    return jnp.concatenate([blocks[0], *arrived], axis=0)


def tp_swap(x):
    return lax.ppermute(x, "tp", [(0, 1), (1, 0)])


def tp_sum(x):
    if lax.axis_size("tp") != 2:
        return lax.psum(x, "tp")
    return x + tp_swap(x)


def tp_reduce(x, axis):
    n_tp = lax.axis_size("tp")
    if n_tp != 2:
        return lax.psum_scatter(x, "tp", scatter_dimension=axis, tiled=True).astype(jnp.float32)
    t = lax.axis_index("tp")
    width = x.shape[axis] // 2
    mine = lax.dynamic_slice_in_dim(x, t * width, width, axis)
    other = lax.dynamic_slice_in_dim(x, (1 - t) * width, width, axis)
    return mine.astype(jnp.float32) + tp_swap(other).astype(jnp.float32)


def tp_gather(x, axis):
    n_tp = lax.axis_size("tp")
    if n_tp != 2:
        return lax.all_gather(x, "tp", axis=axis, tiled=True)
    t = lax.axis_index("tp")
    other = tp_swap(x)
    first = jnp.where(t == 0, x, other)
    second = jnp.where(t == 0, other, x)
    return jnp.concatenate([first, second], axis=axis)


def one_hot_slots(mask, capacity):
    length = mask.shape[-1]
    before = (jnp.arange(length)[:, None] < jnp.arange(length)[None, :]).astype(jnp.bfloat16)
    slots = jnp.einsum(
        "...i,ij->...j", mask.astype(jnp.bfloat16), before, preferred_element_type=jnp.float32
    )
    wanted = jnp.arange(capacity, dtype=jnp.float32)[:, None]
    return (mask[..., None, :] & (slots[..., None, :] == wanted)).astype(jnp.bfloat16)


def on_device(
    hidden_in,
    query,
    key_in,
    value_in,
    out_weight,
    norm_gain,
    router,
    routes,
    w_gate,
    w_up,
    w_down,
    grad_out,
):
    n_ep = lax.axis_size("ep")
    plane = n_ep // DEPTH
    me = lax.axis_index("ep")
    z, place = me // plane, me % plane
    n_tp, t = lax.axis_size("tp"), lax.axis_index("tp")
    length = hidden_in.shape[0]
    slice_width = hidden_in.shape[1]
    capacity = min(length, (5 * length * TOP + 4 * n_ep - 1) // (4 * n_ep))
    bf16 = jnp.bfloat16

    step = Steps(n_ep)
    steps = jnp.arange(plane, dtype=jnp.int32)
    relay_expert = z * plane + (place ^ steps)
    lanes = -(-2 * n_ep // 128) * 128

    def with_lanes(x, extra):
        extra = jnp.pad(extra.astype(bf16), ((0, 0), (0, lanes - extra.shape[1])))
        return jnp.concatenate([x, extra], axis=1)

    def pack(piece, hot):
        packed = jnp.dot(hot, piece[:, :slice_width], preferred_element_type=jnp.float32)
        return packed.astype(bf16).reshape(plane, capacity, slice_width)

    def slots_of(piece):
        named = piece[:, slice_width : slice_width + TOP].astype(jnp.int32)
        mask = jnp.any(named[None] == relay_expert[:, None, None], axis=-1)
        return one_hot_slots(mask, capacity).reshape(plane * capacity, length)

    gate_local = w_gate[0]
    up_local = w_up[0]
    down_local = w_down[0]

    def gate_up(rows):
        gate_part = jnp.dot(rows, gate_local, preferred_element_type=jnp.float32).astype(bf16)
        up_part = jnp.dot(rows, up_local, preferred_element_type=jnp.float32).astype(bf16)
        return gate_part, up_part

    def backward_part(rows):
        part = jnp.einsum("rd,hd->rh", rows, down_local, preferred_element_type=jnp.float32)
        return part.astype(bf16)

    score_lane = (jnp.arange(lanes) == me)[None, :]

    def expert_rows(gate_part, up_part, back_part):
        pre_sums = tp_reduce(jnp.stack([gate_part, up_part, back_part]), 2)
        gate_pre, up_pre, back = pre_sums[0], pre_sums[1], pre_sums[2]
        gate_sigmoid = jax.nn.sigmoid(gate_pre)
        gate_silu = gate_pre * gate_sigmoid
        hidden_b = lax.optimization_barrier((gate_silu * up_pre).astype(bf16)).astype(jnp.float32)
        score = tp_sum(jnp.sum(hidden_b * back, axis=1))[:, None]
        grad_gate = (back * up_pre * gate_sigmoid * (1.0 + gate_pre * (1.0 - gate_sigmoid))).astype(
            bf16
        )
        grad_up = (back * gate_silu).astype(bf16)
        both = tp_gather(jnp.stack([grad_gate, grad_up]), 2)
        expert_grad = jnp.einsum(
            "rh,dh->rd", both[0], gate_local, preferred_element_type=jnp.float32
        ) + jnp.einsum("rh,dh->rd", both[1], up_local, preferred_element_type=jnp.float32)
        rows = jnp.concatenate(
            [expert_grad.astype(bf16), jnp.where(score_lane, score, 0.0).astype(bf16)], axis=1
        )
        return rows.reshape(plane, capacity, -1)

    def relay_sum(hot, table, arrived):
        arrived = arrived.reshape(plane * capacity, -1)
        high = jnp.take(table, relay_expert, axis=1).T[:, None, :]
        low = jnp.take(table, n_ep + relay_expert, axis=1).T[:, None, :]
        tokens = hot.reshape(plane, capacity, length)
        mix = jnp.concatenate([tokens * high, tokens * low], axis=0).reshape(-1, length)
        row_part = arrived[:, :slice_width]
        total = jnp.einsum(
            "ri,rd->id",
            mix,
            jnp.concatenate([row_part, row_part], axis=0),
            preferred_element_type=jnp.float32,
        )
        lane_part = jnp.einsum(
            "ri,rd->id", hot, arrived[:, slice_width:], preferred_element_type=jnp.float32
        )
        return jnp.concatenate([total, lane_part], axis=1)

    def attend(query, key_in, value_in):
        probabilities = softmax_rows(split_heads(query), split_heads(key_in))
        attended = jnp.einsum(
            "hqk,khd->qhd",
            probabilities.astype(bf16),
            split_heads(value_in),
            preferred_element_type=jnp.float32,
        )
        return probabilities, attended.reshape(length, -1).astype(bf16)

    def slots_pack(piece):
        hot = slots_of(piece)
        return hot, pack(piece, hot)

    grad_own = with_lanes(grad_out, routes)
    hot_own, grad_blocks = slots_pack(grad_own)
    cols_partner, cols_near, *arrived, (probabilities, attended) = step.run(
        [(out_weight, SWAP), (out_weight, MIDDLE)] + to_plane(grad_blocks),
        attend,
        (query, key_in, value_in),
    )
    grad_rows_own = from_plane(grad_blocks, arrived)
    query_h = split_heads(query)
    key_h = split_heads(key_in)
    value_h = split_heads(value_in)
    prob_rounded = probabilities.astype(bf16)
    cols_far, outer, *arrived = step.run(
        [(cols_partner, MIDDLE), (cols_near, OUTWARD)] + [(attended, r) for r in range(1, plane)]
    )
    cols_near = cols_near + outer
    outer, grad_near, heads = step.run(
        [(cols_far, OUTWARD), (grad_own, MIDDLE)],
        lambda *parts: tp_gather(jnp.concatenate(parts, axis=0), 1),
        (attended, *arrived),
    )
    columns = jnp.concatenate([out_weight, cols_partner, cols_near, cols_far + outer], axis=1)
    column_count = out_weight.shape[1]
    sources = jnp.stack([z, z ^ 1, jnp.where(z < 2, 2, 1), jnp.where(z < 2, 3, 0)])
    column_owner = ((place ^ steps)[:, None] + sources[None, :] * plane).reshape(n_ep)
    expert_ids = jnp.arange(n_ep, dtype=jnp.int32)
    order = jnp.argmax(column_owner[None, :] == expert_ids[:, None], axis=1)

    projected = jnp.dot(heads, columns, preferred_element_type=jnp.float32).astype(bf16)
    blocks = projected.reshape(plane, length, DEPTH * column_count)
    grad_partner, *arrived = step.run(
        [(grad_own, SWAP)] + [(blocks[r], r) for r in range(1, plane)]
    )
    proj = jnp.stack([blocks[0], *arrived]).reshape(plane, length, DEPTH, column_count)
    proj = proj.transpose(0, 2, 1, 3).reshape(n_ep, length, column_count)

    def normalise(proj):
        proj = proj[order].transpose(1, 0, 2).reshape(length, slice_width)
        residual = (hidden_in.astype(jnp.float32) + proj.astype(jnp.float32)).astype(bf16)
        resid_f = residual.astype(jnp.float32)
        scaled = resid_f * norm_gain.astype(jnp.float32)
        squares = tp_sum(jnp.sum(resid_f * resid_f, axis=1))
        raw_logits = tp_sum(
            jnp.dot(scaled, router.astype(jnp.float32), precision=lax.Precision.HIGHEST)
        )
        inv_rms = lax.rsqrt(squares[:, None] / D + norm_eps)
        normed = (scaled * inv_rms).astype(bf16)
        one_hot = routes[:, :, None] == expert_ids[None, None, :]
        sigmoids = jax.nn.sigmoid(raw_logits * inv_rms)
        picked = jnp.sum(jnp.where(one_hot, sigmoids[:, None, :], 0.0), axis=2)
        totals = jnp.sum(picked, axis=1, keepdims=True)
        weights = route_scale * picked / totals
        table = jnp.sum(jnp.where(one_hot, weights[:, :, None], 0.0), axis=1)
        high = table.astype(bf16)
        low = (table - high.astype(jnp.float32)).astype(bf16)
        normed = with_lanes(normed, jnp.concatenate([high, low], axis=1))
        return residual, inv_rms, picked, totals, normed, pack(normed, hot_own)

    hot_partner, grad_blocks = slots_pack(grad_partner)
    grad_far, outer, *arrived, made = step.run(
        [(grad_partner, MIDDLE), (grad_near, OUTWARD)] + to_plane(grad_blocks),
        normalise,
        (proj,),
    )
    residual, inv_rms, picked, totals, normed_own, blocks = made
    resid_f = residual.astype(jnp.float32)
    gain_f = norm_gain.astype(jnp.float32)
    router_f = router.astype(jnp.float32)
    one_hot = routes[:, :, None] == expert_ids[None, None, :]
    grad_rows_partner = from_plane(grad_blocks, arrived)
    grad_near = grad_near + outer

    normed_partner, normed_near, *arrived, ((hot_near, grad_blocks), back_own) = step.run(
        [(normed_own, SWAP), (normed_own, MIDDLE)] + to_plane(blocks),
        lambda piece, rows: (slots_pack(piece), backward_part(rows)),
        (grad_near, grad_rows_own),
    )
    rows_own = from_plane(blocks, arrived)
    normed_far, outer, *arrived, (pre_own, blocks) = step.run(
        [(normed_partner, MIDDLE), (normed_near, OUTWARD)] + to_plane(grad_blocks),
        lambda rows, piece, hot: (gate_up(rows), pack(piece, hot)),
        (rows_own, normed_partner, hot_partner),
    )
    grad_rows_near = from_plane(grad_blocks, arrived)
    normed_near = normed_near + outer
    outer, *arrived, (back_partner, near_blocks) = step.run(
        [(grad_far, OUTWARD)] + to_plane(blocks),
        lambda rows, piece, hot: (backward_part(rows), pack(piece, hot)),
        (grad_rows_partner, normed_near, hot_near),
    )
    rows_partner = from_plane(blocks, arrived)
    grad_far = grad_far + outer
    outer, *arrived, (pre_partner, (hot_far, grad_blocks)) = step.run(
        [(normed_far, OUTWARD)] + to_plane(near_blocks),
        lambda rows, piece: (gate_up(rows), slots_pack(piece)),
        (rows_partner, grad_far),
    )
    rows_near = from_plane(near_blocks, arrived)
    normed_far = normed_far + outer
    *arrived, (pre_near, back_near, far_blocks) = step.run(
        to_plane(grad_blocks),
        lambda rows, grads, piece, hot: (gate_up(rows), backward_part(grads), pack(piece, hot)),
        (rows_near, grad_rows_near, normed_far, hot_far),
    )
    grad_rows_far = from_plane(grad_blocks, arrived)
    *arrived, (back_far, own_blocks) = step.run(
        to_plane(far_blocks),
        lambda rows, pre, back: (backward_part(rows), expert_rows(*pre, back)),
        (grad_rows_far, pre_own, back_own),
    )
    rows_far = from_plane(far_blocks, arrived)

    *arrived, (near_blocks, blocks) = step.run(
        to_plane(own_blocks),
        lambda rows, back, pre, near_back: (
            expert_rows(*pre, near_back),
            expert_rows(*gate_up(rows), back),
        ),
        (rows_far, back_far, pre_near, back_near),
    )
    own_arrived = from_plane(own_blocks, arrived)
    *arrived, (own_sum, partner_blocks) = step.run(
        to_plane(blocks),
        lambda got, table, pre, back: (
            relay_sum(hot_own, table, got),
            expert_rows(*pre, back),
        ),
        (own_arrived, normed_own[:, slice_width:], pre_partner, back_partner),
    )
    far_sum = relay_sum(hot_far, normed_far[:, slice_width:], from_plane(blocks, arrived))
    inward, *arrived = step.run([(far_sum.astype(bf16), INWARD)] + to_plane(near_blocks))
    far_sum = (far_sum + inward).astype(bf16)
    near_sum = relay_sum(hot_near, normed_near[:, slice_width:], from_plane(near_blocks, arrived))
    across, inward, *arrived = step.run(
        [(far_sum, MIDDLE), (near_sum.astype(bf16), INWARD)] + to_plane(partner_blocks)
    )
    near_sum = (near_sum + inward).astype(bf16)
    partner_sum = relay_sum(
        hot_partner, normed_partner[:, slice_width:], from_plane(partner_blocks, arrived)
    )
    partner_sum = (partner_sum + across).astype(bf16)
    near_in, partner_in = step.run([(near_sum, MIDDLE), (partner_sum, SWAP)])
    dnormed = own_sum + near_in.astype(jnp.float32) + partner_in.astype(jnp.float32)
    ret_scores = dnormed[:, slice_width : slice_width + n_ep]
    dnormed = dnormed[:, :slice_width]
    dweight = jnp.sum(jnp.where(one_hot, ret_scores[:, None, :], 0.0), axis=2)

    dpicked = (
        route_scale / totals * (dweight - jnp.sum(dweight * picked, axis=1, keepdims=True) / totals)
    )
    dlogits = jnp.sum(
        jnp.where(one_hot, (dpicked * picked * (1.0 - picked))[:, :, None], 0.0), axis=1
    )
    dnorm_f = dnormed + jnp.dot(dlogits, router_f.T, precision=lax.Precision.HIGHEST)
    gained = gain_f * dnorm_f
    inner_sum = tp_sum(jnp.sum(gained * resid_f, axis=1))[:, None]
    dresid = inv_rms * gained - resid_f * (inv_rms * inv_rms * inv_rms) * inner_sum / D
    grad_in = (grad_out.astype(jnp.float32) + dresid).astype(bf16)
    blocks = grad_in.reshape(length, n_ep, column_count).transpose(1, 0, 2)[column_owner]
    blocks = blocks.reshape(plane, DEPTH, length, column_count).transpose(0, 2, 1, 3)
    blocks = blocks.reshape(plane, length, DEPTH * column_count)
    arrived = step.run([(blocks[r], r) for r in range(1, plane)])
    partial_heads = jnp.einsum(
        "td,hd->th",
        jnp.concatenate([blocks[0], *arrived], axis=0),
        columns,
        preferred_element_type=jnp.float32,
    )
    head_sums = tp_reduce(partial_heads.astype(bf16), 1)
    blocks = head_sums.astype(bf16).reshape(plane, length, -1)
    arrived = step.run([(blocks[r], r) for r in range(1, plane)])
    grad_attn = head_sums[:length]
    for part in arrived:
        grad_attn = grad_attn + part.astype(jnp.float32)
    grad_attn = grad_attn.astype(bf16)
    grad_h = split_heads(grad_attn)
    grad_value = jnp.einsum(
        "hqk,qhd->khd", prob_rounded, grad_h, preferred_element_type=jnp.float32
    )
    grad_prob = jnp.einsum("qhd,khd->hqk", grad_h, value_h, preferred_element_type=jnp.float32)
    centre = jnp.sum(probabilities * grad_prob, axis=2, keepdims=True)
    grad_score = (probabilities * (grad_prob - centre)).astype(bf16)
    grad_query = jnp.einsum(
        "hqk,khd->qhd", grad_score, key_h, preferred_element_type=jnp.float32
    ) * (1.0 / math.sqrt(HDIM))
    grad_key = jnp.einsum(
        "hqk,qhd->khd", grad_score, query_h, preferred_element_type=jnp.float32
    ) * (1.0 / math.sqrt(HDIM))
    return (
        grad_in,
        grad_query.reshape(length, -1).astype(bf16),
        grad_key.reshape(length, -1).astype(bf16),
        grad_value.reshape(length, -1).astype(bf16),
    )


def solution(mesh):
    in_specs = (
        P("ep", "tp"),
        P("ep", "tp"),
        P("ep", "tp"),
        P("ep", "tp"),
        P(None, ("tp", "ep")),
        P("tp"),
        P("tp", None),
        P("ep", None),
        P("ep", "tp", None),
        P("ep", "tp", None),
        P("ep", None, "tp"),
        P("ep", "tp"),
    )
    out_specs = (P("ep", "tp"), P("ep", "tp"), P("ep", "tp"), P("ep", "tp"))
    return jax.shard_map(
        on_device, mesh=mesh, in_specs=in_specs, out_specs=out_specs, check_vma=False
    )
```

time: 657 us -> 592 us (0.901)
  blocking collectives: 62.1 us -> 0 us
  other arithmetic: 24.7 us -> 47 us
  waiting for transfers between devices: 249 us -> 270 us
  matrix products: 143 us -> 128 us
  between operations: 15.9 us -> 3.25 us
  local copies, waits for them, and re-layouts: 48.2 us -> 39.6 us
    all_gather x1 -> x0, blocking collectives: 62.1 us -> none  [on_device(): routes_all = lax.all_gather(routes, 'ep', axis=0)]
    ppermute x15 -> x20, waiting for transfers between devices: 47.9 us -> 84.4 us  [depth_permute(): lax.ppermute(x, 'ep', [(a * plane + i, b * plane + i) for a, b in pairs f...]
    ppermute x36 -> x48, waiting for transfers between devices: 198 us -> 180 us  [plane_permute(): return lax.ppermute(x, 'ep', [(i, i ^ step) for i in range(n_ep)])]
    dot_general x34 -> x40, matrix products: 139 us -> 124 us  [the longest x4 24.6 us: expert_rows(): jnp.einsum('rh,dh->rd', both[1], up_local, preferred_element_type=jnp.flo...]
    concatenate x0 -> x26, other arithmetic: none -> 11 us  [the longest x12 7.47 us: from_plane(): return jnp.concatenate([blocks[0], *arrived], axis=0)]
    unnamed x140 -> x163, local copies, waits for them, and re-layouts: 21 us -> 10.1 us
    convert_element_type x7 -> x27, other arithmetic: 1.07 us -> 10.8 us  [the longest x1 1.99 us: on_device(): blocks = head_sums.astype(bf16).reshape(plane, length, -1)]
    all_to_all x2 -> x0, starting transfers between devices: 9.41 us -> none  [the longest x1 4.74 us: on_device(): lax.all_to_all(weight_table.T.reshape(n_ep, 1, length), 'ep', split_axis=...]
  transfers between devices with their start and end apart: 69 -> 85, of which waited for: 27 -> 37; matrix products, arithmetic and copies ran while one was open for 30% -> 23% of each run, Pallas kernels for 0% -> 0%
where the time goes in v2:
time: 592 us; the launch traced here: 588 us
  waiting for transfers between devices  270 us (46%)
  matrix products  128 us (22%)
  starting transfers between devices  101 us (17%)
  other arithmetic  47 us (8%)
  local copies, waits for them, and re-layouts  39.6 us (7%)
    ppermute x48, waiting for transfers between devices, plane_permute(): return lax.ppermute(x, 'ep', [(i, i ^ step) for i in range(n_ep)])  180 us
    ppermute x20, waiting for transfers between devices, depth_permute(): lax.ppermute(x, 'ep', [(a * plane + i, b * plane + i) for a, b in pairs f...  84.4 us
    ppermute x48, starting transfers between devices, plane_permute(): return lax.ppermute(x, 'ep', [(i, i ^ step) for i in range(n_ep)])  56.7 us
    ppermute x20, starting transfers between devices, depth_permute(): lax.ppermute(x, 'ep', [(a * plane + i, b * plane + i) for a, b in pairs f...  40.3 us
    dot_general x4, matrix products, expert_rows(): jnp.einsum('rh,dh->rd', both[1], up_local, preferred_element_type=jnp.flo...  24.6 us
    dot_general x4, matrix products, expert_rows(): jnp.einsum('rh,dh->rd', both[0], gate_local, preferred_element_type=jnp.f...  19.8 us
    dot_general x4, matrix products, backward_part(): jnp.einsum('rd,hd->rh', rows, down_local, preferred_element_type=jnp.floa...  18.7 us
    dot_general x4, matrix products, gate_up(): jnp.dot(rows, gate_local, preferred_element_type=jnp.float32).astype(bf16)  18.4 us
  transfers between devices with their start and end apart: 85, of which 37 were waited for; matrix products, arithmetic and copies ran while one was open for 23% of the time, Pallas kernels for 0%

profile of v2, /device:TPU:0, one launch (start us, length us, event | category | flops | bytes accessed | tf_op | source)
XLA Modules:
  0.0 587.5 jit_solution(5451977300118195918)
XLA Ops:
  17.7 9.1 %collective-permute-done.2 = bf16[80,3584]{1,0:T(8,128)(2,1)S(1)} collective-permute-done((bf16[80,3584]{1,0:T(8,128)(2,1)}, bf16[80,3584]{1,0:T(8,128)(2,1)S(1)}, u32[]{:S(2)}, u32[]{:S(2)}) %collective-permute-start.2) | collective-permute-done | bytes 573472 | tf_op jit(solution)/shard_map/ppermute | solution.py:43
  26.8 12.1 %collective-permute-done.3 = bf16[80,3584]{1,0:T(8,128)(2,1)} collective-permute-done((bf16[80,3584]{1,0:T(8,128)(2,1)}, bf16[80,3584]{1,0:T(8,128)(2,1)}, u32[]{:S(2)}, u32[]{:S(2)}) %collective-permute-start.3) | collective-permute-done | bytes 573472 | tf_op jit(solution)/shard_map/ppermute | solution.py:43
  56.0 8.7 %collective-permute-done.6 = bf16[2048,224]{0,1:T(8,128)(2,1)} collective-permute-done((bf16[2048,224]{0,1:T(8,128)(2,1)}, bf16[2048,224]{0,1:T(8,128)(2,1)}, u32[]{:S(2)}, u32[]{:S(2)}) %collective-permute-start.6) | collective-permute-done | bytes 917536 | tf_op jit(solution)/shard_map/ppermute | solution.py:37
  72.3 19.7 %collective-permute-done.10 = bf16[2048,224]{0,1:T(8,128)(2,1)S(1)} collective-permute-done((bf16[2048,224]{0,1:T(8,128)(2,1)}, bf16[2048,224]{0,1:T(8,128)(2,1)S(1)}, u32[]{:S(2)}, u32[]{:S(2)}) %collective-permute-start.10) | collective-permute-done | bytes 917536 | tf_op jit(solution)/shard_map/ppermute | solution.py:37
  112.0 8.7 %collective-permute-done.13 = bf16[128,3712]{0,1:T(8,128)(2,1)} collective-permute-done((bf16[128,3712]{0,1:T(8,128)(2,1)S(1)}, bf16[128,3712]{0,1:T(8,128)(2,1)}, u32[]{:S(2)}, u32[]{:S(2)}) %collective-permute-start.13) | collective-permute-done | bytes 950304 | tf_op jit(solution)/shard_map/ppermute | solution.py:37
  136.2 12.6 %collective-permute-start.17 = (bf16[128,3712]{0,1:T(8,128)(2,1)}, bf16[128,3712]{0,1:T(8,128)(2,1)}, u32[]{:S(2)}, u32[]{:S(2)}) collective-permute-start(bf16[128,3712]{0,1:T(8,128)(2,1)} %collective-permute-done.13), channel_id=1, source_target_pairs={{4,8},{5,9},{6,10},{7,11},{8,4},{9,5},{10,6},{11,7},{20,24},{21,25... | collective-permute-start | bytes 2850824 | tf_op jit(solution)/shard_map/ppermute | solution.py:37
  153.3 21.6 %collective-permute-done.18 = bf16[128,3712]{0,1:T(8,128)(2,1)} collective-permute-done((bf16[128,3712]{0,1:T(8,128)(2,1)}, bf16[128,3712]{0,1:T(8,128)(2,1)}, u32[]{:S(2)}, u32[]{:S(2)}) %collective-permute-start.18) | collective-permute-done | bytes 950304 | tf_op jit(solution)/shard_map/ppermute | solution.py:37
  193.0 11.6 %collective-permute-done.27 = bf16[80,3584]{1,0:T(8,128)(2,1)S(1)} collective-permute-done((bf16[80,3584]{1,0:T(8,128)(2,1)S(1)}, bf16[80,3584]{1,0:T(8,128)(2,1)S(1)}, u32[]{:S(2)}, u32[]{:S(2)}) %collective-permute-start.27) | collective-permute-done | bytes 573472 | tf_op jit(solution)/shard_map/ppermute | solution.py:43
  220.9 9.5 %collective-permute-done.32 = bf16[80,3584]{1,0:T(8,128)(2,1)S(1)} collective-permute-done((bf16[80,3584]{1,0:T(8,128)(2,1)S(1)}, bf16[80,3584]{1,0:T(8,128)(2,1)S(1)}, u32[]{:S(2)}, u32[]{:S(2)}) %collective-permute-start.32) | collective-permute-done | bytes 573472 | tf_op jit(solution)/shard_map/ppermute | solution.py:43
  241.0 6.8 %collective-permute-done.35 = bf16[80,3584]{1,0:T(8,128)(2,1)S(1)} collective-permute-done((bf16[80,3584]{1,0:T(8,128)(2,1)S(1)}, bf16[80,3584]{1,0:T(8,128)(2,1)S(1)}, u32[]{:S(2)}, u32[]{:S(2)}) %collective-permute-start.35) | collective-permute-done | bytes 573472 | tf_op jit(solution)/shard_map/ppermute | solution.py:43
  247.8 8.7 %collective-permute-done.36 = bf16[80,3584]{1,0:T(8,128)(2,1)S(1)} collective-permute-done((bf16[80,3584]{1,0:T(8,128)(2,1)S(1)}, bf16[80,3584]{1,0:T(8,128)(2,1)S(1)}, u32[]{:S(2)}, u32[]{:S(2)}) %collective-permute-start.36) | collective-permute-done | bytes 573472 | tf_op jit(solution)/shard_map/ppermute | solution.py:43
  262.2 6.6 %fusion.124 = bf16[320,1024]{1,0:T(8,128)(2,1)} fusion(bf16[320,3584]{1,0:T(8,128)(2,1)S(1)} %pad_maximum_fusion.12, bf16[1,3584,1024]{2,1,0:T(8,128)(2,1)} %param.23), kind=kOutput, calls=%fused_computation.152 | convolution fusion | flops 2349137920 | bytes 10289152 | tf_op jit(solution)/shard_map/dot_general | solution.py:170
  271.3 6.6 %fusion.112 = bf16[320,1024]{1,0:T(8,128)(2,1)} fusion(bf16[320,3584]{1,0:T(8,128)(2,1)S(1)} %pad_maximum_fusion.12, bf16[1,3584,1024]{2,1,0:T(8,128)(2,1)} %param.22), kind=kOutput, calls=%fused_computation.148 | convolution fusion | flops 2349137920 | bytes 10289152 | tf_op jit(solution)/shard_map/dot_general | solution.py:169
  287.0 6.6 %fusion.127 = bf16[320,1024]{1,0:T(8,128)(2,1)} fusion(bf16[320,3584]{1,0:T(8,128)(2,1)S(1)} %pad_maximum_fusion.13, bf16[1,3584,1024]{2,1,0:T(8,128)(2,1)} %param.23), kind=kOutput, calls=%fused_computation.153 | convolution fusion | flops 2349137920 | bytes 10289152 | tf_op jit(solution)/shard_map/dot_general | solution.py:170
  313.6 8.2 %collective-permute-done.43 = bf16[80,3584]{1,0:T(8,128)(2,1)S(1)} collective-permute-done((bf16[80,3584]{1,0:T(8,128)(2,1)S(1)}, bf16[80,3584]{1,0:T(8,128)(2,1)S(1)}, u32[]{:S(2)}, u32[]{:S(2)}) %collective-permute-start.43) | collective-permute-done | bytes 573472 | tf_op jit(solution)/shard_map/ppermute | solution.py:43
  382.7 7.9 %fusion.23 = f32[320,3584]{1,0:T(8,128)} fusion(bf16[1,3584,1024]{2,1,0:T(8,128)(2,1)} %param.22, bf16[2,320,512]{2,1,0:T(8,128)(2,1)S(1)} %get-tuple-element.514, bf16[2,320,512]{2,1,0:T(8,128)(2,1)S(1)} %get-tuple-element.513), kind=kOutput, calls=%fused_computation.33 | convolution fusion | flops 2350120960 | bytes 13238272 | tf_op jit(solution)/shard_map/rh,dh->rd/dot_general | solution.py:191
  390.6 7.0 %fusion.59 = bf16[320,3584]{1,0:T(8,128)(2,1)S(1)} fusion(f32[320,3584]{1,0:T(8,128)} %fusion.23, bf16[1,3584,1024]{2,1,0:T(8,128)(2,1)} %param.23, bf16[2,320,512]{2,1,0:T(8,128)(2,1)S(1)} %get-tuple-element.513, bf16[2,320,512]{2,1,0:T(8,128)(2,1)S(1)} %get-tuple-element.514), kind=kOutput, calls=%fused_computation.57 | convolution fusion | flops 2352414720 | bytes 15532032 | tf_op jit(solution)/shard_map/rh,dh->rd/dot_general | solution.py:193
  402.3 7.0 %fusion.56 = bf16[320,3584]{1,0:T(8,128)(2,1)S(1)} fusion(f32[320,3584]{1,0:T(8,128)} %fusion.19, bf16[1,3584,1024]{2,1,0:T(8,128)(2,1)} %param.23, bf16[2,320,512]{2,1,0:T(8,128)(2,1)S(1)} %get-tuple-element.511, bf16[2,320,512]{2,1,0:T(8,128)(2,1)S(1)} %get-tuple-element.512), kind=kOutput, calls=%fused_computation.56 | convolution fusion | flops 2352414720 | bytes 15532032 | tf_op jit(solution)/shard_map/rh,dh->rd/dot_general | solution.py:193
  437.3 6.9 %collective-permute-done.61 = bf16[80,3712]{1,0:T(8,128)(2,1)S(1)} collective-permute-done((bf16[80,3712]{1,0:T(8,128)(2,1)}, bf16[80,3712]{1,0:T(8,128)(2,1)S(1)}, u32[]{:S(2)}, u32[]{:S(2)}) %collective-permute-start.61) | collective-permute-done | bytes 593952 | tf_op jit(solution)/shard_map/ppermute | solution.py:43
  451.2 11.2 %collective-permute-done.67 = bf16[80,3712]{1,0:T(8,128)(2,1)S(1)} collective-permute-done((bf16[80,3712]{1,0:T(8,128)(2,1)S(1)}, bf16[80,3712]{1,0:T(8,128)(2,1)S(1)}, u32[]{:S(2)}, u32[]{:S(2)}) %collective-permute-start.67) | collective-permute-done | bytes 593952 | tf_op jit(solution)/shard_map/ppermute | solution.py:43
  462.4 12.4 %collective-permute-done.68 = bf16[80,3712]{1,0:T(8,128)(2,1)S(1)} collective-permute-done((bf16[80,3712]{1,0:T(8,128)(2,1)S(1)}, bf16[80,3712]{1,0:T(8,128)(2,1)S(1)}, u32[]{:S(2)}, u32[]{:S(2)}) %collective-permute-start.68) | collective-permute-done | bytes 593952 | tf_op jit(solution)/shard_map/ppermute | solution.py:43
  487.4 12.8 %collective-permute-done.72 = bf16[80,3712]{1,0:T(8,128)(2,1)S(1)} collective-permute-done((bf16[80,3712]{1,0:T(8,128)(2,1)S(1)}, bf16[80,3712]{1,0:T(8,128)(2,1)S(1)}, u32[]{:S(2)}, u32[]{:S(2)}) %collective-permute-start.72) | collective-permute-done | bytes 593952 | tf_op jit(solution)/shard_map/ppermute | solution.py:43
  500.1 9.4 %collective-permute-done.73 = bf16[80,3712]{1,0:T(8,128)(2,1)S(1)} collective-permute-done((bf16[80,3712]{1,0:T(8,128)(2,1)S(1)}, bf16[80,3712]{1,0:T(8,128)(2,1)S(1)}, u32[]{:S(2)}, u32[]{:S(2)}) %collective-permute-start.73) | collective-permute-done | bytes 593952 | tf_op jit(solution)/shard_map/ppermute | solution.py:43
  513.8 19.2 %collective-permute-done.76 = bf16[128,3712]{1,0:T(8,128)(2,1)} collective-permute-done((bf16[128,3712]{1,0:T(8,128)(2,1)S(1)}, bf16[128,3712]{1,0:T(8,128)(2,1)}, u32[]{:S(2)}, u32[]{:S(2)}) %collective-permute-start.76) | collective-permute-done | bytes 950304 | tf_op jit(solution)/shard_map/ppermute | solution.py:37
  (555 shorter events, 333.5 us)
Async XLA Ops:
  6.1 32.9 %collective-permute-start = (bf16[2048,224]{0,1:T(8,128)(2,1)}, bf16[2048,224]{0,1:T(8,128)(2,1)}, u32[]{:S(2)}, u32[]{:S(2)}) collective-permute-start(bf16[2048,224]{0,1:T(8,128)(2,1)} %param.18), channel_id=1, source_target_pairs={{0,4},{1,5},{2,6},{3,7},{4,0},{5,1},{6,2},{7,3},{8,12},{9,13},{10,... | collective-permute-start | bytes 2752520 | tf_op jit(solution)/shard_map/ppermute | solution.py:37
  9.1 29.8 %collective-permute-start.1 = (bf16[2048,224]{0,1:T(8,128)(2,1)}, bf16[2048,224]{0,1:T(8,128)(2,1)}, u32[]{:S(2)}, u32[]{:S(2)}) collective-permute-start(bf16[2048,224]{0,1:T(8,128)(2,1)} %param.18), channel_id=1, source_target_pairs={{4,8},{5,9},{6,10},{7,11},{8,4},{9,5},{10,6},{11,7},{20,24},{21,25... | collective-permute-start | bytes 2752520 | tf_op jit(solution)/shard_map/ppermute | solution.py:37
  12.2 26.8 %collective-permute-start.3 = (bf16[80,3584]{1,0:T(8,128)(2,1)}, bf16[80,3584]{1,0:T(8,128)(2,1)}, u32[]{:S(2)}, u32[]{:S(2)}) collective-permute-start(bf16[80,3584]{1,0:T(8,128)(2,1)} %get-tuple-element.212), channel_id=1, source_target_pairs={{0,2},{1,3},{2,0},{3,1},{4,6},{5,7},{6,4},{7,5},{8,10},{9,11},{10,... | collective-permute-start | bytes 1720328 | tf_op jit(solution)/shard_map/ppermute | solution.py:43
  13.7 25.2 %collective-permute-start.4 = (bf16[80,3584]{1,0:T(8,128)(2,1)}, bf16[80,3584]{1,0:T(8,128)(2,1)}, u32[]{:S(2)}, u32[]{:S(2)}) collective-permute-start(bf16[80,3584]{1,0:T(8,128)(2,1)} %get-tuple-element.213), channel_id=1, source_target_pairs={{0,3},{1,2},{2,1},{3,0},{4,7},{5,6},{6,5},{7,4},{8,11},{9,10},{10,... | collective-permute-start | bytes 1720328 | tf_op jit(solution)/shard_map/ppermute | solution.py:43
  65.1 27.0 %collective-permute-start.11 = (bf16[128,3712]{0,1:T(8,128)(2,1)}, bf16[128,3712]{0,1:T(8,128)(2,1)}, u32[]{:S(2)}, u32[]{:S(2)}) collective-permute-start(bf16[128,3712]{0,1:T(8,128)(2,1)} %fusion.145), channel_id=1, source_target_pairs={{4,8},{5,9},{6,10},{7,11},{8,4},{9,5},{10,6},{11,7},{20,24},{21,25... | collective-permute-start | bytes 2850824 | tf_op jit(solution)/shard_map/ppermute | solution.py:37
  125.8 26.1 %collective-permute-start.19 = (bf16[80,3584]{1,0:T(8,128)(2,1)}, bf16[80,3584]{1,0:T(8,128)(2,1)}, u32[]{:S(2)}, u32[]{:S(2)}) collective-permute-start(bf16[80,3584]{1,0:T(8,128)(2,1)} %get-tuple-element.253), channel_id=1, source_target_pairs={{0,1},{1,0},{2,3},{3,2},{4,5},{5,4},{6,7},{7,6},{8,9},{9,8},{10,11... | collective-permute-start | bytes 1720328 | tf_op jit(solution)/shard_map/ppermute | solution.py:43
  127.3 26.0 %collective-permute-start.20 = (bf16[80,3584]{1,0:T(8,128)(2,1)}, bf16[80,3584]{1,0:T(8,128)(2,1)}, u32[]{:S(2)}, u32[]{:S(2)}) collective-permute-start(bf16[80,3584]{1,0:T(8,128)(2,1)} %get-tuple-element.254), channel_id=1, source_target_pairs={{0,2},{1,3},{2,0},{3,1},{4,6},{5,7},{6,4},{7,5},{8,10},{9,11},{10,... | collective-permute-start | bytes 1720328 | tf_op jit(solution)/shard_map/ppermute | solution.py:43
  127.9 25.4 %collective-permute-start.21 = (bf16[80,3584]{1,0:T(8,128)(2,1)}, bf16[80,3584]{1,0:T(8,128)(2,1)}, u32[]{:S(2)}, u32[]{:S(2)}) collective-permute-start(bf16[80,3584]{1,0:T(8,128)(2,1)} %get-tuple-element.255), channel_id=1, source_target_pairs={{0,3},{1,2},{2,1},{3,0},{4,7},{5,6},{6,5},{7,4},{8,11},{9,10},{10,... | collective-permute-start | bytes 1720328 | tf_op jit(solution)/shard_map/ppermute | solution.py:43
  149.8 25.2 %collective-permute-start.18 = (bf16[128,3712]{0,1:T(8,128)(2,1)}, bf16[128,3712]{0,1:T(8,128)(2,1)}, u32[]{:S(2)}, u32[]{:S(2)}) collective-permute-start(bf16[128,3712]{0,1:T(8,128)(2,1)} %collective-permute-done.11), channel_id=1, source_target_pairs={{4,0},{5,1},{6,2},{7,3},{8,12},{9,13},{10,14},{11,15},{20,16},{21,... | collective-permute-start | bytes 2850824 | tf_op jit(solution)/shard_map/ppermute | solution.py:37
  178.5 26.1 %collective-permute-start.27 = (bf16[80,3584]{1,0:T(8,128)(2,1)S(1)}, bf16[80,3584]{1,0:T(8,128)(2,1)S(1)}, u32[]{:S(2)}, u32[]{:S(2)}) collective-permute-start(bf16[80,3584]{1,0:T(8,128)(2,1)S(1)} %get-tuple-element.272), channel_id=1, source_target_pairs={{0,2},{1,3},{2,0},{3,1},{4,6},{5,7},{6,4},{7,5},{8,10},{9,11},{10,... | collective-permute-start | bytes 1720328 | tf_op jit(solution)/shard_map/ppermute | solution.py:43
  179.0 25.5 %collective-permute-start.28 = (bf16[80,3584]{1,0:T(8,128)(2,1)S(1)}, bf16[80,3584]{1,0:T(8,128)(2,1)S(1)}, u32[]{:S(2)}, u32[]{:S(2)}) collective-permute-start(bf16[80,3584]{1,0:T(8,128)(2,1)S(1)} %get-tuple-element.273), channel_id=1, source_target_pairs={{0,3},{1,2},{2,1},{3,0},{4,7},{5,6},{6,5},{7,4},{8,11},{9,10},{10,... | collective-permute-start | bytes 1720328 | tf_op jit(solution)/shard_map/ppermute | solution.py:43
  327.6 25.9 %collective-permute-start.46 = (bf16[80,3584]{1,0:T(8,128)(2,1)}, bf16[80,3584]{1,0:T(8,128)(2,1)S(1)}, u32[]{:S(2)}, u32[]{:S(2)}) collective-permute-start(bf16[80,3584]{1,0:T(8,128)(2,1)} %get-tuple-element.342), channel_id=1, source_target_pairs={{0,2},{1,3},{2,0},{3,1},{4,6},{5,7},{6,4},{7,5},{8,10},{9,11},{10,... | collective-permute-start | bytes 1720328 | tf_op jit(solution)/shard_map/ppermute | solution.py:43
  328.2 27.0 %collective-permute-start.47 = (bf16[80,3584]{1,0:T(8,128)(2,1)}, bf16[80,3584]{1,0:T(8,128)(2,1)S(1)}, u32[]{:S(2)}, u32[]{:S(2)}) collective-permute-start(bf16[80,3584]{1,0:T(8,128)(2,1)} %get-tuple-element.343), channel_id=1, source_target_pairs={{0,3},{1,2},{2,1},{3,0},{4,7},{5,6},{6,5},{7,4},{8,11},{9,10},{10,... | collective-permute-start | bytes 1720328 | tf_op jit(solution)/shard_map/ppermute | solution.py:43
  371.9 37.7 %collective-permute-start.51 = (bf16[80,3712]{1,0:T(8,128)(2,1)}, bf16[80,3712]{1,0:T(8,128)(2,1)S(1)}, u32[]{:S(2)}, u32[]{:S(2)}) collective-permute-start(bf16[80,3712]{1,0:T(8,128)(2,1)} %get-tuple-element.353), channel_id=1, source_target_pairs={{0,1},{1,0},{2,3},{3,2},{4,5},{5,4},{6,7},{7,6},{8,9},{9,8},{10,11... | collective-permute-start | bytes 1781768 | tf_op jit(solution)/shard_map/ppermute | solution.py:43
  372.6 37.1 %collective-permute-start.52 = (bf16[80,3712]{1,0:T(8,128)(2,1)}, bf16[80,3712]{1,0:T(8,128)(2,1)S(1)}, u32[]{:S(2)}, u32[]{:S(2)}) collective-permute-start(bf16[80,3712]{1,0:T(8,128)(2,1)} %get-tuple-element.354), channel_id=1, source_target_pairs={{0,2},{1,3},{2,0},{3,1},{4,6},{5,7},{6,4},{7,5},{8,10},{9,11},{10,... | collective-permute-start | bytes 1781768 | tf_op jit(solution)/shard_map/ppermute | solution.py:43
  381.0 28.7 %collective-permute-start.53 = (bf16[80,3712]{1,0:T(8,128)(2,1)S(1)}, bf16[80,3712]{1,0:T(8,128)(2,1)S(1)}, u32[]{:S(2)}, u32[]{:S(2)}) collective-permute-start(bf16[80,3712]{1,0:T(8,128)(2,1)S(1)} %copy-done.31), channel_id=1, source_target_pairs={{0,3},{1,2},{2,1},{3,0},{4,7},{5,6},{6,5},{7,4},{8,11},{9,10},{10,... | collective-permute-start | bytes 1781768 | tf_op jit(solution)/shard_map/ppermute | solution.py:43
  415.9 28.3 %collective-permute-start.61 = (bf16[80,3712]{1,0:T(8,128)(2,1)}, bf16[80,3712]{1,0:T(8,128)(2,1)S(1)}, u32[]{:S(2)}, u32[]{:S(2)}) collective-permute-start(bf16[80,3712]{1,0:T(8,128)(2,1)} %get-tuple-element.367), channel_id=1, source_target_pairs={{0,2},{1,3},{2,0},{3,1},{4,6},{5,7},{6,4},{7,5},{8,10},{9,11},{10,... | collective-permute-start | bytes 1781768 | tf_op jit(solution)/shard_map/ppermute | solution.py:43
  417.6 26.5 %collective-permute-start.62 = (bf16[80,3712]{1,0:T(8,128)(2,1)}, bf16[80,3712]{1,0:T(8,128)(2,1)S(1)}, u32[]{:S(2)}, u32[]{:S(2)}) collective-permute-start(bf16[80,3712]{1,0:T(8,128)(2,1)} %get-tuple-element.368), channel_id=1, source_target_pairs={{0,3},{1,2},{2,1},{3,0},{4,7},{5,6},{6,5},{7,4},{8,11},{9,10},{10,... | collective-permute-start | bytes 1781768 | tf_op jit(solution)/shard_map/ppermute | solution.py:43
  447.5 27.3 %collective-permute-start.68 = (bf16[80,3712]{1,0:T(8,128)(2,1)S(1)}, bf16[80,3712]{1,0:T(8,128)(2,1)S(1)}, u32[]{:S(2)}, u32[]{:S(2)}) collective-permute-start(bf16[80,3712]{1,0:T(8,128)(2,1)S(1)} %get-tuple-element.381), channel_id=1, source_target_pairs={{0,2},{1,3},{2,0},{3,1},{4,6},{5,7},{6,4},{7,5},{8,10},{9,11},{10,... | collective-permute-start | bytes 1781768 | tf_op jit(solution)/shard_map/ppermute | solution.py:43
  448.1 26.6 %collective-permute-start.69 = (bf16[80,3712]{1,0:T(8,128)(2,1)S(1)}, bf16[80,3712]{1,0:T(8,128)(2,1)S(1)}, u32[]{:S(2)}, u32[]{:S(2)}) collective-permute-start(bf16[80,3712]{1,0:T(8,128)(2,1)S(1)} %get-tuple-element.382), channel_id=1, source_target_pairs={{0,3},{1,2},{2,1},{3,0},{4,7},{5,6},{6,5},{7,4},{8,11},{9,10},{10,... | collective-permute-start | bytes 1781768 | tf_op jit(solution)/shard_map/ppermute | solution.py:43
  449.5 25.2 %collective-permute-start.66 = (bf16[128,3712]{1,0:T(8,128)(2,1)S(1)}, bf16[128,3712]{1,0:T(8,128)(2,1)S(1)}, u32[]{:S(2)}, u32[]{:S(2)}) collective-permute-start(bf16[128,3712]{1,0:T(8,128)(2,1)S(1)} %fusion.96), channel_id=1, source_target_pairs={{0,4},{1,5},{2,6},{3,7},{12,8},{13,9},{14,10},{15,11},{16,20},{17,... | collective-permute-start | bytes 2850824 | tf_op jit(solution)/shard_map/ppermute | solution.py:37
  476.8 32.8 %collective-permute-start.70 = (bf16[128,3712]{1,0:T(8,128)(2,1)S(1)}, bf16[128,3712]{1,0:T(8,128)(2,1)S(1)}, u32[]{:S(2)}, u32[]{:S(2)}) collective-permute-start(bf16[128,3712]{1,0:T(8,128)(2,1)S(1)} %add_convert_fusion.1), channel_id=1, source_target_pairs={{4,8},{5,9},{6,10},{7,11},{8,4},{9,5},{10,6},{11,7},{20,24},{21,25... | collective-permute-start | bytes 2850824 | tf_op jit(solution)/shard_map/ppermute | solution.py:37
  477.5 32.0 %collective-permute-start.71 = (bf16[128,3712]{1,0:T(8,128)(2,1)S(1)}, bf16[128,3712]{1,0:T(8,128)(2,1)S(1)}, u32[]{:S(2)}, u32[]{:S(2)}) collective-permute-start(bf16[128,3712]{1,0:T(8,128)(2,1)S(1)} %fusion.95), channel_id=1, source_target_pairs={{0,4},{1,5},{2,6},{3,7},{12,8},{13,9},{14,10},{15,11},{16,20},{17,... | collective-permute-start | bytes 2850824 | tf_op jit(solution)/shard_map/ppermute | solution.py:37
  484.2 25.4 %collective-permute-start.73 = (bf16[80,3712]{1,0:T(8,128)(2,1)S(1)}, bf16[80,3712]{1,0:T(8,128)(2,1)S(1)}, u32[]{:S(2)}, u32[]{:S(2)}) collective-permute-start(bf16[80,3712]{1,0:T(8,128)(2,1)S(1)} %get-tuple-element.390), channel_id=1, source_target_pairs={{0,2},{1,3},{2,0},{3,1},{4,6},{5,7},{6,4},{7,5},{8,10},{9,11},{10,... | collective-permute-start | bytes 1781768 | tf_op jit(solution)/shard_map/ppermute | solution.py:43
  (140 other events, 1882.5 us)

commit v3 on v2

--- a/solution.py
+++ b/solution.py
@@ -3,6 +3,8 @@
 import jax
 import jax.numpy as jnp
 from jax import lax
+from jax.experimental import pallas as pl
+from jax.experimental.pallas import tpu as pltpu
 from jax.sharding import PartitionSpec as P
 
 D = 7168
@@ -47,6 +49,67 @@
 MIDDLE = [(1, 2), (2, 1)]
 OUTWARD = [(1, 0), (2, 3)]
 INWARD = [(0, 1), (3, 2)]
+
+
+HINT = pl.CostEstimate(flops=1 << 20, bytes_accessed=1 << 16, transcendentals=0)
+PARAMS = pltpu.CompilerParams(vmem_limit_bytes=30 << 20)
+
+
+def whole(array):
+    return pl.BlockSpec(array.shape, lambda i: (0, 0))
+
+
+def products_kernel(rows_ref, *refs):
+    half = len(refs) // 2
+    for weight_ref, out_ref in zip(refs[:half], refs[half:]):
+        out_ref[...] = jnp.dot(
+            rows_ref[...], weight_ref[...], preferred_element_type=jnp.float32
+        ).astype(out_ref.dtype)
+
+
+def products(rows, *weights):
+    count, depth = rows.shape
+    width = weights[0].shape[1]
+    tile = math.gcd(width, 256)
+    return pl.pallas_call(
+        products_kernel,
+        grid=(width // tile,),
+        in_specs=[whole(rows)] + [pl.BlockSpec((depth, tile), lambda i: (0, i))] * len(weights),
+        out_specs=[pl.BlockSpec((count, tile), lambda i: (0, i))] * len(weights),
+        out_shape=[jax.ShapeDtypeStruct((count, width), jnp.bfloat16)] * len(weights),
+        compiler_params=PARAMS,
+        cost_estimate=HINT,
+    )(rows, *weights)
+
+
+def summed_kernel(*refs):
+    half = len(refs) // 2
+    total = None
+    for rows_ref, weight_ref in zip(refs[:half], refs[half : 2 * half]):
+        part = lax.dot_general(
+            rows_ref[...],
+            weight_ref[...],
+            (((1,), (1,)), ((), ())),
+            preferred_element_type=jnp.float32,
+        )
+        total = part if total is None else total + part
+    refs[-1][...] = total.astype(refs[-1].dtype)
+
+
+def summed_products(rows, weights):
+    count, depth = rows[0].shape
+    height = weights[0].shape[0]
+    tile = math.gcd(height, 512 if depth <= 1024 else 256)
+    return pl.pallas_call(
+        summed_kernel,
+        grid=(height // tile,),
+        in_specs=[whole(x) for x in rows]
+        + [pl.BlockSpec((tile, depth), lambda i: (i, 0))] * len(weights),
+        out_specs=pl.BlockSpec((count, tile), lambda i: (0, i)),
+        out_shape=jax.ShapeDtypeStruct((count, height), jnp.bfloat16),
+        compiler_params=PARAMS,
+        cost_estimate=HINT,
+    )(*rows, *weights)
 
 
 class Steps:
@@ -146,7 +209,7 @@
     step = Steps(n_ep)
     steps = jnp.arange(plane, dtype=jnp.int32)
     relay_expert = z * plane + (place ^ steps)
-    lanes = -(-2 * n_ep // 128) * 128
+    lanes = -(-(2 * n_ep + TOP) // 128) * 128
 
     def with_lanes(x, extra):
         extra = jnp.pad(extra.astype(bf16), ((0, 0), (0, lanes - extra.shape[1])))
@@ -156,8 +219,9 @@
         packed = jnp.dot(hot, piece[:, :slice_width], preferred_element_type=jnp.float32)
         return packed.astype(bf16).reshape(plane, capacity, slice_width)
 
-    def slots_of(piece):
-        named = piece[:, slice_width : slice_width + TOP].astype(jnp.int32)
+    def slots_of(piece, first=0):
+        first += slice_width
+        named = piece[:, first : first + TOP].astype(jnp.int32)
         mask = jnp.any(named[None] == relay_expert[:, None, None], axis=-1)
         return one_hot_slots(mask, capacity).reshape(plane * capacity, length)
 
@@ -166,13 +230,10 @@
     down_local = w_down[0]
 
     def gate_up(rows):
-        gate_part = jnp.dot(rows, gate_local, preferred_element_type=jnp.float32).astype(bf16)
-        up_part = jnp.dot(rows, up_local, preferred_element_type=jnp.float32).astype(bf16)
-        return gate_part, up_part
+        return products(rows, gate_local, up_local)
 
     def backward_part(rows):
-        part = jnp.einsum("rd,hd->rh", rows, down_local, preferred_element_type=jnp.float32)
-        return part.astype(bf16)
+        return summed_products([rows], [down_local])
 
     score_lane = (jnp.arange(lanes) == me)[None, :]
 
@@ -188,11 +249,9 @@
         )
         grad_up = (back * gate_silu).astype(bf16)
         both = tp_gather(jnp.stack([grad_gate, grad_up]), 2)
-        expert_grad = jnp.einsum(
-            "rh,dh->rd", both[0], gate_local, preferred_element_type=jnp.float32
-        ) + jnp.einsum("rh,dh->rd", both[1], up_local, preferred_element_type=jnp.float32)
+        expert_grad = summed_products([both[0], both[1]], [gate_local, up_local])
         rows = jnp.concatenate(
-            [expert_grad.astype(bf16), jnp.where(score_lane, score, 0.0).astype(bf16)], axis=1
+            [expert_grad, jnp.where(score_lane, score, 0.0).astype(bf16)], axis=1
         )
         return rows.reshape(plane, capacity, -1)
 
@@ -229,13 +288,11 @@
         return hot, pack(piece, hot)
 
     grad_own = with_lanes(grad_out, routes)
-    hot_own, grad_blocks = slots_pack(grad_own)
-    cols_partner, cols_near, *arrived, (probabilities, attended) = step.run(
-        [(out_weight, SWAP), (out_weight, MIDDLE)] + to_plane(grad_blocks),
-        attend,
-        (query, key_in, value_in),
-    )
-    grad_rows_own = from_plane(grad_blocks, arrived)
+    cols_partner, cols_near, ((probabilities, attended), (hot_own, grad_blocks)) = step.run(
+        [(out_weight, SWAP), (out_weight, MIDDLE)],
+        lambda *given: (attend(*given[:3]), slots_pack(given[3])),
+        (query, key_in, value_in, grad_own),
+    )
     query_h = split_heads(query)
     key_h = split_heads(key_in)
     value_h = split_heads(value_in)
@@ -244,11 +301,12 @@
         [(cols_partner, MIDDLE), (cols_near, OUTWARD)] + [(attended, r) for r in range(1, plane)]
     )
     cols_near = cols_near + outer
-    outer, grad_near, heads = step.run(
-        [(cols_far, OUTWARD), (grad_own, MIDDLE)],
+    outer, *grads, heads = step.run(
+        [(cols_far, OUTWARD)] + to_plane(grad_blocks),
         lambda *parts: tp_gather(jnp.concatenate(parts, axis=0), 1),
         (attended, *arrived),
     )
+    grad_rows_own = from_plane(grad_blocks, grads)
     columns = jnp.concatenate([out_weight, cols_partner, cols_near, cols_far + outer], axis=1)
     column_count = out_weight.shape[1]
     sources = jnp.stack([z, z ^ 1, jnp.where(z < 2, 2, 1), jnp.where(z < 2, 3, 0)])
@@ -258,8 +316,8 @@
 
     projected = jnp.dot(heads, columns, preferred_element_type=jnp.float32).astype(bf16)
     blocks = projected.reshape(plane, length, DEPTH * column_count)
-    grad_partner, *arrived = step.run(
-        [(grad_own, SWAP)] + [(blocks[r], r) for r in range(1, plane)]
+    grad_partner, grad_near, *arrived = step.run(
+        [(grad_own, SWAP), (grad_own, MIDDLE)] + [(blocks[r], r) for r in range(1, plane)]
     )
     proj = jnp.stack([blocks[0], *arrived]).reshape(plane, length, DEPTH, column_count)
     proj = proj.transpose(0, 2, 1, 3).reshape(n_ep, length, column_count)
@@ -269,11 +327,11 @@
         residual = (hidden_in.astype(jnp.float32) + proj.astype(jnp.float32)).astype(bf16)
         resid_f = residual.astype(jnp.float32)
         scaled = resid_f * norm_gain.astype(jnp.float32)
-        squares = tp_sum(jnp.sum(resid_f * resid_f, axis=1))
-        raw_logits = tp_sum(
-            jnp.dot(scaled, router.astype(jnp.float32), precision=lax.Precision.HIGHEST)
-        )
-        inv_rms = lax.rsqrt(squares[:, None] / D + norm_eps)
+        products = jnp.dot(scaled, router.astype(jnp.float32), precision=lax.Precision.HIGHEST)
+        squares = jnp.sum(resid_f * resid_f, axis=1, keepdims=True)
+        sums = tp_sum(jnp.concatenate([products, squares], axis=1))
+        raw_logits, squares = sums[:, :n_ep], sums[:, n_ep:]
+        inv_rms = lax.rsqrt(squares / D + norm_eps)
         normed = (scaled * inv_rms).astype(bf16)
         one_hot = routes[:, :, None] == expert_ids[None, None, :]
         sigmoids = jax.nn.sigmoid(raw_logits * inv_rms)
@@ -283,16 +341,16 @@
         table = jnp.sum(jnp.where(one_hot, weights[:, :, None], 0.0), axis=1)
         high = table.astype(bf16)
         low = (table - high.astype(jnp.float32)).astype(bf16)
-        normed = with_lanes(normed, jnp.concatenate([high, low], axis=1))
-        return residual, inv_rms, picked, totals, normed, pack(normed, hot_own)
+        marks = jnp.concatenate([high, low, routes.astype(bf16)], axis=1)
+        return residual, inv_rms, picked, totals, with_lanes(normed, marks)
 
     hot_partner, grad_blocks = slots_pack(grad_partner)
-    grad_far, outer, *arrived, made = step.run(
-        [(grad_partner, MIDDLE), (grad_near, OUTWARD)] + to_plane(grad_blocks),
+    outer, *arrived, made = step.run(
+        [(grad_near, OUTWARD)] + to_plane(grad_blocks),
         normalise,
         (proj,),
     )
-    residual, inv_rms, picked, totals, normed_own, blocks = made
+    residual, inv_rms, picked, totals, normed_own = made
     resid_f = residual.astype(jnp.float32)
     gain_f = norm_gain.astype(jnp.float32)
     router_f = router.astype(jnp.float32)
@@ -300,76 +358,76 @@
     grad_rows_partner = from_plane(grad_blocks, arrived)
     grad_near = grad_near + outer
 
-    normed_partner, normed_near, *arrived, ((hot_near, grad_blocks), back_own) = step.run(
-        [(normed_own, SWAP), (normed_own, MIDDLE)] + to_plane(blocks),
-        lambda piece, rows: (slots_pack(piece), backward_part(rows)),
-        (grad_near, grad_rows_own),
-    )
-    rows_own = from_plane(blocks, arrived)
-    normed_far, outer, *arrived, (pre_own, blocks) = step.run(
-        [(normed_partner, MIDDLE), (normed_near, OUTWARD)] + to_plane(grad_blocks),
-        lambda rows, piece, hot: (gate_up(rows), pack(piece, hot)),
-        (rows_own, normed_partner, hot_partner),
+    hot_near, grad_blocks = slots_pack(grad_near)
+    normed_partner, normed_near, *arrived, (back_own, back_partner, own_packed) = step.run(
+        [(normed_own, SWAP), (normed_own, MIDDLE)] + to_plane(grad_blocks),
+        lambda own, partner, piece, hot: (
+            backward_part(own),
+            backward_part(partner),
+            pack(piece, hot),
+        ),
+        (grad_rows_own, grad_rows_partner, normed_own, hot_own),
     )
     grad_rows_near = from_plane(grad_blocks, arrived)
+    blocks = pack(normed_partner, hot_partner)
+    normed_far, outer, *arrived, back_near = step.run(
+        [(normed_partner, MIDDLE), (normed_near, OUTWARD)] + to_plane(blocks),
+        backward_part,
+        (grad_rows_near,),
+    )
+    rows_partner = from_plane(blocks, arrived)
     normed_near = normed_near + outer
-    outer, *arrived, (back_partner, near_blocks) = step.run(
-        [(grad_far, OUTWARD)] + to_plane(blocks),
-        lambda rows, piece, hot: (backward_part(rows), pack(piece, hot)),
-        (grad_rows_partner, normed_near, hot_near),
-    )
-    rows_partner = from_plane(blocks, arrived)
-    grad_far = grad_far + outer
-    outer, *arrived, (pre_partner, (hot_far, grad_blocks)) = step.run(
-        [(normed_far, OUTWARD)] + to_plane(near_blocks),
-        lambda rows, piece: (gate_up(rows), slots_pack(piece)),
-        (rows_partner, grad_far),
-    )
-    rows_near = from_plane(near_blocks, arrived)
+    blocks = pack(normed_near, hot_near)
+    outer, grad_far, *arrived, pre_partner = step.run(
+        [(normed_far, OUTWARD), (grad_partner, MIDDLE)] + to_plane(blocks),
+        gate_up,
+        (rows_partner,),
+    )
+    rows_near = from_plane(blocks, arrived)
     normed_far = normed_far + outer
-    *arrived, (pre_near, back_near, far_blocks) = step.run(
-        to_plane(grad_blocks),
-        lambda rows, grads, piece, hot: (gate_up(rows), backward_part(grads), pack(piece, hot)),
-        (rows_near, grad_rows_near, normed_far, hot_far),
-    )
-    grad_rows_far = from_plane(grad_blocks, arrived)
-    *arrived, (back_far, own_blocks) = step.run(
-        to_plane(far_blocks),
-        lambda rows, pre, back: (backward_part(rows), expert_rows(*pre, back)),
-        (grad_rows_far, pre_own, back_own),
-    )
-    rows_far = from_plane(far_blocks, arrived)
-
-    *arrived, (near_blocks, blocks) = step.run(
-        to_plane(own_blocks),
-        lambda rows, back, pre, near_back: (
-            expert_rows(*pre, near_back),
-            expert_rows(*gate_up(rows), back),
-        ),
-        (rows_far, back_far, pre_near, back_near),
-    )
-    own_arrived = from_plane(own_blocks, arrived)
-    *arrived, (own_sum, partner_blocks) = step.run(
+    hot_far = slots_of(normed_far, 2 * n_ep)
+    blocks = pack(normed_far, hot_far)
+    outer, *arrived, pre_near = step.run(
+        [(grad_far, OUTWARD)] + to_plane(blocks), gate_up, (rows_near,)
+    )
+    rows_far = from_plane(blocks, arrived)
+    blocks = pack(grad_far + outer, hot_far)
+    *arrived, pre_far = step.run(to_plane(blocks), gate_up, (rows_far,))
+    grad_rows_far = from_plane(blocks, arrived)
+    *arrived, blocks = step.run(
+        to_plane(own_packed),
+        lambda rows, pre: expert_rows(*pre, backward_part(rows)),
+        (grad_rows_far, pre_far),
+    )
+    rows_own = from_plane(own_packed, arrived)
+
+    *arrived, (near_blocks, pre_own) = step.run(
         to_plane(blocks),
-        lambda got, table, pre, back: (
-            relay_sum(hot_own, table, got),
-            expert_rows(*pre, back),
-        ),
-        (own_arrived, normed_own[:, slice_width:], pre_partner, back_partner),
+        lambda pre, back, rows: (expert_rows(*pre, back), gate_up(rows)),
+        (pre_near, back_near, rows_own),
     )
     far_sum = relay_sum(hot_far, normed_far[:, slice_width:], from_plane(blocks, arrived))
-    inward, *arrived = step.run([(far_sum.astype(bf16), INWARD)] + to_plane(near_blocks))
+    inward, *arrived, partner_blocks = step.run(
+        [(far_sum.astype(bf16), INWARD)] + to_plane(near_blocks),
+        lambda pre, back: expert_rows(*pre, back),
+        (pre_partner, back_partner),
+    )
     far_sum = (far_sum + inward).astype(bf16)
     near_sum = relay_sum(hot_near, normed_near[:, slice_width:], from_plane(near_blocks, arrived))
-    across, inward, *arrived = step.run(
-        [(far_sum, MIDDLE), (near_sum.astype(bf16), INWARD)] + to_plane(partner_blocks)
+    across, inward, *arrived, own_blocks = step.run(
+        [(far_sum, MIDDLE), (near_sum.astype(bf16), INWARD)] + to_plane(partner_blocks),
+        lambda pre, back: expert_rows(*pre, back),
+        (pre_own, back_own),
     )
     near_sum = (near_sum + inward).astype(bf16)
     partner_sum = relay_sum(
         hot_partner, normed_partner[:, slice_width:], from_plane(partner_blocks, arrived)
     )
     partner_sum = (partner_sum + across).astype(bf16)
-    near_in, partner_in = step.run([(near_sum, MIDDLE), (partner_sum, SWAP)])
+    near_in, partner_in, *arrived = step.run(
+        [(near_sum, MIDDLE), (partner_sum, SWAP)] + to_plane(own_blocks)
+    )
+    own_sum = relay_sum(hot_own, normed_own[:, slice_width:], from_plane(own_blocks, arrived))
     dnormed = own_sum + near_in.astype(jnp.float32) + partner_in.astype(jnp.float32)
     ret_scores = dnormed[:, slice_width : slice_width + n_ep]
     dnormed = dnormed[:, :slice_width]

time: 592 us -> 581 us (0.981)
  matrix products: 128 us -> 32.2 us
  Pallas kernels: 0 us -> 68.6 us
  local copies, waits for them, and re-layouts: 39.6 us -> 69.2 us
  waiting for transfers between devices: 270 us -> 257 us
  other arithmetic: 47 us -> 34.6 us
    dot_general x20 -> x0, matrix products: 99.9 us -> none  [the longest x4 24.6 us: expert_rows(): jnp.einsum('rh,dh->rd', both[1], up_local, preferred_element_type=jnp.flo...]
    pallas_call x0 -> x12, Pallas kernels: none -> 68.6 us  [the longest x8 38.5 us: summed_products(): pl.pallas_call(summed_kernel, grid=(height // tile,), in_specs=[whole(x)...]
    ppermute x20, waiting for transfers between devices: 84.4 us -> 41.1 us  [depth_permute(): lax.ppermute(x, 'ep', [(a * plane + i, b * plane + i) for a, b in pairs f...]
    unnamed x163 -> x173, local copies, waits for them, and re-layouts: 10.1 us -> 42.6 us
    ppermute x48, waiting for transfers between devices: 180 us -> 204 us  [plane_permute(): return lax.ppermute(x, 'ep', [(i, i ^ step) for i in range(n_ep)])]
    ppermute x17 -> x16, waiting for transfers between devices: 5.14 us -> 12 us  [tp_swap(): return lax.ppermute(x, 'tp', [(0, 1), (1, 0)])]
  transfers between devices with their start and end apart: 85 -> 84, of which waited for: 37 -> 42; matrix products, arithmetic and copies ran while one was open for 23% -> 5% of each run, Pallas kernels for 0% -> 11%
where the time goes in v3:
time: 581 us; the launch traced here: 571 us
  waiting for transfers between devices  257 us (44%)
  starting transfers between devices  105 us (18%)
  local copies, waits for them, and re-layouts  69.2 us (12%)
  Pallas kernels  68.6 us (12%)
  other arithmetic  34.6 us (6%)
  matrix products  32.2 us (6%)
    ppermute x48, waiting for transfers between devices, plane_permute(): return lax.ppermute(x, 'ep', [(i, i ^ step) for i in range(n_ep)])  204 us
    ppermute x48, starting transfers between devices, plane_permute(): return lax.ppermute(x, 'ep', [(i, i ^ step) for i in range(n_ep)])  56.4 us
    ppermute x20, starting transfers between devices, depth_permute(): lax.ppermute(x, 'ep', [(a * plane + i, b * plane + i) for a, b in pairs f...  46.1 us
    unnamed x173, local copies, waits for them, and re-layouts  42.6 us
    ppermute x20, waiting for transfers between devices, depth_permute(): lax.ppermute(x, 'ep', [(a * plane + i, b * plane + i) for a, b in pairs f...  41.1 us
    pallas_call x8, Pallas kernels, summed_products(): pl.pallas_call(summed_kernel, grid=(height // tile,), in_specs=[whole(x)...  38.5 us
    pallas_call x4, Pallas kernels, products(): pl.pallas_call(products_kernel, grid=(width // tile,), in_specs=[whole(ro...  30.2 us
    ppermute x16, waiting for transfers between devices, tp_swap(): return lax.ppermute(x, 'tp', [(0, 1), (1, 0)])  12 us
  transfers between devices with their start and end apart: 84, of which 42 were waited for; matrix products, arithmetic and copies ran while one was open for 5% of the time, Pallas kernels for 11%

profile of v3, /device:TPU:0, one launch (start us, length us, event | category | flops | bytes accessed | tf_op | source)
XLA Modules:
  0.0 570.7 jit_solution(15768600234235239251)
XLA Ops:
  10.7 16.1 %collective-permute-done = bf16[2048,224]{0,1:T(8,128)(2,1)} collective-permute-done((bf16[2048,224]{0,1:T(8,128)(2,1)}, bf16[2048,224]{0,1:T(8,128)(2,1)}, u32[]{:S(2)}, u32[]{:S(2)}) %collective-permute-start) | collective-permute-done | bytes 917536 | tf_op jit(solution)/shard_map/ppermute | solution.py:39
  41.0 17.2 %collective-permute-done.3 = bf16[2048,224]{0,1:T(8,128)(2,1)S(1)} collective-permute-done((bf16[2048,224]{0,1:T(8,128)(2,1)}, bf16[2048,224]{0,1:T(8,128)(2,1)S(1)}, u32[]{:S(2)}, u32[]{:S(2)}) %collective-permute-start.3) | collective-permute-done | bytes 917536 | tf_op jit(solution)/shard_map/ppermute | solution.py:39
  67.9 10.7 %collective-permute-done.8 = bf16[80,3584]{1,0:T(8,128)(2,1)S(1)} collective-permute-done((bf16[80,3584]{1,0:T(8,128)(2,1)S(1)}, bf16[80,3584]{1,0:T(8,128)(2,1)S(1)}, u32[]{:S(2)}, u32[]{:S(2)}) %collective-permute-start.8) | collective-permute-done | bytes 573472 | tf_op jit(solution)/shard_map/ppermute | solution.py:45
  78.7 13.1 %collective-permute-done.9 = bf16[80,3584]{1,0:T(8,128)(2,1)S(1)} collective-permute-done((bf16[80,3584]{1,0:T(8,128)(2,1)S(1)}, bf16[80,3584]{1,0:T(8,128)(2,1)S(1)}, u32[]{:S(2)}, u32[]{:S(2)}) %collective-permute-start.9) | collective-permute-done | bytes 573472 | tf_op jit(solution)/shard_map/ppermute | solution.py:45
  137.3 10.0 %collective-permute-done.18 = bf16[80,3584]{1,0:T(8,128)(2,1)S(1)} collective-permute-done((bf16[80,3584]{1,0:T(8,128)(2,1)S(1)}, bf16[80,3584]{1,0:T(8,128)(2,1)S(1)}, u32[]{:S(2)}, u32[]{:S(2)}) %collective-permute-start.18) | collective-permute-done | bytes 573472 | tf_op jit(solution)/shard_map/ppermute | solution.py:45
  147.3 10.9 %collective-permute-done.19 = bf16[80,3584]{1,0:T(8,128)(2,1)S(1)} collective-permute-done((bf16[80,3584]{1,0:T(8,128)(2,1)S(1)}, bf16[80,3584]{1,0:T(8,128)(2,1)S(1)}, u32[]{:S(2)}, u32[]{:S(2)}) %collective-permute-start.19) | collective-permute-done | bytes 573472 | tf_op jit(solution)/shard_map/ppermute | solution.py:45
  184.3 10.3 %collective-permute-done.25 = bf16[80,3584]{1,0:T(8,128)(2,1)S(1)} collective-permute-done((bf16[80,3584]{1,0:T(8,128)(2,1)S(1)}, bf16[80,3584]{1,0:T(8,128)(2,1)S(1)}, u32[]{:S(2)}, u32[]{:S(2)}) %collective-permute-start.25) | collective-permute-done | bytes 573472 | tf_op jit(solution)/shard_map/ppermute | solution.py:45
  204.7 9.1 %collective-permute-done.29 = bf16[80,3584]{1,0:T(8,128)(2,1)S(1)} collective-permute-done((bf16[80,3584]{1,0:T(8,128)(2,1)S(1)}, bf16[80,3584]{1,0:T(8,128)(2,1)S(1)}, u32[]{:S(2)}, u32[]{:S(2)}) %collective-permute-start.29) | collective-permute-done | bytes 573472 | tf_op jit(solution)/shard_map/ppermute | solution.py:45
  213.8 8.4 %collective-permute-done.30 = bf16[80,3584]{1,0:T(8,128)(2,1)S(1)} collective-permute-done((bf16[80,3584]{1,0:T(8,128)(2,1)S(1)}, bf16[80,3584]{1,0:T(8,128)(2,1)S(1)}, u32[]{:S(2)}, u32[]{:S(2)}) %collective-permute-start.30) | collective-permute-done | bytes 573472 | tf_op jit(solution)/shard_map/ppermute | solution.py:45
  232.9 7.5 %shard_map.150 = (bf16[320,1024]{1,0:T(8,128)(2,1)S(1)}, bf16[320,1024]{1,0:T(8,128)(2,1)S(1)}) custom-call(bf16[320,3584]{1,0:T(8,128)(2,1)S(1)} %pad_maximum_fusion.12.rows_ref, bf16[3584,1024]{1,0:T(8,128)(2,1)S(1)} %bitcast.348, bf16[3584,1024]{1,0:T(8,128)(2,1)S(1)} %bitcast.364), custom_call_target="tpu_custom_call" | custom-call | flops 1048576 | bytes 65536 | tf_op jit(solution)/shard_map/pallas_call | solution.py:74
  245.3 8.4 %collective-permute-done.35 = bf16[80,3584]{1,0:T(8,128)(2,1)S(1)} collective-permute-done((bf16[80,3584]{1,0:T(8,128)(2,1)S(1)}, bf16[80,3584]{1,0:T(8,128)(2,1)S(1)}, u32[]{:S(2)}, u32[]{:S(2)}) %collective-permute-start.35) | collective-permute-done | bytes 573472 | tf_op jit(solution)/shard_map/ppermute | solution.py:45
  268.1 7.5 %shard_map.151 = (bf16[320,1024]{1,0:T(8,128)(2,1)S(1)}, bf16[320,1024]{1,0:T(8,128)(2,1)S(1)}) custom-call(bf16[320,3584]{1,0:T(8,128)(2,1)S(1)} %pad_maximum_fusion.13.rows_ref, bf16[3584,1024]{1,0:T(8,128)(2,1)S(1)} %bitcast.349, bf16[3584,1024]{1,0:T(8,128)(2,1)S(1)} %bitcast.365), custom_call_target="tpu_custom_call" | custom-call | flops 1048576 | bytes 65536 | tf_op jit(solution)/shard_map/pallas_call | solution.py:74
  292.3 7.5 %shard_map.152 = (bf16[320,1024]{1,0:T(8,128)(2,1)S(1)}, bf16[320,1024]{1,0:T(8,128)(2,1)S(1)}) custom-call(bf16[320,3584]{1,0:T(8,128)(2,1)S(1)} %pad_maximum_fusion.14.rows_ref, bf16[3584,1024]{1,0:T(8,128)(2,1)S(1)} %bitcast.352, bf16[3584,1024]{1,0:T(8,128)(2,1)S(1)} %bitcast.366), custom_call_target="tpu_custom_call" | custom-call | flops 1048576 | bytes 65536 | tf_op jit(solution)/shard_map/pallas_call | solution.py:74
  303.2 6.6 %collective-permute-done.42 = bf16[80,3584]{1,0:T(8,128)(2,1)S(1)} collective-permute-done((bf16[80,3584]{1,0:T(8,128)(2,1)S(1)}, bf16[80,3584]{1,0:T(8,128)(2,1)S(1)}, u32[]{:S(2)}, u32[]{:S(2)}) %collective-permute-start.42) | collective-permute-done | bytes 573472 | tf_op jit(solution)/shard_map/ppermute | solution.py:45
  339.6 12.9 %collective-permute-done.45 = bf16[80,3584]{1,0:T(8,128)(2,1)S(1)} collective-permute-done((bf16[80,3584]{1,0:T(8,128)(2,1)S(1)}, bf16[80,3584]{1,0:T(8,128)(2,1)S(1)}, u32[]{:S(2)}, u32[]{:S(2)}) %collective-permute-start.45) | collective-permute-done | bytes 573472 | tf_op jit(solution)/shard_map/ppermute | solution.py:45
  378.2 7.6 %shard_map.156 = (bf16[320,1024]{1,0:T(8,128)(2,1)S(1)}, bf16[320,1024]{1,0:T(8,128)(2,1)S(1)}) custom-call(bf16[320,3584]{1,0:T(8,128)(2,1)S(1)} %pad_maximum_fusion.16.rows_ref, bf16[3584,1024]{1,0:T(8,128)(2,1)S(1)} %bitcast.356, bf16[3584,1024]{1,0:T(8,128)(2,1)S(1)} %bitcast.368), custom_call_target="tpu_custom_call" | custom-call | flops 1048576 | bytes 65536 | tf_op jit(solution)/shard_map/pallas_call | solution.py:74
  412.2 6.4 %collective-permute-start.56 = (bf16[128,3712]{0,1:T(8,128)(2,1)S(1)}, bf16[128,3712]{0,1:T(8,128)(2,1)S(1)}, u32[]{:S(2)}, u32[]{:S(2)}) collective-permute-start(bf16[128,3712]{0,1:T(8,128)(2,1)S(1)} %fusion.33), channel_id=1, source_target_pairs={{0,4},{1,5},{2,6},{3,7},{12,8},{13,9},{14,10},{15,11},{16,20},{17,... | collective-permute-start | bytes 2850824 | tf_op jit(solution)/shard_map/ppermute | solution.py:39
  419.1 6.6 %shard_map.157 = bf16[320,3584]{1,0:T(8,128)(2,1)S(1)} custom-call(bf16[320,1024]{1,0:T(8,128)(2,1)S(1)} %get-tuple-element.506.refs_0_, bf16[320,1024]{1,0:T(8,128)(2,1)S(1)} %get-tuple-element.505.refs_1_, bf16[3584,1024]{1,0:T(8,128)(2,1)S(1)} %bitcast.360, bf16[3584,1024]{1,0:T(8,128)(2,1)S(1)} %bitcast.370), custom_call_target="tpu_custom_call" | custom-call | flops 1048576 | bytes 65536 | tf_op jit(solution)/shard_map/pallas_call | solution.py:103
  425.9 11.1 %collective-permute-done.58 = bf16[80,3712]{1,0:T(8,128)(2,1)S(1)} collective-permute-done((bf16[80,3712]{1,0:T(8,128)(2,1)S(1)}, bf16[80,3712]{1,0:T(8,128)(2,1)S(1)}, u32[]{:S(2)}, u32[]{:S(2)}) %collective-permute-start.58) | collective-permute-done | bytes 593952 | tf_op jit(solution)/shard_map/ppermute | solution.py:45
  448.7 7.8 %collective-permute-start.64 = (bf16[128,3712]{0,1:T(8,128)(2,1)S(1)}, bf16[128,3712]{0,1:T(8,128)(2,1)S(1)}, u32[]{:S(2)}, u32[]{:S(2)}) collective-permute-start(bf16[128,3712]{0,1:T(8,128)(2,1)S(1)} %fusion.32), channel_id=1, source_target_pairs={{0,4},{1,5},{2,6},{3,7},{12,8},{13,9},{14,10},{15,11},{16,20},{17,... | collective-permute-start | bytes 2850824 | tf_op jit(solution)/shard_map/ppermute | solution.py:39
  458.5 6.3 %shard_map.158 = bf16[320,3584]{1,0:T(8,128)(2,1)S(1)} custom-call(bf16[320,1024]{1,0:T(8,128)(2,1)S(1)} %get-tuple-element.502.refs_0_, bf16[320,1024]{1,0:T(8,128)(2,1)S(1)} %get-tuple-element.501.refs_1_, bf16[3584,1024]{1,0:T(8,128)(2,1)S(1)} %bitcast.361, bf16[3584,1024]{1,0:T(8,128)(2,1)S(1)} %bitcast.371), custom_call_target="tpu_custom_call" | custom-call | flops 1048576 | bytes 65536 | tf_op jit(solution)/shard_map/pallas_call | solution.py:103
  465.0 9.4 %collective-permute-done.66 = bf16[80,3712]{1,0:T(8,128)(2,1)S(1)} collective-permute-done((bf16[80,3712]{1,0:T(8,128)(2,1)S(1)}, bf16[80,3712]{1,0:T(8,128)(2,1)S(1)}, u32[]{:S(2)}, u32[]{:S(2)}) %collective-permute-start.66) | collective-permute-done | bytes 593952 | tf_op jit(solution)/shard_map/ppermute | solution.py:45
  491.2 13.0 %collective-permute-done.73 = bf16[80,3712]{1,0:T(8,128)(2,1)S(1)} collective-permute-done((bf16[80,3712]{1,0:T(8,128)(2,1)}, bf16[80,3712]{1,0:T(8,128)(2,1)S(1)}, u32[]{:S(2)}, u32[]{:S(2)}) %collective-permute-start.73) | collective-permute-done | bytes 593952 | tf_op jit(solution)/shard_map/ppermute | solution.py:45
  504.2 10.2 %collective-permute-done.74 = bf16[80,3712]{1,0:T(8,128)(2,1)S(1)} collective-permute-done((bf16[80,3712]{1,0:T(8,128)(2,1)}, bf16[80,3712]{1,0:T(8,128)(2,1)S(1)}, u32[]{:S(2)}, u32[]{:S(2)}) %collective-permute-start.74) | collective-permute-done | bytes 593952 | tf_op jit(solution)/shard_map/ppermute | solution.py:45
  (550 shorter events, 332.6 us)
Async XLA Ops:
  31.1 27.2 %collective-permute-start.3 = (bf16[2048,224]{0,1:T(8,128)(2,1)}, bf16[2048,224]{0,1:T(8,128)(2,1)S(1)}, u32[]{:S(2)}, u32[]{:S(2)}) collective-permute-start(bf16[2048,224]{0,1:T(8,128)(2,1)} %collective-permute-done.1), channel_id=1, source_target_pairs={{4,0},{5,1},{6,2},{7,3},{8,12},{9,13},{10,14},{11,15},{20,16},{21,... | collective-permute-start | bytes 2752520 | tf_op jit(solution)/shard_map/ppermute | solution.py:39
  59.5 32.2 %collective-permute-start.7 = (bf16[2048,224]{0,1:T(8,128)(2,1)S(1)}, bf16[2048,224]{0,1:T(8,128)(2,1)}, u32[]{:S(2)}, u32[]{:S(2)}) collective-permute-start(bf16[2048,224]{0,1:T(8,128)(2,1)S(1)} %collective-permute-done.2), channel_id=1, source_target_pairs={{4,0},{5,1},{6,2},{7,3},{8,12},{9,13},{10,14},{11,15},{20,16},{21,... | collective-permute-start | bytes 2752520 | tf_op jit(solution)/shard_map/ppermute | solution.py:39
  64.4 27.4 %collective-permute-start.9 = (bf16[80,3584]{1,0:T(8,128)(2,1)S(1)}, bf16[80,3584]{1,0:T(8,128)(2,1)S(1)}, u32[]{:S(2)}, u32[]{:S(2)}) collective-permute-start(bf16[80,3584]{1,0:T(8,128)(2,1)S(1)} %copy-done.58), channel_id=1, source_target_pairs={{0,2},{1,3},{2,0},{3,1},{4,6},{5,7},{6,4},{7,5},{8,10},{9,11},{10,... | collective-permute-start | bytes 1720328 | tf_op jit(solution)/shard_map/ppermute | solution.py:45
  133.5 26.5 %collective-permute-start.20 = (bf16[80,3584]{1,0:T(8,128)(2,1)S(1)}, bf16[80,3584]{1,0:T(8,128)(2,1)S(1)}, u32[]{:S(2)}, u32[]{:S(2)}) collective-permute-start(bf16[80,3584]{1,0:T(8,128)(2,1)S(1)} %copy-done.55), channel_id=1, source_target_pairs={{0,3},{1,2},{2,1},{3,0},{4,7},{5,6},{6,5},{7,4},{8,11},{9,10},{10,... | collective-permute-start | bytes 1720328 | tf_op jit(solution)/shard_map/ppermute | solution.py:45
  164.6 30.1 %collective-permute-start.22 = (bf16[128,3712]{0,1:T(8,128)(2,1)S(1)}, bf16[128,3712]{0,1:T(8,128)(2,1)S(1)}, u32[]{:S(2)}, u32[]{:S(2)}) collective-permute-start(bf16[128,3712]{0,1:T(8,128)(2,1)S(1)} %pad_maximum_fusion.25), channel_id=1, source_target_pairs={{0,4},{1,5},{2,6},{3,7},{4,0},{5,1},{6,2},{7,3},{8,12},{9,13},{10,... | collective-permute-start | bytes 2850824 | tf_op jit(solution)/shard_map/ppermute | solution.py:39
  167.6 27.0 %collective-permute-start.23 = (bf16[128,3712]{0,1:T(8,128)(2,1)S(1)}, bf16[128,3712]{0,1:T(8,128)(2,1)S(1)}, u32[]{:S(2)}, u32[]{:S(2)}) collective-permute-start(bf16[128,3712]{0,1:T(8,128)(2,1)S(1)} %pad_maximum_fusion.25), channel_id=1, source_target_pairs={{4,8},{5,9},{6,10},{7,11},{8,4},{9,5},{10,6},{11,7},{20,24},{21,25... | collective-permute-start | bytes 2850824 | tf_op jit(solution)/shard_map/ppermute | solution.py:39
  195.8 28.2 %collective-permute-start.27 = (bf16[128,3712]{0,1:T(8,128)(2,1)S(1)}, bf16[128,3712]{0,1:T(8,128)(2,1)S(1)}, u32[]{:S(2)}, u32[]{:S(2)}) collective-permute-start(bf16[128,3712]{0,1:T(8,128)(2,1)S(1)} %collective-permute-done.22), channel_id=1, source_target_pairs={{4,8},{5,9},{6,10},{7,11},{8,4},{9,5},{10,6},{11,7},{20,24},{21,25... | collective-permute-start | bytes 2850824 | tf_op jit(solution)/shard_map/ppermute | solution.py:39
  196.5 27.5 %collective-permute-start.28 = (bf16[128,3712]{0,1:T(8,128)(2,1)S(1)}, bf16[128,3712]{0,1:T(8,128)(2,1)S(1)}, u32[]{:S(2)}, u32[]{:S(2)}) collective-permute-start(bf16[128,3712]{0,1:T(8,128)(2,1)S(1)} %collective-permute-done.23), channel_id=1, source_target_pairs={{4,0},{5,1},{6,2},{7,3},{8,12},{9,13},{10,14},{11,15},{20,16},{21,... | collective-permute-start | bytes 2850824 | tf_op jit(solution)/shard_map/ppermute | solution.py:39
  226.3 27.3 %collective-permute-start.32 = (bf16[128,3712]{0,1:T(8,128)(2,1)S(1)}, bf16[128,3712]{0,1:T(8,128)(2,1)S(1)}, u32[]{:S(2)}, u32[]{:S(2)}) collective-permute-start(bf16[128,3712]{0,1:T(8,128)(2,1)S(1)} %collective-permute-done.27), channel_id=1, source_target_pairs={{4,0},{5,1},{6,2},{7,3},{8,12},{9,13},{10,14},{11,15},{20,16},{21,... | collective-permute-start | bytes 2850824 | tf_op jit(solution)/shard_map/ppermute | solution.py:39
  256.7 26.3 %collective-permute-start.37 = (bf16[128,3712]{0,1:T(8,128)(2,1)}, bf16[128,3712]{0,1:T(8,128)(2,1)}, u32[]{:S(2)}, u32[]{:S(2)}) collective-permute-start(bf16[128,3712]{0,1:T(8,128)(2,1)} %collective-permute-done.33), channel_id=1, source_target_pairs={{4,0},{5,1},{6,2},{7,3},{8,12},{9,13},{10,14},{11,15},{20,16},{21,... | collective-permute-start | bytes 2850824 | tf_op jit(solution)/shard_map/ppermute | solution.py:39
  325.5 27.1 %collective-permute-start.45 = (bf16[80,3584]{1,0:T(8,128)(2,1)S(1)}, bf16[80,3584]{1,0:T(8,128)(2,1)S(1)}, u32[]{:S(2)}, u32[]{:S(2)}) collective-permute-start(bf16[80,3584]{1,0:T(8,128)(2,1)S(1)} %copy-done.53), channel_id=1, source_target_pairs={{0,2},{1,3},{2,0},{3,1},{4,6},{5,7},{6,4},{7,5},{8,10},{9,11},{10,... | collective-permute-start | bytes 1720328 | tf_op jit(solution)/shard_map/ppermute | solution.py:45
  325.8 26.8 %collective-permute-start.46 = (bf16[80,3584]{1,0:T(8,128)(2,1)S(1)}, bf16[80,3584]{1,0:T(8,128)(2,1)S(1)}, u32[]{:S(2)}, u32[]{:S(2)}) collective-permute-start(bf16[80,3584]{1,0:T(8,128)(2,1)S(1)} %copy-done.52), channel_id=1, source_target_pairs={{0,3},{1,2},{2,1},{3,0},{4,7},{5,6},{6,5},{7,4},{8,11},{9,10},{10,... | collective-permute-start | bytes 1720328 | tf_op jit(solution)/shard_map/ppermute | solution.py:45
  368.5 30.4 %collective-permute-start.50 = (bf16[80,3712]{1,0:T(8,128)(2,1)S(1)}, bf16[80,3712]{1,0:T(8,128)(2,1)S(1)}, u32[]{:S(2)}, u32[]{:S(2)}) collective-permute-start(bf16[80,3712]{1,0:T(8,128)(2,1)S(1)} %copy-done.45), channel_id=1, source_target_pairs={{0,1},{1,0},{2,3},{3,2},{4,5},{5,4},{6,7},{7,6},{8,9},{9,8},{10,11... | collective-permute-start | bytes 1781768 | tf_op jit(solution)/shard_map/ppermute | solution.py:45
  369.0 30.0 %collective-permute-start.51 = (bf16[80,3712]{1,0:T(8,128)(2,1)S(1)}, bf16[80,3712]{1,0:T(8,128)(2,1)S(1)}, u32[]{:S(2)}, u32[]{:S(2)}) collective-permute-start(bf16[80,3712]{1,0:T(8,128)(2,1)S(1)} %copy-done.44), channel_id=1, source_target_pairs={{0,2},{1,3},{2,0},{3,1},{4,6},{5,7},{6,4},{7,5},{8,10},{9,11},{10,... | collective-permute-start | bytes 1781768 | tf_op jit(solution)/shard_map/ppermute | solution.py:45
  370.7 28.2 %collective-permute-start.52 = (bf16[80,3712]{1,0:T(8,128)(2,1)S(1)}, bf16[80,3712]{1,0:T(8,128)(2,1)S(1)}, u32[]{:S(2)}, u32[]{:S(2)}) collective-permute-start(bf16[80,3712]{1,0:T(8,128)(2,1)S(1)} %copy-done.43), channel_id=1, source_target_pairs={{0,3},{1,2},{2,1},{3,0},{4,7},{5,6},{6,5},{7,4},{8,11},{9,10},{10,... | collective-permute-start | bytes 1781768 | tf_op jit(solution)/shard_map/ppermute | solution.py:45
  409.1 27.9 %collective-permute-start.58 = (bf16[80,3712]{1,0:T(8,128)(2,1)S(1)}, bf16[80,3712]{1,0:T(8,128)(2,1)S(1)}, u32[]{:S(2)}, u32[]{:S(2)}) collective-permute-start(bf16[80,3712]{1,0:T(8,128)(2,1)S(1)} %get-tuple-element.361), channel_id=1, source_target_pairs={{0,2},{1,3},{2,0},{3,1},{4,6},{5,7},{6,4},{7,5},{8,10},{9,11},{10,... | collective-permute-start | bytes 1781768 | tf_op jit(solution)/shard_map/ppermute | solution.py:45
  410.9 26.2 %collective-permute-start.59 = (bf16[80,3712]{1,0:T(8,128)(2,1)S(1)}, bf16[80,3712]{1,0:T(8,128)(2,1)S(1)}, u32[]{:S(2)}, u32[]{:S(2)}) collective-permute-start(bf16[80,3712]{1,0:T(8,128)(2,1)S(1)} %get-tuple-element.362), channel_id=1, source_target_pairs={{0,3},{1,2},{2,1},{3,0},{4,7},{5,6},{6,5},{7,4},{8,11},{9,10},{10,... | collective-permute-start | bytes 1781768 | tf_op jit(solution)/shard_map/ppermute | solution.py:45
  412.2 26.1 %collective-permute-start.56 = (bf16[128,3712]{0,1:T(8,128)(2,1)S(1)}, bf16[128,3712]{0,1:T(8,128)(2,1)S(1)}, u32[]{:S(2)}, u32[]{:S(2)}) collective-permute-start(bf16[128,3712]{0,1:T(8,128)(2,1)S(1)} %fusion.33), channel_id=1, source_target_pairs={{0,4},{1,5},{2,6},{3,7},{12,8},{13,9},{14,10},{15,11},{16,20},{17,... | collective-permute-start | bytes 2850824 | tf_op jit(solution)/shard_map/ppermute | solution.py:39
  446.4 27.9 %collective-permute-start.66 = (bf16[80,3712]{1,0:T(8,128)(2,1)S(1)}, bf16[80,3712]{1,0:T(8,128)(2,1)S(1)}, u32[]{:S(2)}, u32[]{:S(2)}) collective-permute-start(bf16[80,3712]{1,0:T(8,128)(2,1)S(1)} %get-tuple-element.374), channel_id=1, source_target_pairs={{0,2},{1,3},{2,0},{3,1},{4,6},{5,7},{6,4},{7,5},{8,10},{9,11},{10,... | collective-permute-start | bytes 1781768 | tf_op jit(solution)/shard_map/ppermute | solution.py:45
  448.0 26.4 %collective-permute-start.63 = (bf16[128,3712]{0,1:T(8,128)(2,1)S(1)}, bf16[128,3712]{0,1:T(8,128)(2,1)S(1)}, u32[]{:S(2)}, u32[]{:S(2)}) collective-permute-start(bf16[128,3712]{0,1:T(8,128)(2,1)S(1)} %add_convert_fusion.1), channel_id=1, source_target_pairs={{4,8},{5,9},{6,10},{7,11},{8,4},{9,5},{10,6},{11,7},{20,24},{21,25... | collective-permute-start | bytes 2850824 | tf_op jit(solution)/shard_map/ppermute | solution.py:39
  448.7 27.5 %collective-permute-start.64 = (bf16[128,3712]{0,1:T(8,128)(2,1)S(1)}, bf16[128,3712]{0,1:T(8,128)(2,1)S(1)}, u32[]{:S(2)}, u32[]{:S(2)}) collective-permute-start(bf16[128,3712]{0,1:T(8,128)(2,1)S(1)} %fusion.32), channel_id=1, source_target_pairs={{0,4},{1,5},{2,6},{3,7},{12,8},{13,9},{14,10},{15,11},{16,20},{17,... | collective-permute-start | bytes 2850824 | tf_op jit(solution)/shard_map/ppermute | solution.py:39
  481.2 33.1 %collective-permute-start.71 = (bf16[128,3712]{0,1:T(8,128)(2,1)S(1)}, bf16[128,3712]{0,1:T(8,128)(2,1)S(1)}, u32[]{:S(2)}, u32[]{:S(2)}) collective-permute-start(bf16[128,3712]{0,1:T(8,128)(2,1)S(1)} %add_convert_fusion), channel_id=1, source_target_pairs={{4,8},{5,9},{6,10},{7,11},{8,4},{9,5},{10,6},{11,7},{20,24},{21,25... | collective-permute-start | bytes 2850824 | tf_op jit(solution)/shard_map/ppermute | solution.py:39
  482.2 32.2 %collective-permute-start.72 = (bf16[128,3712]{0,1:T(8,128)(2,1)}, bf16[128,3712]{0,1:T(8,128)(2,1)}, u32[]{:S(2)}, u32[]{:S(2)}) collective-permute-start(bf16[128,3712]{0,1:T(8,128)(2,1)} %fusion.20), channel_id=1, source_target_pairs={{0,4},{1,5},{2,6},{3,7},{4,0},{5,1},{6,2},{7,3},{8,12},{9,13},{10,... | collective-permute-start | bytes 2850824 | tf_op jit(solution)/shard_map/ppermute | solution.py:39
  488.2 26.1 %collective-permute-start.74 = (bf16[80,3712]{1,0:T(8,128)(2,1)}, bf16[80,3712]{1,0:T(8,128)(2,1)S(1)}, u32[]{:S(2)}, u32[]{:S(2)}) collective-permute-start(bf16[80,3712]{1,0:T(8,128)(2,1)} %get-tuple-element.388), channel_id=1, source_target_pairs={{0,2},{1,3},{2,0},{3,1},{4,6},{5,7},{6,4},{7,5},{8,10},{9,11},{10,... | collective-permute-start | bytes 1781768 | tf_op jit(solution)/shard_map/ppermute | solution.py:45
  (142 other events, 1557.4 us)

commit v4 on v3

--- a/solution.py
+++ b/solution.py
@@ -52,7 +52,7 @@
 
 
 HINT = pl.CostEstimate(flops=1 << 20, bytes_accessed=1 << 16, transcendentals=0)
-PARAMS = pltpu.CompilerParams(vmem_limit_bytes=30 << 20)
+PARAMS = pltpu.CompilerParams(vmem_limit_bytes=16 << 20)
 
 
 def whole(array):

time: 581 us -> 576 us (level)
    unnamed x173 -> x183, local copies, waits for them, and re-layouts: 42.6 us -> 39.1 us
  transfers between devices with their start and end apart: 84 -> 84, of which waited for: 42 -> 40; matrix products, arithmetic and copies ran while one was open for 5% -> 5% of each run, Pallas kernels for 11% -> 12%
where the time goes in v4:
time: 576 us; the launch traced here: 566 us
  waiting for transfers between devices  256 us (44%)
  starting transfers between devices  106 us (18%)
  Pallas kernels  68.7 us (12%)
  local copies, waits for them, and re-layouts  65.6 us (11%)
  other arithmetic  34.6 us (6%)
  matrix products  32.3 us (6%)
    ppermute x48, waiting for transfers between devices, plane_permute(): return lax.ppermute(x, 'ep', [(i, i ^ step) for i in range(n_ep)])  203 us
    ppermute x48, starting transfers between devices, plane_permute(): return lax.ppermute(x, 'ep', [(i, i ^ step) for i in range(n_ep)])  56.5 us
    ppermute x20, starting transfers between devices, depth_permute(): lax.ppermute(x, 'ep', [(a * plane + i, b * plane + i) for a, b in pairs f...  46.2 us
    ppermute x20, waiting for transfers between devices, depth_permute(): lax.ppermute(x, 'ep', [(a * plane + i, b * plane + i) for a, b in pairs f...  41.1 us
    unnamed x183, local copies, waits for them, and re-layouts  39.1 us
    pallas_call x8, Pallas kernels, summed_products(): pl.pallas_call(summed_kernel, grid=(height // tile,), in_specs=[whole(x)...  38.5 us
    pallas_call x4, Pallas kernels, products(): pl.pallas_call(products_kernel, grid=(width // tile,), in_specs=[whole(ro...  30.2 us
    ppermute x16, waiting for transfers between devices, tp_swap(): return lax.ppermute(x, 'tp', [(0, 1), (1, 0)])  12 us
  transfers between devices with their start and end apart: 84, of which 40 were waited for; matrix products, arithmetic and copies ran while one was open for 5% of the time, Pallas kernels for 12%

profile of v4, /device:TPU:0, one launch (start us, length us, event | category | flops | bytes accessed | tf_op | source)
XLA Modules:
  0.0 566.2 jit_solution(7235208317011787537)
XLA Ops:
  10.8 16.1 %collective-permute-done = bf16[2048,224]{0,1:T(8,128)(2,1)} collective-permute-done((bf16[2048,224]{0,1:T(8,128)(2,1)}, bf16[2048,224]{0,1:T(8,128)(2,1)}, u32[]{:S(2)}, u32[]{:S(2)}) %collective-permute-start) | collective-permute-done | bytes 917536 | tf_op jit(solution)/shard_map/ppermute | solution.py:39
  41.0 17.2 %collective-permute-done.3 = bf16[2048,224]{0,1:T(8,128)(2,1)S(1)} collective-permute-done((bf16[2048,224]{0,1:T(8,128)(2,1)}, bf16[2048,224]{0,1:T(8,128)(2,1)S(1)}, u32[]{:S(2)}, u32[]{:S(2)}) %collective-permute-start.3) | collective-permute-done | bytes 917536 | tf_op jit(solution)/shard_map/ppermute | solution.py:39
  67.9 10.7 %collective-permute-done.8 = bf16[80,3584]{1,0:T(8,128)(2,1)S(1)} collective-permute-done((bf16[80,3584]{1,0:T(8,128)(2,1)S(1)}, bf16[80,3584]{1,0:T(8,128)(2,1)S(1)}, u32[]{:S(2)}, u32[]{:S(2)}) %collective-permute-start.8) | collective-permute-done | bytes 573472 | tf_op jit(solution)/shard_map/ppermute | solution.py:45
  78.7 13.1 %collective-permute-done.9 = bf16[80,3584]{1,0:T(8,128)(2,1)S(1)} collective-permute-done((bf16[80,3584]{1,0:T(8,128)(2,1)S(1)}, bf16[80,3584]{1,0:T(8,128)(2,1)S(1)}, u32[]{:S(2)}, u32[]{:S(2)}) %collective-permute-start.9) | collective-permute-done | bytes 573472 | tf_op jit(solution)/shard_map/ppermute | solution.py:45
  137.2 10.0 %collective-permute-done.18 = bf16[80,3584]{1,0:T(8,128)(2,1)S(1)} collective-permute-done((bf16[80,3584]{1,0:T(8,128)(2,1)S(1)}, bf16[80,3584]{1,0:T(8,128)(2,1)S(1)}, u32[]{:S(2)}, u32[]{:S(2)}) %collective-permute-start.18) | collective-permute-done | bytes 573472 | tf_op jit(solution)/shard_map/ppermute | solution.py:45
  147.2 12.7 %collective-permute-done.19 = bf16[80,3584]{1,0:T(8,128)(2,1)S(1)} collective-permute-done((bf16[80,3584]{1,0:T(8,128)(2,1)S(1)}, bf16[80,3584]{1,0:T(8,128)(2,1)S(1)}, u32[]{:S(2)}, u32[]{:S(2)}) %collective-permute-start.19) | collective-permute-done | bytes 573472 | tf_op jit(solution)/shard_map/ppermute | solution.py:45
  184.2 10.3 %collective-permute-done.25 = bf16[80,3584]{1,0:T(8,128)(2,1)S(1)} collective-permute-done((bf16[80,3584]{1,0:T(8,128)(2,1)S(1)}, bf16[80,3584]{1,0:T(8,128)(2,1)S(1)}, u32[]{:S(2)}, u32[]{:S(2)}) %collective-permute-start.25) | collective-permute-done | bytes 573472 | tf_op jit(solution)/shard_map/ppermute | solution.py:45
  205.4 8.3 %collective-permute-done.29 = bf16[80,3584]{1,0:T(8,128)(2,1)S(1)} collective-permute-done((bf16[80,3584]{1,0:T(8,128)(2,1)S(1)}, bf16[80,3584]{1,0:T(8,128)(2,1)S(1)}, u32[]{:S(2)}, u32[]{:S(2)}) %collective-permute-start.29) | collective-permute-done | bytes 573472 | tf_op jit(solution)/shard_map/ppermute | solution.py:45
  213.7 8.3 %collective-permute-done.30 = bf16[80,3584]{1,0:T(8,128)(2,1)S(1)} collective-permute-done((bf16[80,3584]{1,0:T(8,128)(2,1)S(1)}, bf16[80,3584]{1,0:T(8,128)(2,1)S(1)}, u32[]{:S(2)}, u32[]{:S(2)}) %collective-permute-start.30) | collective-permute-done | bytes 573472 | tf_op jit(solution)/shard_map/ppermute | solution.py:45
  232.7 7.5 %shard_map.150 = (bf16[320,1024]{1,0:T(8,128)(2,1)S(1)}, bf16[320,1024]{1,0:T(8,128)(2,1)S(1)}) custom-call(bf16[320,3584]{1,0:T(8,128)(2,1)S(1)} %pad_maximum_fusion.12.rows_ref, bf16[3584,1024]{1,0:T(8,128)(2,1)S(1)} %bitcast.348, bf16[3584,1024]{1,0:T(8,128)(2,1)S(1)} %bitcast.364), custom_call_target="tpu_custom_call" | custom-call | flops 1048576 | bytes 65536 | tf_op jit(solution)/shard_map/pallas_call | solution.py:74
  245.1 8.3 %collective-permute-done.35 = bf16[80,3584]{1,0:T(8,128)(2,1)S(1)} collective-permute-done((bf16[80,3584]{1,0:T(8,128)(2,1)S(1)}, bf16[80,3584]{1,0:T(8,128)(2,1)S(1)}, u32[]{:S(2)}, u32[]{:S(2)}) %collective-permute-start.35) | collective-permute-done | bytes 573472 | tf_op jit(solution)/shard_map/ppermute | solution.py:45
  267.9 7.5 %shard_map.151 = (bf16[320,1024]{1,0:T(8,128)(2,1)S(1)}, bf16[320,1024]{1,0:T(8,128)(2,1)S(1)}) custom-call(bf16[320,3584]{1,0:T(8,128)(2,1)S(1)} %pad_maximum_fusion.13.rows_ref, bf16[3584,1024]{1,0:T(8,128)(2,1)S(1)} %bitcast.349, bf16[3584,1024]{1,0:T(8,128)(2,1)S(1)} %bitcast.365), custom_call_target="tpu_custom_call" | custom-call | flops 1048576 | bytes 65536 | tf_op jit(solution)/shard_map/pallas_call | solution.py:74
  292.1 7.6 %shard_map.152 = (bf16[320,1024]{1,0:T(8,128)(2,1)S(1)}, bf16[320,1024]{1,0:T(8,128)(2,1)S(1)}) custom-call(bf16[320,3584]{1,0:T(8,128)(2,1)S(1)} %pad_maximum_fusion.14.rows_ref, bf16[3584,1024]{1,0:T(8,128)(2,1)S(1)} %bitcast.352, bf16[3584,1024]{1,0:T(8,128)(2,1)S(1)} %bitcast.368), custom_call_target="tpu_custom_call" | custom-call | flops 1048576 | bytes 65536 | tf_op jit(solution)/shard_map/pallas_call | solution.py:74
  303.0 6.5 %collective-permute-done.42 = bf16[80,3584]{1,0:T(8,128)(2,1)S(1)} collective-permute-done((bf16[80,3584]{1,0:T(8,128)(2,1)S(1)}, bf16[80,3584]{1,0:T(8,128)(2,1)S(1)}, u32[]{:S(2)}, u32[]{:S(2)}) %collective-permute-start.42) | collective-permute-done | bytes 573472 | tf_op jit(solution)/shard_map/ppermute | solution.py:45
  336.3 12.9 %collective-permute-done.45 = bf16[80,3584]{1,0:T(8,128)(2,1)S(1)} collective-permute-done((bf16[80,3584]{1,0:T(8,128)(2,1)S(1)}, bf16[80,3584]{1,0:T(8,128)(2,1)S(1)}, u32[]{:S(2)}, u32[]{:S(2)}) %collective-permute-start.45) | collective-permute-done | bytes 573472 | tf_op jit(solution)/shard_map/ppermute | solution.py:45
  374.9 7.6 %shard_map.156 = (bf16[320,1024]{1,0:T(8,128)(2,1)S(1)}, bf16[320,1024]{1,0:T(8,128)(2,1)S(1)}) custom-call(bf16[320,3584]{1,0:T(8,128)(2,1)S(1)} %pad_maximum_fusion.16.rows_ref, bf16[3584,1024]{1,0:T(8,128)(2,1)S(1)} %bitcast.356, bf16[3584,1024]{1,0:T(8,128)(2,1)S(1)} %bitcast.370), custom_call_target="tpu_custom_call" | custom-call | flops 1048576 | bytes 65536 | tf_op jit(solution)/shard_map/pallas_call | solution.py:74
  407.6 6.6 %collective-permute-start.56 = (bf16[128,3712]{0,1:T(8,128)(2,1)S(1)}, bf16[128,3712]{0,1:T(8,128)(2,1)S(1)}, u32[]{:S(2)}, u32[]{:S(2)}) collective-permute-start(bf16[128,3712]{0,1:T(8,128)(2,1)S(1)} %fusion.33), channel_id=1, source_target_pairs={{0,4},{1,5},{2,6},{3,7},{12,8},{13,9},{14,10},{15,11},{16,20},{17,... | collective-permute-start | bytes 2850824 | tf_op jit(solution)/shard_map/ppermute | solution.py:39
  414.6 6.6 %shard_map.157 = bf16[320,3584]{1,0:T(8,128)(2,1)S(1)} custom-call(bf16[320,1024]{1,0:T(8,128)(2,1)S(1)} %get-tuple-element.506.refs_0_, bf16[320,1024]{1,0:T(8,128)(2,1)S(1)} %get-tuple-element.505.refs_1_, bf16[3584,1024]{1,0:T(8,128)(2,1)S(1)} %bitcast.360, bf16[3584,1024]{1,0:T(8,128)(2,1)S(1)} %bitcast.374), custom_call_target="tpu_custom_call" | custom-call | flops 1048576 | bytes 65536 | tf_op jit(solution)/shard_map/pallas_call | solution.py:103
  421.5 10.9 %collective-permute-done.58 = bf16[80,3712]{1,0:T(8,128)(2,1)S(1)} collective-permute-done((bf16[80,3712]{1,0:T(8,128)(2,1)S(1)}, bf16[80,3712]{1,0:T(8,128)(2,1)S(1)}, u32[]{:S(2)}, u32[]{:S(2)}) %collective-permute-start.58) | collective-permute-done | bytes 593952 | tf_op jit(solution)/shard_map/ppermute | solution.py:45
  444.2 7.7 %collective-permute-start.64 = (bf16[128,3712]{0,1:T(8,128)(2,1)S(1)}, bf16[128,3712]{0,1:T(8,128)(2,1)S(1)}, u32[]{:S(2)}, u32[]{:S(2)}) collective-permute-start(bf16[128,3712]{0,1:T(8,128)(2,1)S(1)} %fusion.32), channel_id=1, source_target_pairs={{0,4},{1,5},{2,6},{3,7},{12,8},{13,9},{14,10},{15,11},{16,20},{17,... | collective-permute-start | bytes 2850824 | tf_op jit(solution)/shard_map/ppermute | solution.py:39
  453.9 6.3 %shard_map.158 = bf16[320,3584]{1,0:T(8,128)(2,1)S(1)} custom-call(bf16[320,1024]{1,0:T(8,128)(2,1)S(1)} %get-tuple-element.502.refs_0_, bf16[320,1024]{1,0:T(8,128)(2,1)S(1)} %get-tuple-element.501.refs_1_, bf16[3584,1024]{1,0:T(8,128)(2,1)S(1)} %bitcast.361, bf16[3584,1024]{1,0:T(8,128)(2,1)S(1)} %bitcast.375), custom_call_target="tpu_custom_call" | custom-call | flops 1048576 | bytes 65536 | tf_op jit(solution)/shard_map/pallas_call | solution.py:103
  460.4 9.4 %collective-permute-done.66 = bf16[80,3712]{1,0:T(8,128)(2,1)S(1)} collective-permute-done((bf16[80,3712]{1,0:T(8,128)(2,1)S(1)}, bf16[80,3712]{1,0:T(8,128)(2,1)S(1)}, u32[]{:S(2)}, u32[]{:S(2)}) %collective-permute-start.66) | collective-permute-done | bytes 593952 | tf_op jit(solution)/shard_map/ppermute | solution.py:45
  486.6 13.0 %collective-permute-done.73 = bf16[80,3712]{1,0:T(8,128)(2,1)S(1)} collective-permute-done((bf16[80,3712]{1,0:T(8,128)(2,1)}, bf16[80,3712]{1,0:T(8,128)(2,1)S(1)}, u32[]{:S(2)}, u32[]{:S(2)}) %collective-permute-start.73) | collective-permute-done | bytes 593952 | tf_op jit(solution)/shard_map/ppermute | solution.py:45
  499.6 10.2 %collective-permute-done.74 = bf16[80,3712]{1,0:T(8,128)(2,1)S(1)} collective-permute-done((bf16[80,3712]{1,0:T(8,128)(2,1)}, bf16[80,3712]{1,0:T(8,128)(2,1)S(1)}, u32[]{:S(2)}, u32[]{:S(2)}) %collective-permute-start.74) | collective-permute-done | bytes 593952 | tf_op jit(solution)/shard_map/ppermute | solution.py:45
  (563 shorter events, 327.3 us)
Async XLA Ops:
  31.1 27.2 %collective-permute-start.3 = (bf16[2048,224]{0,1:T(8,128)(2,1)}, bf16[2048,224]{0,1:T(8,128)(2,1)S(1)}, u32[]{:S(2)}, u32[]{:S(2)}) collective-permute-start(bf16[2048,224]{0,1:T(8,128)(2,1)} %collective-permute-done.1), channel_id=1, source_target_pairs={{4,0},{5,1},{6,2},{7,3},{8,12},{9,13},{10,14},{11,15},{20,16},{21,... | collective-permute-start | bytes 2752520 | tf_op jit(solution)/shard_map/ppermute | solution.py:39
  59.5 32.2 %collective-permute-start.7 = (bf16[2048,224]{0,1:T(8,128)(2,1)S(1)}, bf16[2048,224]{0,1:T(8,128)(2,1)}, u32[]{:S(2)}, u32[]{:S(2)}) collective-permute-start(bf16[2048,224]{0,1:T(8,128)(2,1)S(1)} %collective-permute-done.2), channel_id=1, source_target_pairs={{4,0},{5,1},{6,2},{7,3},{8,12},{9,13},{10,14},{11,15},{20,16},{21,... | collective-permute-start | bytes 2752520 | tf_op jit(solution)/shard_map/ppermute | solution.py:39
  64.4 27.4 %collective-permute-start.9 = (bf16[80,3584]{1,0:T(8,128)(2,1)S(1)}, bf16[80,3584]{1,0:T(8,128)(2,1)S(1)}, u32[]{:S(2)}, u32[]{:S(2)}) collective-permute-start(bf16[80,3584]{1,0:T(8,128)(2,1)S(1)} %copy-done.57), channel_id=1, source_target_pairs={{0,2},{1,3},{2,0},{3,1},{4,6},{5,7},{6,4},{7,5},{8,10},{9,11},{10,... | collective-permute-start | bytes 1720328 | tf_op jit(solution)/shard_map/ppermute | solution.py:45
  132.8 27.1 %collective-permute-start.19 = (bf16[80,3584]{1,0:T(8,128)(2,1)S(1)}, bf16[80,3584]{1,0:T(8,128)(2,1)S(1)}, u32[]{:S(2)}, u32[]{:S(2)}) collective-permute-start(bf16[80,3584]{1,0:T(8,128)(2,1)S(1)} %copy-done.56), channel_id=1, source_target_pairs={{0,2},{1,3},{2,0},{3,1},{4,6},{5,7},{6,4},{7,5},{8,10},{9,11},{10,... | collective-permute-start | bytes 1720328 | tf_op jit(solution)/shard_map/ppermute | solution.py:45
  133.4 26.5 %collective-permute-start.20 = (bf16[80,3584]{1,0:T(8,128)(2,1)S(1)}, bf16[80,3584]{1,0:T(8,128)(2,1)S(1)}, u32[]{:S(2)}, u32[]{:S(2)}) collective-permute-start(bf16[80,3584]{1,0:T(8,128)(2,1)S(1)} %copy-done.54), channel_id=1, source_target_pairs={{0,3},{1,2},{2,1},{3,0},{4,7},{5,6},{6,5},{7,4},{8,11},{9,10},{10,... | collective-permute-start | bytes 1720328 | tf_op jit(solution)/shard_map/ppermute | solution.py:45
  164.5 30.1 %collective-permute-start.22 = (bf16[128,3712]{0,1:T(8,128)(2,1)S(1)}, bf16[128,3712]{0,1:T(8,128)(2,1)S(1)}, u32[]{:S(2)}, u32[]{:S(2)}) collective-permute-start(bf16[128,3712]{0,1:T(8,128)(2,1)S(1)} %pad_maximum_fusion.25), channel_id=1, source_target_pairs={{0,4},{1,5},{2,6},{3,7},{4,0},{5,1},{6,2},{7,3},{8,12},{9,13},{10,... | collective-permute-start | bytes 2850824 | tf_op jit(solution)/shard_map/ppermute | solution.py:39
  167.5 27.0 %collective-permute-start.23 = (bf16[128,3712]{0,1:T(8,128)(2,1)S(1)}, bf16[128,3712]{0,1:T(8,128)(2,1)S(1)}, u32[]{:S(2)}, u32[]{:S(2)}) collective-permute-start(bf16[128,3712]{0,1:T(8,128)(2,1)S(1)} %pad_maximum_fusion.25), channel_id=1, source_target_pairs={{4,8},{5,9},{6,10},{7,11},{8,4},{9,5},{10,6},{11,7},{20,24},{21,25... | collective-permute-start | bytes 2850824 | tf_op jit(solution)/shard_map/ppermute | solution.py:39
  195.7 28.2 %collective-permute-start.27 = (bf16[128,3712]{0,1:T(8,128)(2,1)S(1)}, bf16[128,3712]{0,1:T(8,128)(2,1)S(1)}, u32[]{:S(2)}, u32[]{:S(2)}) collective-permute-start(bf16[128,3712]{0,1:T(8,128)(2,1)S(1)} %collective-permute-done.22), channel_id=1, source_target_pairs={{4,8},{5,9},{6,10},{7,11},{8,4},{9,5},{10,6},{11,7},{20,24},{21,25... | collective-permute-start | bytes 2850824 | tf_op jit(solution)/shard_map/ppermute | solution.py:39
  196.4 27.4 %collective-permute-start.28 = (bf16[128,3712]{0,1:T(8,128)(2,1)S(1)}, bf16[128,3712]{0,1:T(8,128)(2,1)S(1)}, u32[]{:S(2)}, u32[]{:S(2)}) collective-permute-start(bf16[128,3712]{0,1:T(8,128)(2,1)S(1)} %collective-permute-done.23), channel_id=1, source_target_pairs={{4,0},{5,1},{6,2},{7,3},{8,12},{9,13},{10,14},{11,15},{20,16},{21,... | collective-permute-start | bytes 2850824 | tf_op jit(solution)/shard_map/ppermute | solution.py:39
  226.2 27.3 %collective-permute-start.32 = (bf16[128,3712]{0,1:T(8,128)(2,1)S(1)}, bf16[128,3712]{0,1:T(8,128)(2,1)S(1)}, u32[]{:S(2)}, u32[]{:S(2)}) collective-permute-start(bf16[128,3712]{0,1:T(8,128)(2,1)S(1)} %collective-permute-done.27), channel_id=1, source_target_pairs={{4,0},{5,1},{6,2},{7,3},{8,12},{9,13},{10,14},{11,15},{20,16},{21,... | collective-permute-start | bytes 2850824 | tf_op jit(solution)/shard_map/ppermute | solution.py:39
  256.4 26.3 %collective-permute-start.37 = (bf16[128,3712]{0,1:T(8,128)(2,1)}, bf16[128,3712]{0,1:T(8,128)(2,1)}, u32[]{:S(2)}, u32[]{:S(2)}) collective-permute-start(bf16[128,3712]{0,1:T(8,128)(2,1)} %collective-permute-done.33), channel_id=1, source_target_pairs={{4,0},{5,1},{6,2},{7,3},{8,12},{9,13},{10,14},{11,15},{20,16},{21,... | collective-permute-start | bytes 2850824 | tf_op jit(solution)/shard_map/ppermute | solution.py:39
  322.2 27.1 %collective-permute-start.45 = (bf16[80,3584]{1,0:T(8,128)(2,1)S(1)}, bf16[80,3584]{1,0:T(8,128)(2,1)S(1)}, u32[]{:S(2)}, u32[]{:S(2)}) collective-permute-start(bf16[80,3584]{1,0:T(8,128)(2,1)S(1)} %copy-done.52), channel_id=1, source_target_pairs={{0,2},{1,3},{2,0},{3,1},{4,6},{5,7},{6,4},{7,5},{8,10},{9,11},{10,... | collective-permute-start | bytes 1720328 | tf_op jit(solution)/shard_map/ppermute | solution.py:45
  322.5 26.8 %collective-permute-start.46 = (bf16[80,3584]{1,0:T(8,128)(2,1)S(1)}, bf16[80,3584]{1,0:T(8,128)(2,1)S(1)}, u32[]{:S(2)}, u32[]{:S(2)}) collective-permute-start(bf16[80,3584]{1,0:T(8,128)(2,1)S(1)} %copy-done.51), channel_id=1, source_target_pairs={{0,3},{1,2},{2,1},{3,0},{4,7},{5,6},{6,5},{7,4},{8,11},{9,10},{10,... | collective-permute-start | bytes 1720328 | tf_op jit(solution)/shard_map/ppermute | solution.py:45
  365.1 30.4 %collective-permute-start.50 = (bf16[80,3712]{1,0:T(8,128)(2,1)S(1)}, bf16[80,3712]{1,0:T(8,128)(2,1)S(1)}, u32[]{:S(2)}, u32[]{:S(2)}) collective-permute-start(bf16[80,3712]{1,0:T(8,128)(2,1)S(1)} %copy-done.44), channel_id=1, source_target_pairs={{0,1},{1,0},{2,3},{3,2},{4,5},{5,4},{6,7},{7,6},{8,9},{9,8},{10,11... | collective-permute-start | bytes 1781768 | tf_op jit(solution)/shard_map/ppermute | solution.py:45
  365.6 30.0 %collective-permute-start.51 = (bf16[80,3712]{1,0:T(8,128)(2,1)S(1)}, bf16[80,3712]{1,0:T(8,128)(2,1)S(1)}, u32[]{:S(2)}, u32[]{:S(2)}) collective-permute-start(bf16[80,3712]{1,0:T(8,128)(2,1)S(1)} %copy-done.43), channel_id=1, source_target_pairs={{0,2},{1,3},{2,0},{3,1},{4,6},{5,7},{6,4},{7,5},{8,10},{9,11},{10,... | collective-permute-start | bytes 1781768 | tf_op jit(solution)/shard_map/ppermute | solution.py:45
  367.3 28.3 %collective-permute-start.52 = (bf16[80,3712]{1,0:T(8,128)(2,1)S(1)}, bf16[80,3712]{1,0:T(8,128)(2,1)S(1)}, u32[]{:S(2)}, u32[]{:S(2)}) collective-permute-start(bf16[80,3712]{1,0:T(8,128)(2,1)S(1)} %copy-done.42), channel_id=1, source_target_pairs={{0,3},{1,2},{2,1},{3,0},{4,7},{5,6},{6,5},{7,4},{8,11},{9,10},{10,... | collective-permute-start | bytes 1781768 | tf_op jit(solution)/shard_map/ppermute | solution.py:45
  404.5 27.9 %collective-permute-start.58 = (bf16[80,3712]{1,0:T(8,128)(2,1)S(1)}, bf16[80,3712]{1,0:T(8,128)(2,1)S(1)}, u32[]{:S(2)}, u32[]{:S(2)}) collective-permute-start(bf16[80,3712]{1,0:T(8,128)(2,1)S(1)} %get-tuple-element.361), channel_id=1, source_target_pairs={{0,2},{1,3},{2,0},{3,1},{4,6},{5,7},{6,4},{7,5},{8,10},{9,11},{10,... | collective-permute-start | bytes 1781768 | tf_op jit(solution)/shard_map/ppermute | solution.py:45
  406.2 26.2 %collective-permute-start.59 = (bf16[80,3712]{1,0:T(8,128)(2,1)S(1)}, bf16[80,3712]{1,0:T(8,128)(2,1)S(1)}, u32[]{:S(2)}, u32[]{:S(2)}) collective-permute-start(bf16[80,3712]{1,0:T(8,128)(2,1)S(1)} %get-tuple-element.362), channel_id=1, source_target_pairs={{0,3},{1,2},{2,1},{3,0},{4,7},{5,6},{6,5},{7,4},{8,11},{9,10},{10,... | collective-permute-start | bytes 1781768 | tf_op jit(solution)/shard_map/ppermute | solution.py:45
  407.6 26.3 %collective-permute-start.56 = (bf16[128,3712]{0,1:T(8,128)(2,1)S(1)}, bf16[128,3712]{0,1:T(8,128)(2,1)S(1)}, u32[]{:S(2)}, u32[]{:S(2)}) collective-permute-start(bf16[128,3712]{0,1:T(8,128)(2,1)S(1)} %fusion.33), channel_id=1, source_target_pairs={{0,4},{1,5},{2,6},{3,7},{12,8},{13,9},{14,10},{15,11},{16,20},{17,... | collective-permute-start | bytes 2850824 | tf_op jit(solution)/shard_map/ppermute | solution.py:39
  441.9 27.9 %collective-permute-start.66 = (bf16[80,3712]{1,0:T(8,128)(2,1)S(1)}, bf16[80,3712]{1,0:T(8,128)(2,1)S(1)}, u32[]{:S(2)}, u32[]{:S(2)}) collective-permute-start(bf16[80,3712]{1,0:T(8,128)(2,1)S(1)} %get-tuple-element.374), channel_id=1, source_target_pairs={{0,2},{1,3},{2,0},{3,1},{4,6},{5,7},{6,4},{7,5},{8,10},{9,11},{10,... | collective-permute-start | bytes 1781768 | tf_op jit(solution)/shard_map/ppermute | solution.py:45
  443.5 26.3 %collective-permute-start.63 = (bf16[128,3712]{0,1:T(8,128)(2,1)S(1)}, bf16[128,3712]{0,1:T(8,128)(2,1)S(1)}, u32[]{:S(2)}, u32[]{:S(2)}) collective-permute-start(bf16[128,3712]{0,1:T(8,128)(2,1)S(1)} %add_convert_fusion.1), channel_id=1, source_target_pairs={{4,8},{5,9},{6,10},{7,11},{8,4},{9,5},{10,6},{11,7},{20,24},{21,25... | collective-permute-start | bytes 2850824 | tf_op jit(solution)/shard_map/ppermute | solution.py:39
  444.2 27.4 %collective-permute-start.64 = (bf16[128,3712]{0,1:T(8,128)(2,1)S(1)}, bf16[128,3712]{0,1:T(8,128)(2,1)S(1)}, u32[]{:S(2)}, u32[]{:S(2)}) collective-permute-start(bf16[128,3712]{0,1:T(8,128)(2,1)S(1)} %fusion.32), channel_id=1, source_target_pairs={{0,4},{1,5},{2,6},{3,7},{12,8},{13,9},{14,10},{15,11},{16,20},{17,... | collective-permute-start | bytes 2850824 | tf_op jit(solution)/shard_map/ppermute | solution.py:39
  476.7 33.1 %collective-permute-start.71 = (bf16[128,3712]{0,1:T(8,128)(2,1)S(1)}, bf16[128,3712]{0,1:T(8,128)(2,1)S(1)}, u32[]{:S(2)}, u32[]{:S(2)}) collective-permute-start(bf16[128,3712]{0,1:T(8,128)(2,1)S(1)} %add_convert_fusion), channel_id=1, source_target_pairs={{4,8},{5,9},{6,10},{7,11},{8,4},{9,5},{10,6},{11,7},{20,24},{21,25... | collective-permute-start | bytes 2850824 | tf_op jit(solution)/shard_map/ppermute | solution.py:39
  477.7 32.2 %collective-permute-start.72 = (bf16[128,3712]{0,1:T(8,128)(2,1)}, bf16[128,3712]{0,1:T(8,128)(2,1)}, u32[]{:S(2)}, u32[]{:S(2)}) collective-permute-start(bf16[128,3712]{0,1:T(8,128)(2,1)} %fusion.20), channel_id=1, source_target_pairs={{0,4},{1,5},{2,6},{3,7},{4,0},{5,1},{6,2},{7,3},{8,12},{9,13},{10,... | collective-permute-start | bytes 2850824 | tf_op jit(solution)/shard_map/ppermute | solution.py:39
  (147 other events, 1639.0 us)

commit v5 on v4

--- a/solution.py
+++ b/solution.py
@@ -209,7 +209,7 @@
     step = Steps(n_ep)
     steps = jnp.arange(plane, dtype=jnp.int32)
     relay_expert = z * plane + (place ^ steps)
-    lanes = -(-(2 * n_ep + TOP) // 128) * 128
+    lanes = -(-(n_ep + TOP) // 128) * 128
 
     def with_lanes(x, extra):
         extra = jnp.pad(extra.astype(bf16), ((0, 0), (0, lanes - extra.shape[1])))
@@ -257,16 +257,11 @@
 
     def relay_sum(hot, table, arrived):
         arrived = arrived.reshape(plane * capacity, -1)
-        high = jnp.take(table, relay_expert, axis=1).T[:, None, :]
-        low = jnp.take(table, n_ep + relay_expert, axis=1).T[:, None, :]
+        picked_weights = jnp.take(table, relay_expert, axis=1).T[:, None, :]
         tokens = hot.reshape(plane, capacity, length)
-        mix = jnp.concatenate([tokens * high, tokens * low], axis=0).reshape(-1, length)
-        row_part = arrived[:, :slice_width]
+        mix = (tokens * picked_weights).reshape(-1, length)
         total = jnp.einsum(
-            "ri,rd->id",
-            mix,
-            jnp.concatenate([row_part, row_part], axis=0),
-            preferred_element_type=jnp.float32,
+            "ri,rd->id", mix, arrived[:, :slice_width], preferred_element_type=jnp.float32
         )
         lane_part = jnp.einsum(
             "ri,rd->id", hot, arrived[:, slice_width:], preferred_element_type=jnp.float32
@@ -339,9 +334,7 @@
         totals = jnp.sum(picked, axis=1, keepdims=True)
         weights = route_scale * picked / totals
         table = jnp.sum(jnp.where(one_hot, weights[:, :, None], 0.0), axis=1)
-        high = table.astype(bf16)
-        low = (table - high.astype(jnp.float32)).astype(bf16)
-        marks = jnp.concatenate([high, low, routes.astype(bf16)], axis=1)
+        marks = jnp.concatenate([table.astype(bf16), routes.astype(bf16)], axis=1)
         return residual, inv_rms, picked, totals, with_lanes(normed, marks)
 
     hot_partner, grad_blocks = slots_pack(grad_partner)
@@ -385,7 +378,7 @@
     )
     rows_near = from_plane(blocks, arrived)
     normed_far = normed_far + outer
-    hot_far = slots_of(normed_far, 2 * n_ep)
+    hot_far = slots_of(normed_far, n_ep)
     blocks = pack(normed_far, hot_far)
     outer, *arrived, pre_near = step.run(
         [(grad_far, OUTWARD)] + to_plane(blocks), gate_up, (rows_near,)

time: 576 us -> 571 us (level)
  transfers between devices with their start and end apart: 84 -> 84, of which waited for: 40 -> 41; matrix products, arithmetic and copies ran while one was open for 5% -> 4% of each run, Pallas kernels for 12% -> 12%
where the time goes in v5:
time: 571 us; the launch traced here: 561 us
  waiting for transfers between devices  256 us (45%)
  starting transfers between devices  105 us (18%)
  Pallas kernels  68.5 us (12%)
  local copies, waits for them, and re-layouts  62 us (11%)
  other arithmetic  35.8 us (6%)
  matrix products  29.9 us (5%)
    ppermute x48, waiting for transfers between devices, plane_permute(): return lax.ppermute(x, 'ep', [(i, i ^ step) for i in range(n_ep)])  203 us
    ppermute x48, starting transfers between devices, plane_permute(): return lax.ppermute(x, 'ep', [(i, i ^ step) for i in range(n_ep)])  56.3 us
    ppermute x20, starting transfers between devices, depth_permute(): lax.ppermute(x, 'ep', [(a * plane + i, b * plane + i) for a, b in pairs f...  46.1 us
    ppermute x20, waiting for transfers between devices, depth_permute(): lax.ppermute(x, 'ep', [(a * plane + i, b * plane + i) for a, b in pairs f...  41.1 us
    unnamed x183, local copies, waits for them, and re-layouts  40 us
    pallas_call x8, Pallas kernels, summed_products(): pl.pallas_call(summed_kernel, grid=(height // tile,), in_specs=[whole(x)...  38.3 us
    pallas_call x4, Pallas kernels, products(): pl.pallas_call(products_kernel, grid=(width // tile,), in_specs=[whole(ro...  30.2 us
    ppermute x16, waiting for transfers between devices, tp_swap(): return lax.ppermute(x, 'tp', [(0, 1), (1, 0)])  12.1 us
  transfers between devices with their start and end apart: 84, of which 41 were waited for; matrix products, arithmetic and copies ran while one was open for 4% of the time, Pallas kernels for 12%

profile of v5, /device:TPU:0, one launch (start us, length us, event | category | flops | bytes accessed | tf_op | source)
XLA Modules:
  0.0 561.2 jit_solution(4040588531456144295)
XLA Ops:
  10.8 16.1 %collective-permute-done = bf16[2048,224]{0,1:T(8,128)(2,1)} collective-permute-done((bf16[2048,224]{0,1:T(8,128)(2,1)}, bf16[2048,224]{0,1:T(8,128)(2,1)}, u32[]{:S(2)}, u32[]{:S(2)}) %collective-permute-start) | collective-permute-done | bytes 917536 | tf_op jit(solution)/shard_map/ppermute | solution.py:39
  41.0 17.2 %collective-permute-done.3 = bf16[2048,224]{0,1:T(8,128)(2,1)S(1)} collective-permute-done((bf16[2048,224]{0,1:T(8,128)(2,1)}, bf16[2048,224]{0,1:T(8,128)(2,1)S(1)}, u32[]{:S(2)}, u32[]{:S(2)}) %collective-permute-start.3) | collective-permute-done | bytes 917536 | tf_op jit(solution)/shard_map/ppermute | solution.py:39
  67.9 10.7 %collective-permute-done.8 = bf16[80,3584]{1,0:T(8,128)(2,1)S(1)} collective-permute-done((bf16[80,3584]{1,0:T(8,128)(2,1)S(1)}, bf16[80,3584]{1,0:T(8,128)(2,1)S(1)}, u32[]{:S(2)}, u32[]{:S(2)}) %collective-permute-start.8) | collective-permute-done | bytes 573472 | tf_op jit(solution)/shard_map/ppermute | solution.py:45
  78.7 13.1 %collective-permute-done.9 = bf16[80,3584]{1,0:T(8,128)(2,1)S(1)} collective-permute-done((bf16[80,3584]{1,0:T(8,128)(2,1)S(1)}, bf16[80,3584]{1,0:T(8,128)(2,1)S(1)}, u32[]{:S(2)}, u32[]{:S(2)}) %collective-permute-start.9) | collective-permute-done | bytes 573472 | tf_op jit(solution)/shard_map/ppermute | solution.py:45
  137.2 10.0 %collective-permute-done.18 = bf16[80,3584]{1,0:T(8,128)(2,1)S(1)} collective-permute-done((bf16[80,3584]{1,0:T(8,128)(2,1)S(1)}, bf16[80,3584]{1,0:T(8,128)(2,1)S(1)}, u32[]{:S(2)}, u32[]{:S(2)}) %collective-permute-start.18) | collective-permute-done | bytes 573472 | tf_op jit(solution)/shard_map/ppermute | solution.py:45
  147.3 12.7 %collective-permute-done.19 = bf16[80,3584]{1,0:T(8,128)(2,1)S(1)} collective-permute-done((bf16[80,3584]{1,0:T(8,128)(2,1)S(1)}, bf16[80,3584]{1,0:T(8,128)(2,1)S(1)}, u32[]{:S(2)}, u32[]{:S(2)}) %collective-permute-start.19) | collective-permute-done | bytes 573472 | tf_op jit(solution)/shard_map/ppermute | solution.py:45
  184.3 10.3 %collective-permute-done.25 = bf16[80,3584]{1,0:T(8,128)(2,1)S(1)} collective-permute-done((bf16[80,3584]{1,0:T(8,128)(2,1)S(1)}, bf16[80,3584]{1,0:T(8,128)(2,1)S(1)}, u32[]{:S(2)}, u32[]{:S(2)}) %collective-permute-start.25) | collective-permute-done | bytes 573472 | tf_op jit(solution)/shard_map/ppermute | solution.py:45
  205.5 8.3 %collective-permute-done.29 = bf16[80,3584]{1,0:T(8,128)(2,1)S(1)} collective-permute-done((bf16[80,3584]{1,0:T(8,128)(2,1)S(1)}, bf16[80,3584]{1,0:T(8,128)(2,1)S(1)}, u32[]{:S(2)}, u32[]{:S(2)}) %collective-permute-start.29) | collective-permute-done | bytes 573472 | tf_op jit(solution)/shard_map/ppermute | solution.py:45
  213.8 8.4 %collective-permute-done.30 = bf16[80,3584]{1,0:T(8,128)(2,1)S(1)} collective-permute-done((bf16[80,3584]{1,0:T(8,128)(2,1)S(1)}, bf16[80,3584]{1,0:T(8,128)(2,1)S(1)}, u32[]{:S(2)}, u32[]{:S(2)}) %collective-permute-start.30) | collective-permute-done | bytes 573472 | tf_op jit(solution)/shard_map/ppermute | solution.py:45
  232.8 7.5 %shard_map.150 = (bf16[320,1024]{1,0:T(8,128)(2,1)S(1)}, bf16[320,1024]{1,0:T(8,128)(2,1)S(1)}) custom-call(bf16[320,3584]{1,0:T(8,128)(2,1)S(1)} %pad_maximum_fusion.12.rows_ref, bf16[3584,1024]{1,0:T(8,128)(2,1)S(1)} %bitcast.351, bf16[3584,1024]{1,0:T(8,128)(2,1)S(1)} %bitcast.367), custom_call_target="tpu_custom_call" | custom-call | flops 1048576 | bytes 65536 | tf_op jit(solution)/shard_map/pallas_call | solution.py:74
  245.2 8.4 %collective-permute-done.35 = bf16[80,3584]{1,0:T(8,128)(2,1)S(1)} collective-permute-done((bf16[80,3584]{1,0:T(8,128)(2,1)S(1)}, bf16[80,3584]{1,0:T(8,128)(2,1)S(1)}, u32[]{:S(2)}, u32[]{:S(2)}) %collective-permute-start.35) | collective-permute-done | bytes 573472 | tf_op jit(solution)/shard_map/ppermute | solution.py:45
  268.0 7.5 %shard_map.151 = (bf16[320,1024]{1,0:T(8,128)(2,1)S(1)}, bf16[320,1024]{1,0:T(8,128)(2,1)S(1)}) custom-call(bf16[320,3584]{1,0:T(8,128)(2,1)S(1)} %pad_maximum_fusion.13.rows_ref, bf16[3584,1024]{1,0:T(8,128)(2,1)S(1)} %bitcast.352, bf16[3584,1024]{1,0:T(8,128)(2,1)S(1)} %bitcast.368), custom_call_target="tpu_custom_call" | custom-call | flops 1048576 | bytes 65536 | tf_op jit(solution)/shard_map/pallas_call | solution.py:74
  292.2 7.6 %shard_map.152 = (bf16[320,1024]{1,0:T(8,128)(2,1)S(1)}, bf16[320,1024]{1,0:T(8,128)(2,1)S(1)}) custom-call(bf16[320,3584]{1,0:T(8,128)(2,1)S(1)} %pad_maximum_fusion.14.rows_ref, bf16[3584,1024]{1,0:T(8,128)(2,1)S(1)} %bitcast.355, bf16[3584,1024]{1,0:T(8,128)(2,1)S(1)} %bitcast.371), custom_call_target="tpu_custom_call" | custom-call | flops 1048576 | bytes 65536 | tf_op jit(solution)/shard_map/pallas_call | solution.py:74
  303.2 6.6 %collective-permute-done.42 = bf16[80,3584]{1,0:T(8,128)(2,1)S(1)} collective-permute-done((bf16[80,3584]{1,0:T(8,128)(2,1)S(1)}, bf16[80,3584]{1,0:T(8,128)(2,1)S(1)}, u32[]{:S(2)}, u32[]{:S(2)}) %collective-permute-start.42) | collective-permute-done | bytes 573472 | tf_op jit(solution)/shard_map/ppermute | solution.py:45
  336.5 12.9 %collective-permute-done.45 = bf16[80,3584]{1,0:T(8,128)(2,1)S(1)} collective-permute-done((bf16[80,3584]{1,0:T(8,128)(2,1)S(1)}, bf16[80,3584]{1,0:T(8,128)(2,1)S(1)}, u32[]{:S(2)}, u32[]{:S(2)}) %collective-permute-start.45) | collective-permute-done | bytes 573472 | tf_op jit(solution)/shard_map/ppermute | solution.py:45
  372.1 7.6 %shard_map.156 = (bf16[320,1024]{1,0:T(8,128)(2,1)S(1)}, bf16[320,1024]{1,0:T(8,128)(2,1)S(1)}) custom-call(bf16[320,3584]{1,0:T(8,128)(2,1)S(1)} %pad_maximum_fusion.16.rows_ref, bf16[3584,1024]{1,0:T(8,128)(2,1)S(1)} %bitcast.359, bf16[3584,1024]{1,0:T(8,128)(2,1)S(1)} %bitcast.373), custom_call_target="tpu_custom_call" | custom-call | flops 1048576 | bytes 65536 | tf_op jit(solution)/shard_map/pallas_call | solution.py:74
  404.1 6.5 %collective-permute-start.56 = (bf16[128,3712]{0,1:T(8,128)(2,1)S(1)}, bf16[128,3712]{0,1:T(8,128)(2,1)S(1)}, u32[]{:S(2)}, u32[]{:S(2)}) collective-permute-start(bf16[128,3712]{0,1:T(8,128)(2,1)S(1)} %fusion.25), channel_id=1, source_target_pairs={{0,4},{1,5},{2,6},{3,7},{12,8},{13,9},{14,10},{15,11},{16,20},{17,... | collective-permute-start | bytes 2850824 | tf_op jit(solution)/shard_map/ppermute | solution.py:39
  411.1 6.4 %shard_map.157 = bf16[320,3584]{1,0:T(8,128)(2,1)S(1)} custom-call(bf16[320,1024]{1,0:T(8,128)(2,1)S(1)} %get-tuple-element.502.refs_0_, bf16[320,1024]{1,0:T(8,128)(2,1)S(1)} %get-tuple-element.501.refs_1_, bf16[3584,1024]{1,0:T(8,128)(2,1)S(1)} %bitcast.363, bf16[3584,1024]{1,0:T(8,128)(2,1)S(1)} %bitcast.377), custom_call_target="tpu_custom_call" | custom-call | flops 1048576 | bytes 65536 | tf_op jit(solution)/shard_map/pallas_call | solution.py:103
  417.7 11.2 %collective-permute-done.58 = bf16[80,3712]{1,0:T(8,128)(2,1)S(1)} collective-permute-done((bf16[80,3712]{1,0:T(8,128)(2,1)S(1)}, bf16[80,3712]{1,0:T(8,128)(2,1)S(1)}, u32[]{:S(2)}, u32[]{:S(2)}) %collective-permute-start.58) | collective-permute-done | bytes 593952 | tf_op jit(solution)/shard_map/ppermute | solution.py:45
  439.9 7.9 %collective-permute-start.64 = (bf16[128,3712]{0,1:T(8,128)(2,1)S(1)}, bf16[128,3712]{0,1:T(8,128)(2,1)S(1)}, u32[]{:S(2)}, u32[]{:S(2)}) collective-permute-start(bf16[128,3712]{0,1:T(8,128)(2,1)S(1)} %fusion.24), channel_id=1, source_target_pairs={{0,4},{1,5},{2,6},{3,7},{12,8},{13,9},{14,10},{15,11},{16,20},{17,... | collective-permute-start | bytes 2850824 | tf_op jit(solution)/shard_map/ppermute | solution.py:39
  449.8 6.3 %shard_map.158 = bf16[320,3584]{1,0:T(8,128)(2,1)S(1)} custom-call(bf16[320,1024]{1,0:T(8,128)(2,1)S(1)} %get-tuple-element.498.refs_0_, bf16[320,1024]{1,0:T(8,128)(2,1)S(1)} %get-tuple-element.497.refs_1_, bf16[3584,1024]{1,0:T(8,128)(2,1)S(1)} %bitcast.364, bf16[3584,1024]{1,0:T(8,128)(2,1)S(1)} %bitcast.378), custom_call_target="tpu_custom_call" | custom-call | flops 1048576 | bytes 65536 | tf_op jit(solution)/shard_map/pallas_call | solution.py:103
  456.3 9.2 %collective-permute-done.66 = bf16[80,3712]{1,0:T(8,128)(2,1)S(1)} collective-permute-done((bf16[80,3712]{1,0:T(8,128)(2,1)S(1)}, bf16[80,3712]{1,0:T(8,128)(2,1)S(1)}, u32[]{:S(2)}, u32[]{:S(2)}) %collective-permute-start.66) | collective-permute-done | bytes 593952 | tf_op jit(solution)/shard_map/ppermute | solution.py:45
  482.2 13.0 %collective-permute-done.73 = bf16[80,3712]{1,0:T(8,128)(2,1)S(1)} collective-permute-done((bf16[80,3712]{1,0:T(8,128)(2,1)}, bf16[80,3712]{1,0:T(8,128)(2,1)S(1)}, u32[]{:S(2)}, u32[]{:S(2)}) %collective-permute-start.73) | collective-permute-done | bytes 593952 | tf_op jit(solution)/shard_map/ppermute | solution.py:45
  495.1 10.2 %collective-permute-done.74 = bf16[80,3712]{1,0:T(8,128)(2,1)S(1)} collective-permute-done((bf16[80,3712]{1,0:T(8,128)(2,1)}, bf16[80,3712]{1,0:T(8,128)(2,1)S(1)}, u32[]{:S(2)}, u32[]{:S(2)}) %collective-permute-start.74) | collective-permute-done | bytes 593952 | tf_op jit(solution)/shard_map/ppermute | solution.py:45
  (547 shorter events, 322.3 us)
Async XLA Ops:
  31.1 27.2 %collective-permute-start.3 = (bf16[2048,224]{0,1:T(8,128)(2,1)}, bf16[2048,224]{0,1:T(8,128)(2,1)S(1)}, u32[]{:S(2)}, u32[]{:S(2)}) collective-permute-start(bf16[2048,224]{0,1:T(8,128)(2,1)} %collective-permute-done.1), channel_id=1, source_target_pairs={{4,0},{5,1},{6,2},{7,3},{8,12},{9,13},{10,14},{11,15},{20,16},{21,... | collective-permute-start | bytes 2752520 | tf_op jit(solution)/shard_map/ppermute | solution.py:39
  59.5 32.2 %collective-permute-start.7 = (bf16[2048,224]{0,1:T(8,128)(2,1)S(1)}, bf16[2048,224]{0,1:T(8,128)(2,1)}, u32[]{:S(2)}, u32[]{:S(2)}) collective-permute-start(bf16[2048,224]{0,1:T(8,128)(2,1)S(1)} %collective-permute-done.2), channel_id=1, source_target_pairs={{4,0},{5,1},{6,2},{7,3},{8,12},{9,13},{10,14},{11,15},{20,16},{21,... | collective-permute-start | bytes 2752520 | tf_op jit(solution)/shard_map/ppermute | solution.py:39
  64.4 27.4 %collective-permute-start.9 = (bf16[80,3584]{1,0:T(8,128)(2,1)S(1)}, bf16[80,3584]{1,0:T(8,128)(2,1)S(1)}, u32[]{:S(2)}, u32[]{:S(2)}) collective-permute-start(bf16[80,3584]{1,0:T(8,128)(2,1)S(1)} %copy-done.55), channel_id=1, source_target_pairs={{0,2},{1,3},{2,0},{3,1},{4,6},{5,7},{6,4},{7,5},{8,10},{9,11},{10,... | collective-permute-start | bytes 1720328 | tf_op jit(solution)/shard_map/ppermute | solution.py:45
  132.9 27.1 %collective-permute-start.19 = (bf16[80,3584]{1,0:T(8,128)(2,1)S(1)}, bf16[80,3584]{1,0:T(8,128)(2,1)S(1)}, u32[]{:S(2)}, u32[]{:S(2)}) collective-permute-start(bf16[80,3584]{1,0:T(8,128)(2,1)S(1)} %copy-done.58), channel_id=1, source_target_pairs={{0,2},{1,3},{2,0},{3,1},{4,6},{5,7},{6,4},{7,5},{8,10},{9,11},{10,... | collective-permute-start | bytes 1720328 | tf_op jit(solution)/shard_map/ppermute | solution.py:45
  133.4 26.5 %collective-permute-start.20 = (bf16[80,3584]{1,0:T(8,128)(2,1)S(1)}, bf16[80,3584]{1,0:T(8,128)(2,1)S(1)}, u32[]{:S(2)}, u32[]{:S(2)}) collective-permute-start(bf16[80,3584]{1,0:T(8,128)(2,1)S(1)} %copy-done.56), channel_id=1, source_target_pairs={{0,3},{1,2},{2,1},{3,0},{4,7},{5,6},{6,5},{7,4},{8,11},{9,10},{10,... | collective-permute-start | bytes 1720328 | tf_op jit(solution)/shard_map/ppermute | solution.py:45
  164.5 30.1 %collective-permute-start.22 = (bf16[128,3712]{0,1:T(8,128)(2,1)S(1)}, bf16[128,3712]{0,1:T(8,128)(2,1)S(1)}, u32[]{:S(2)}, u32[]{:S(2)}) collective-permute-start(bf16[128,3712]{0,1:T(8,128)(2,1)S(1)} %pad_maximum_fusion.25), channel_id=1, source_target_pairs={{0,4},{1,5},{2,6},{3,7},{4,0},{5,1},{6,2},{7,3},{8,12},{9,13},{10,... | collective-permute-start | bytes 2850824 | tf_op jit(solution)/shard_map/ppermute | solution.py:39
  167.6 27.1 %collective-permute-start.23 = (bf16[128,3712]{0,1:T(8,128)(2,1)S(1)}, bf16[128,3712]{0,1:T(8,128)(2,1)S(1)}, u32[]{:S(2)}, u32[]{:S(2)}) collective-permute-start(bf16[128,3712]{0,1:T(8,128)(2,1)S(1)} %pad_maximum_fusion.25), channel_id=1, source_target_pairs={{4,8},{5,9},{6,10},{7,11},{8,4},{9,5},{10,6},{11,7},{20,24},{21,25... | collective-permute-start | bytes 2850824 | tf_op jit(solution)/shard_map/ppermute | solution.py:39
  195.8 28.2 %collective-permute-start.27 = (bf16[128,3712]{0,1:T(8,128)(2,1)S(1)}, bf16[128,3712]{0,1:T(8,128)(2,1)S(1)}, u32[]{:S(2)}, u32[]{:S(2)}) collective-permute-start(bf16[128,3712]{0,1:T(8,128)(2,1)S(1)} %collective-permute-done.22), channel_id=1, source_target_pairs={{4,8},{5,9},{6,10},{7,11},{8,4},{9,5},{10,6},{11,7},{20,24},{21,25... | collective-permute-start | bytes 2850824 | tf_op jit(solution)/shard_map/ppermute | solution.py:39
  196.5 27.5 %collective-permute-start.28 = (bf16[128,3712]{0,1:T(8,128)(2,1)S(1)}, bf16[128,3712]{0,1:T(8,128)(2,1)S(1)}, u32[]{:S(2)}, u32[]{:S(2)}) collective-permute-start(bf16[128,3712]{0,1:T(8,128)(2,1)S(1)} %collective-permute-done.23), channel_id=1, source_target_pairs={{4,0},{5,1},{6,2},{7,3},{8,12},{9,13},{10,14},{11,15},{20,16},{21,... | collective-permute-start | bytes 2850824 | tf_op jit(solution)/shard_map/ppermute | solution.py:39
  226.3 27.3 %collective-permute-start.32 = (bf16[128,3712]{0,1:T(8,128)(2,1)S(1)}, bf16[128,3712]{0,1:T(8,128)(2,1)S(1)}, u32[]{:S(2)}, u32[]{:S(2)}) collective-permute-start(bf16[128,3712]{0,1:T(8,128)(2,1)S(1)} %collective-permute-done.27), channel_id=1, source_target_pairs={{4,0},{5,1},{6,2},{7,3},{8,12},{9,13},{10,14},{11,15},{20,16},{21,... | collective-permute-start | bytes 2850824 | tf_op jit(solution)/shard_map/ppermute | solution.py:39
  256.6 26.3 %collective-permute-start.37 = (bf16[128,3712]{0,1:T(8,128)(2,1)}, bf16[128,3712]{0,1:T(8,128)(2,1)}, u32[]{:S(2)}, u32[]{:S(2)}) collective-permute-start(bf16[128,3712]{0,1:T(8,128)(2,1)} %collective-permute-done.33), channel_id=1, source_target_pairs={{4,0},{5,1},{6,2},{7,3},{8,12},{9,13},{10,14},{11,15},{20,16},{21,... | collective-permute-start | bytes 2850824 | tf_op jit(solution)/shard_map/ppermute | solution.py:39
  322.4 27.1 %collective-permute-start.45 = (bf16[80,3584]{1,0:T(8,128)(2,1)S(1)}, bf16[80,3584]{1,0:T(8,128)(2,1)S(1)}, u32[]{:S(2)}, u32[]{:S(2)}) collective-permute-start(bf16[80,3584]{1,0:T(8,128)(2,1)S(1)} %copy-done.52), channel_id=1, source_target_pairs={{0,2},{1,3},{2,0},{3,1},{4,6},{5,7},{6,4},{7,5},{8,10},{9,11},{10,... | collective-permute-start | bytes 1720328 | tf_op jit(solution)/shard_map/ppermute | solution.py:45
  322.7 26.8 %collective-permute-start.46 = (bf16[80,3584]{1,0:T(8,128)(2,1)S(1)}, bf16[80,3584]{1,0:T(8,128)(2,1)S(1)}, u32[]{:S(2)}, u32[]{:S(2)}) collective-permute-start(bf16[80,3584]{1,0:T(8,128)(2,1)S(1)} %copy-done.51), channel_id=1, source_target_pairs={{0,3},{1,2},{2,1},{3,0},{4,7},{5,6},{6,5},{7,4},{8,11},{9,10},{10,... | collective-permute-start | bytes 1720328 | tf_op jit(solution)/shard_map/ppermute | solution.py:45
  362.4 30.4 %collective-permute-start.50 = (bf16[80,3712]{1,0:T(8,128)(2,1)S(1)}, bf16[80,3712]{1,0:T(8,128)(2,1)S(1)}, u32[]{:S(2)}, u32[]{:S(2)}) collective-permute-start(bf16[80,3712]{1,0:T(8,128)(2,1)S(1)} %copy-done.44), channel_id=1, source_target_pairs={{0,1},{1,0},{2,3},{3,2},{4,5},{5,4},{6,7},{7,6},{8,9},{9,8},{10,11... | collective-permute-start | bytes 1781768 | tf_op jit(solution)/shard_map/ppermute | solution.py:45
  362.9 30.0 %collective-permute-start.51 = (bf16[80,3712]{1,0:T(8,128)(2,1)S(1)}, bf16[80,3712]{1,0:T(8,128)(2,1)S(1)}, u32[]{:S(2)}, u32[]{:S(2)}) collective-permute-start(bf16[80,3712]{1,0:T(8,128)(2,1)S(1)} %copy-done.43), channel_id=1, source_target_pairs={{0,2},{1,3},{2,0},{3,1},{4,6},{5,7},{6,4},{7,5},{8,10},{9,11},{10,... | collective-permute-start | bytes 1781768 | tf_op jit(solution)/shard_map/ppermute | solution.py:45
  364.6 28.2 %collective-permute-start.52 = (bf16[80,3712]{1,0:T(8,128)(2,1)S(1)}, bf16[80,3712]{1,0:T(8,128)(2,1)S(1)}, u32[]{:S(2)}, u32[]{:S(2)}) collective-permute-start(bf16[80,3712]{1,0:T(8,128)(2,1)S(1)} %copy-done.42), channel_id=1, source_target_pairs={{0,3},{1,2},{2,1},{3,0},{4,7},{5,6},{6,5},{7,4},{8,11},{9,10},{10,... | collective-permute-start | bytes 1781768 | tf_op jit(solution)/shard_map/ppermute | solution.py:45
  401.0 27.9 %collective-permute-start.58 = (bf16[80,3712]{1,0:T(8,128)(2,1)S(1)}, bf16[80,3712]{1,0:T(8,128)(2,1)S(1)}, u32[]{:S(2)}, u32[]{:S(2)}) collective-permute-start(bf16[80,3712]{1,0:T(8,128)(2,1)S(1)} %get-tuple-element.361), channel_id=1, source_target_pairs={{0,2},{1,3},{2,0},{3,1},{4,6},{5,7},{6,4},{7,5},{8,10},{9,11},{10,... | collective-permute-start | bytes 1781768 | tf_op jit(solution)/shard_map/ppermute | solution.py:45
  402.7 26.2 %collective-permute-start.59 = (bf16[80,3712]{1,0:T(8,128)(2,1)S(1)}, bf16[80,3712]{1,0:T(8,128)(2,1)S(1)}, u32[]{:S(2)}, u32[]{:S(2)}) collective-permute-start(bf16[80,3712]{1,0:T(8,128)(2,1)S(1)} %get-tuple-element.362), channel_id=1, source_target_pairs={{0,3},{1,2},{2,1},{3,0},{4,7},{5,6},{6,5},{7,4},{8,11},{9,10},{10,... | collective-permute-start | bytes 1781768 | tf_op jit(solution)/shard_map/ppermute | solution.py:45
  404.1 26.2 %collective-permute-start.56 = (bf16[128,3712]{0,1:T(8,128)(2,1)S(1)}, bf16[128,3712]{0,1:T(8,128)(2,1)S(1)}, u32[]{:S(2)}, u32[]{:S(2)}) collective-permute-start(bf16[128,3712]{0,1:T(8,128)(2,1)S(1)} %fusion.25), channel_id=1, source_target_pairs={{0,4},{1,5},{2,6},{3,7},{12,8},{13,9},{14,10},{15,11},{16,20},{17,... | collective-permute-start | bytes 2850824 | tf_op jit(solution)/shard_map/ppermute | solution.py:39
  437.6 27.9 %collective-permute-start.66 = (bf16[80,3712]{1,0:T(8,128)(2,1)S(1)}, bf16[80,3712]{1,0:T(8,128)(2,1)S(1)}, u32[]{:S(2)}, u32[]{:S(2)}) collective-permute-start(bf16[80,3712]{1,0:T(8,128)(2,1)S(1)} %get-tuple-element.374), channel_id=1, source_target_pairs={{0,2},{1,3},{2,0},{3,1},{4,6},{5,7},{6,4},{7,5},{8,10},{9,11},{10,... | collective-permute-start | bytes 1781768 | tf_op jit(solution)/shard_map/ppermute | solution.py:45
  439.2 26.3 %collective-permute-start.63 = (bf16[128,3712]{0,1:T(8,128)(2,1)S(1)}, bf16[128,3712]{0,1:T(8,128)(2,1)S(1)}, u32[]{:S(2)}, u32[]{:S(2)}) collective-permute-start(bf16[128,3712]{0,1:T(8,128)(2,1)S(1)} %add_convert_fusion.1), channel_id=1, source_target_pairs={{4,8},{5,9},{6,10},{7,11},{8,4},{9,5},{10,6},{11,7},{20,24},{21,25... | collective-permute-start | bytes 2850824 | tf_op jit(solution)/shard_map/ppermute | solution.py:39
  439.9 27.4 %collective-permute-start.64 = (bf16[128,3712]{0,1:T(8,128)(2,1)S(1)}, bf16[128,3712]{0,1:T(8,128)(2,1)S(1)}, u32[]{:S(2)}, u32[]{:S(2)}) collective-permute-start(bf16[128,3712]{0,1:T(8,128)(2,1)S(1)} %fusion.24), channel_id=1, source_target_pairs={{0,4},{1,5},{2,6},{3,7},{12,8},{13,9},{14,10},{15,11},{16,20},{17,... | collective-permute-start | bytes 2850824 | tf_op jit(solution)/shard_map/ppermute | solution.py:39
  472.5 32.8 %collective-permute-start.71 = (bf16[128,3712]{0,1:T(8,128)(2,1)}, bf16[128,3712]{0,1:T(8,128)(2,1)}, u32[]{:S(2)}, u32[]{:S(2)}) collective-permute-start(bf16[128,3712]{0,1:T(8,128)(2,1)} %add_convert_fusion), channel_id=1, source_target_pairs={{4,8},{5,9},{6,10},{7,11},{8,4},{9,5},{10,6},{11,7},{20,24},{21,25... | collective-permute-start | bytes 2850824 | tf_op jit(solution)/shard_map/ppermute | solution.py:39
  474.2 31.2 %collective-permute-start.72 = (bf16[128,3712]{0,1:T(8,128)(2,1)}, bf16[128,3712]{0,1:T(8,128)(2,1)}, u32[]{:S(2)}, u32[]{:S(2)}) collective-permute-start(bf16[128,3712]{0,1:T(8,128)(2,1)} %fusion.12), channel_id=1, source_target_pairs={{0,4},{1,5},{2,6},{3,7},{4,0},{5,1},{6,2},{7,3},{8,12},{9,13},{10,... | collective-permute-start | bytes 2850824 | tf_op jit(solution)/shard_map/ppermute | solution.py:39
  (149 other events, 1639.0 us)

commit v6 on v5

--- a/solution.py
+++ b/solution.py
@@ -394,16 +394,16 @@
     )
     rows_own = from_plane(own_packed, arrived)
 
-    *arrived, (near_blocks, pre_own) = step.run(
+    *arrived, near_blocks = step.run(
         to_plane(blocks),
+        lambda pre, back: expert_rows(*pre, back),
+        (pre_near, back_near),
+    )
+    far_sum = relay_sum(hot_far, normed_far[:, slice_width:], from_plane(blocks, arrived))
+    inward, *arrived, (partner_blocks, pre_own) = step.run(
+        [(far_sum.astype(bf16), INWARD)] + to_plane(near_blocks),
         lambda pre, back, rows: (expert_rows(*pre, back), gate_up(rows)),
-        (pre_near, back_near, rows_own),
-    )
-    far_sum = relay_sum(hot_far, normed_far[:, slice_width:], from_plane(blocks, arrived))
-    inward, *arrived, partner_blocks = step.run(
-        [(far_sum.astype(bf16), INWARD)] + to_plane(near_blocks),
-        lambda pre, back: expert_rows(*pre, back),
-        (pre_partner, back_partner),
+        (pre_partner, back_partner, rows_own),
     )
     far_sum = (far_sum + inward).astype(bf16)
     near_sum = relay_sum(hot_near, normed_near[:, slice_width:], from_plane(near_blocks, arrived))

time: 571 us -> 577 us (1.011)
  waiting for transfers between devices: 256 us -> 273 us
  local copies, waits for them, and re-layouts: 62 us -> 52.1 us
    unnamed x183 -> x221, local copies, waits for them, and re-layouts: 40 us -> 29.5 us
    ppermute x48, waiting for transfers between devices: 203 us -> 213 us  [plane_permute(): return lax.ppermute(x, 'ep', [(i, i ^ step) for i in range(n_ep)])]
    ppermute x20, waiting for transfers between devices: 41.1 us -> 47.7 us  [depth_permute(): lax.ppermute(x, 'ep', [(a * plane + i, b * plane + i) for a, b in pairs f...]
  transfers between devices with their start and end apart: 84 -> 84, of which waited for: 41 -> 44; matrix products, arithmetic and copies ran while one was open for 4% -> 4% of each run, Pallas kernels for 12% -> 12%
where the time goes in v6:
time: 577 us; the launch traced here: 567 us
  waiting for transfers between devices  273 us (47%)
  starting transfers between devices  102 us (18%)
  Pallas kernels  69.1 us (12%)
  local copies, waits for them, and re-layouts  52.1 us (9%)
  other arithmetic  37.8 us (7%)
  matrix products  30 us (5%)
    ppermute x48, waiting for transfers between devices, plane_permute(): return lax.ppermute(x, 'ep', [(i, i ^ step) for i in range(n_ep)])  213 us
    ppermute x48, starting transfers between devices, plane_permute(): return lax.ppermute(x, 'ep', [(i, i ^ step) for i in range(n_ep)])  55.7 us
    ppermute x20, waiting for transfers between devices, depth_permute(): lax.ppermute(x, 'ep', [(a * plane + i, b * plane + i) for a, b in pairs f...  47.7 us
    ppermute x20, starting transfers between devices, depth_permute(): lax.ppermute(x, 'ep', [(a * plane + i, b * plane + i) for a, b in pairs f...  43.7 us
    pallas_call x8, Pallas kernels, summed_products(): pl.pallas_call(summed_kernel, grid=(height // tile,), in_specs=[whole(x)...  38.8 us
    pallas_call x4, Pallas kernels, products(): pl.pallas_call(products_kernel, grid=(width // tile,), in_specs=[whole(ro...  30.3 us
    unnamed x221, local copies, waits for them, and re-layouts  29.5 us
    ppermute x16, waiting for transfers between devices, tp_swap(): return lax.ppermute(x, 'tp', [(0, 1), (1, 0)])  12.1 us
  transfers between devices with their start and end apart: 84, of which 44 were waited for; matrix products, arithmetic and copies ran while one was open for 4% of the time, Pallas kernels for 12%

profile of v6, /device:TPU:0, one launch (start us, length us, event | category | flops | bytes accessed | tf_op | source)
XLA Modules:
  0.0 567.4 jit_solution(15300711698480048965)
XLA Ops:
  11.2 15.6 %collective-permute-done = bf16[2048,224]{0,1:T(8,128)(2,1)} collective-permute-done((bf16[2048,224]{0,1:T(8,128)(2,1)}, bf16[2048,224]{0,1:T(8,128)(2,1)}, u32[]{:S(2)}, u32[]{:S(2)}) %collective-permute-start) | collective-permute-done | bytes 917536 | tf_op jit(solution)/shard_map/ppermute | solution.py:39
  41.0 17.2 %collective-permute-done.3 = bf16[2048,224]{0,1:T(8,128)(2,1)S(1)} collective-permute-done((bf16[2048,224]{0,1:T(8,128)(2,1)}, bf16[2048,224]{0,1:T(8,128)(2,1)S(1)}, u32[]{:S(2)}, u32[]{:S(2)}) %collective-permute-start.3) | collective-permute-done | bytes 917536 | tf_op jit(solution)/shard_map/ppermute | solution.py:39
  67.9 10.7 %collective-permute-done.8 = bf16[80,3584]{1,0:T(8,128)(2,1)S(1)} collective-permute-done((bf16[80,3584]{1,0:T(8,128)(2,1)S(1)}, bf16[80,3584]{1,0:T(8,128)(2,1)S(1)}, u32[]{:S(2)}, u32[]{:S(2)}) %collective-permute-start.8) | collective-permute-done | bytes 573472 | tf_op jit(solution)/shard_map/ppermute | solution.py:45
  78.7 13.1 %collective-permute-done.9 = bf16[80,3584]{1,0:T(8,128)(2,1)S(1)} collective-permute-done((bf16[80,3584]{1,0:T(8,128)(2,1)S(1)}, bf16[80,3584]{1,0:T(8,128)(2,1)S(1)}, u32[]{:S(2)}, u32[]{:S(2)}) %collective-permute-start.9) | collective-permute-done | bytes 573472 | tf_op jit(solution)/shard_map/ppermute | solution.py:45
  138.4 9.5 %collective-permute-done.18 = bf16[80,3584]{1,0:T(8,128)(2,1)S(1)} collective-permute-done((bf16[80,3584]{1,0:T(8,128)(2,1)S(1)}, bf16[80,3584]{1,0:T(8,128)(2,1)S(1)}, u32[]{:S(2)}, u32[]{:S(2)}) %collective-permute-start.18) | collective-permute-done | bytes 573472 | tf_op jit(solution)/shard_map/ppermute | solution.py:45
  147.9 10.9 %collective-permute-done.19 = bf16[80,3584]{1,0:T(8,128)(2,1)S(1)} collective-permute-done((bf16[80,3584]{1,0:T(8,128)(2,1)S(1)}, bf16[80,3584]{1,0:T(8,128)(2,1)S(1)}, u32[]{:S(2)}, u32[]{:S(2)}) %collective-permute-start.19) | collective-permute-done | bytes 573472 | tf_op jit(solution)/shard_map/ppermute | solution.py:45
  185.0 10.3 %collective-permute-done.25 = bf16[80,3584]{1,0:T(8,128)(2,1)S(1)} collective-permute-done((bf16[80,3584]{1,0:T(8,128)(2,1)S(1)}, bf16[80,3584]{1,0:T(8,128)(2,1)S(1)}, u32[]{:S(2)}, u32[]{:S(2)}) %collective-permute-start.25) | collective-permute-done | bytes 573472 | tf_op jit(solution)/shard_map/ppermute | solution.py:45
  206.1 8.3 %collective-permute-done.29 = bf16[80,3584]{1,0:T(8,128)(2,1)S(1)} collective-permute-done((bf16[80,3584]{1,0:T(8,128)(2,1)S(1)}, bf16[80,3584]{1,0:T(8,128)(2,1)S(1)}, u32[]{:S(2)}, u32[]{:S(2)}) %collective-permute-start.29) | collective-permute-done | bytes 573472 | tf_op jit(solution)/shard_map/ppermute | solution.py:45
  214.5 8.4 %collective-permute-done.30 = bf16[80,3584]{1,0:T(8,128)(2,1)S(1)} collective-permute-done((bf16[80,3584]{1,0:T(8,128)(2,1)S(1)}, bf16[80,3584]{1,0:T(8,128)(2,1)S(1)}, u32[]{:S(2)}, u32[]{:S(2)}) %collective-permute-start.30) | collective-permute-done | bytes 573472 | tf_op jit(solution)/shard_map/ppermute | solution.py:45
  233.5 7.5 %shard_map.150 = (bf16[320,1024]{1,0:T(8,128)(2,1)S(1)}, bf16[320,1024]{1,0:T(8,128)(2,1)S(1)}) custom-call(bf16[320,3584]{1,0:T(8,128)(2,1)S(1)} %pad_maximum_fusion.12.rows_ref, bf16[3584,1024]{1,0:T(8,128)(2,1)S(1)} %bitcast.351, bf16[3584,1024]{1,0:T(8,128)(2,1)S(1)} %bitcast.367), custom_call_target="tpu_custom_call" | custom-call | flops 1048576 | bytes 65536 | tf_op jit(solution)/shard_map/pallas_call | solution.py:74
  245.9 8.3 %collective-permute-done.35 = bf16[80,3584]{1,0:T(8,128)(2,1)S(1)} collective-permute-done((bf16[80,3584]{1,0:T(8,128)(2,1)S(1)}, bf16[80,3584]{1,0:T(8,128)(2,1)S(1)}, u32[]{:S(2)}, u32[]{:S(2)}) %collective-permute-start.35) | collective-permute-done | bytes 573472 | tf_op jit(solution)/shard_map/ppermute | solution.py:45
  268.4 7.7 %shard_map.151 = (bf16[320,1024]{1,0:T(8,128)(2,1)S(1)}, bf16[320,1024]{1,0:T(8,128)(2,1)S(1)}) custom-call(bf16[320,3584]{1,0:T(8,128)(2,1)S(1)} %pad_maximum_fusion.13.rows_ref, bf16[3584,1024]{1,0:T(8,128)(2,1)S(1)} %bitcast.352, bf16[3584,1024]{1,0:T(8,128)(2,1)S(1)} %bitcast.368), custom_call_target="tpu_custom_call" | custom-call | flops 1048576 | bytes 65536 | tf_op jit(solution)/shard_map/pallas_call | solution.py:74
  292.6 7.6 %shard_map.152 = (bf16[320,1024]{1,0:T(8,128)(2,1)S(1)}, bf16[320,1024]{1,0:T(8,128)(2,1)S(1)}) custom-call(bf16[320,3584]{1,0:T(8,128)(2,1)S(1)} %pad_maximum_fusion.14.rows_ref, bf16[3584,1024]{1,0:T(8,128)(2,1)S(1)} %bitcast.355, bf16[3584,1024]{1,0:T(8,128)(2,1)S(1)} %bitcast.371), custom_call_target="tpu_custom_call" | custom-call | flops 1048576 | bytes 65536 | tf_op jit(solution)/shard_map/pallas_call | solution.py:74
  303.6 6.6 %collective-permute-done.42 = bf16[80,3584]{1,0:T(8,128)(2,1)S(1)} collective-permute-done((bf16[80,3584]{1,0:T(8,128)(2,1)S(1)}, bf16[80,3584]{1,0:T(8,128)(2,1)S(1)}, u32[]{:S(2)}, u32[]{:S(2)}) %collective-permute-start.42) | collective-permute-done | bytes 573472 | tf_op jit(solution)/shard_map/ppermute | solution.py:45
  337.0 12.9 %collective-permute-done.45 = bf16[80,3584]{1,0:T(8,128)(2,1)S(1)} collective-permute-done((bf16[80,3584]{1,0:T(8,128)(2,1)S(1)}, bf16[80,3584]{1,0:T(8,128)(2,1)S(1)}, u32[]{:S(2)}, u32[]{:S(2)}) %collective-permute-start.45) | collective-permute-done | bytes 573472 | tf_op jit(solution)/shard_map/ppermute | solution.py:45
  369.5 6.7 %shard_map.155 = bf16[320,3584]{1,0:T(8,128)(2,1)S(1)} custom-call(bf16[320,1024]{1,0:T(8,128)(2,1)S(1)} %get-tuple-element.506.refs_0_, bf16[320,1024]{1,0:T(8,128)(2,1)S(1)} %get-tuple-element.505.refs_1_, bf16[3584,1024]{1,0:T(8,128)(2,1)S(1)} %bitcast.361, bf16[3584,1024]{1,0:T(8,128)(2,1)S(1)} %bitcast.373), custom_call_target="tpu_custom_call" | custom-call | flops 1048576 | bytes 65536 | tf_op jit(solution)/shard_map/pallas_call | solution.py:103
  378.7 13.4 %collective-permute-done.51 = bf16[80,3712]{1,0:T(8,128)(2,1)S(1)} collective-permute-done((bf16[80,3712]{1,0:T(8,128)(2,1)S(1)}, bf16[80,3712]{1,0:T(8,128)(2,1)S(1)}, u32[]{:S(2)}, u32[]{:S(2)}) %collective-permute-start.51) | collective-permute-done | bytes 593952 | tf_op jit(solution)/shard_map/ppermute | solution.py:45
  403.7 7.5 %shard_map.157 = (bf16[320,1024]{1,0:T(8,128)(2,1)S(1)}, bf16[320,1024]{1,0:T(8,128)(2,1)S(1)}) custom-call(bf16[320,3584]{1,0:T(8,128)(2,1)S(1)} %pad_maximum_fusion.16.rows_ref, bf16[3584,1024]{1,0:T(8,128)(2,1)S(1)} %bitcast.362, bf16[3584,1024]{1,0:T(8,128)(2,1)S(1)} %bitcast.376), custom_call_target="tpu_custom_call" | custom-call | flops 1048576 | bytes 65536 | tf_op jit(solution)/shard_map/pallas_call | solution.py:74
  428.8 8.7 %collective-permute-done.56 = bf16[128,3712]{0,1:T(8,128)(2,1)S(1)} collective-permute-done((bf16[128,3712]{0,1:T(8,128)(2,1)S(1)}, bf16[128,3712]{0,1:T(8,128)(2,1)S(1)}, u32[]{:S(2)}, u32[]{:S(2)}) %collective-permute-start.56) | collective-permute-done | bytes 950304 | tf_op jit(solution)/shard_map/ppermute | solution.py:39
  447.0 7.0 %collective-permute-start.64 = (bf16[128,3712]{0,1:T(8,128)(2,1)S(1)}, bf16[128,3712]{0,1:T(8,128)(2,1)S(1)}, u32[]{:S(2)}, u32[]{:S(2)}) collective-permute-start(bf16[128,3712]{0,1:T(8,128)(2,1)S(1)} %fusion.24), channel_id=1, source_target_pairs={{0,4},{1,5},{2,6},{3,7},{12,8},{13,9},{14,10},{15,11},{16,20},{17,... | collective-permute-start | bytes 2850824 | tf_op jit(solution)/shard_map/ppermute | solution.py:39
  456.1 6.5 %shard_map.158 = bf16[320,3584]{1,0:T(8,128)(2,1)S(1)} custom-call(bf16[320,1024]{1,0:T(8,128)(2,1)S(1)} %get-tuple-element.498.refs_0_, bf16[320,1024]{1,0:T(8,128)(2,1)S(1)} %get-tuple-element.497.refs_1_, bf16[3584,1024]{1,0:T(8,128)(2,1)S(1)} %bitcast.364, bf16[3584,1024]{1,0:T(8,128)(2,1)S(1)} %bitcast.378), custom_call_target="tpu_custom_call" | custom-call | flops 1048576 | bytes 65536 | tf_op jit(solution)/shard_map/pallas_call | solution.py:103
  462.7 10.1 %collective-permute-done.66 = bf16[80,3712]{1,0:T(8,128)(2,1)S(1)} collective-permute-done((bf16[80,3712]{1,0:T(8,128)(2,1)S(1)}, bf16[80,3712]{1,0:T(8,128)(2,1)S(1)}, u32[]{:S(2)}, u32[]{:S(2)}) %collective-permute-start.66) | collective-permute-done | bytes 593952 | tf_op jit(solution)/shard_map/ppermute | solution.py:45
  487.5 13.0 %collective-permute-done.73 = bf16[80,3712]{1,0:T(8,128)(2,1)S(1)} collective-permute-done((bf16[80,3712]{1,0:T(8,128)(2,1)}, bf16[80,3712]{1,0:T(8,128)(2,1)S(1)}, u32[]{:S(2)}, u32[]{:S(2)}) %collective-permute-start.73) | collective-permute-done | bytes 593952 | tf_op jit(solution)/shard_map/ppermute | solution.py:45
  500.5 11.2 %collective-permute-done.74 = bf16[80,3712]{1,0:T(8,128)(2,1)S(1)} collective-permute-done((bf16[80,3712]{1,0:T(8,128)(2,1)}, bf16[80,3712]{1,0:T(8,128)(2,1)S(1)}, u32[]{:S(2)}, u32[]{:S(2)}) %collective-permute-start.74) | collective-permute-done | bytes 593952 | tf_op jit(solution)/shard_map/ppermute | solution.py:45
  (585 shorter events, 325.4 us)
Async XLA Ops:
  31.1 27.2 %collective-permute-start.3 = (bf16[2048,224]{0,1:T(8,128)(2,1)}, bf16[2048,224]{0,1:T(8,128)(2,1)S(1)}, u32[]{:S(2)}, u32[]{:S(2)}) collective-permute-start(bf16[2048,224]{0,1:T(8,128)(2,1)} %collective-permute-done.1), channel_id=1, source_target_pairs={{4,0},{5,1},{6,2},{7,3},{8,12},{9,13},{10,14},{11,15},{20,16},{21,... | collective-permute-start | bytes 2752520 | tf_op jit(solution)/shard_map/ppermute | solution.py:39
  59.5 32.2 %collective-permute-start.7 = (bf16[2048,224]{0,1:T(8,128)(2,1)S(1)}, bf16[2048,224]{0,1:T(8,128)(2,1)}, u32[]{:S(2)}, u32[]{:S(2)}) collective-permute-start(bf16[2048,224]{0,1:T(8,128)(2,1)S(1)} %collective-permute-done.2), channel_id=1, source_target_pairs={{4,0},{5,1},{6,2},{7,3},{8,12},{9,13},{10,14},{11,15},{20,16},{21,... | collective-permute-start | bytes 2752520 | tf_op jit(solution)/shard_map/ppermute | solution.py:39
  64.4 27.4 %collective-permute-start.9 = (bf16[80,3584]{1,0:T(8,128)(2,1)S(1)}, bf16[80,3584]{1,0:T(8,128)(2,1)S(1)}, u32[]{:S(2)}, u32[]{:S(2)}) collective-permute-start(bf16[80,3584]{1,0:T(8,128)(2,1)S(1)} %copy-done.63), channel_id=1, source_target_pairs={{0,2},{1,3},{2,0},{3,1},{4,6},{5,7},{6,4},{7,5},{8,10},{9,11},{10,... | collective-permute-start | bytes 1720328 | tf_op jit(solution)/shard_map/ppermute | solution.py:45
  134.1 26.5 %collective-permute-start.20 = (bf16[80,3584]{1,0:T(8,128)(2,1)S(1)}, bf16[80,3584]{1,0:T(8,128)(2,1)S(1)}, u32[]{:S(2)}, u32[]{:S(2)}) collective-permute-start(bf16[80,3584]{1,0:T(8,128)(2,1)S(1)} %copy-done.64), channel_id=1, source_target_pairs={{0,3},{1,2},{2,1},{3,0},{4,7},{5,6},{6,5},{7,4},{8,11},{9,10},{10,... | collective-permute-start | bytes 1720328 | tf_op jit(solution)/shard_map/ppermute | solution.py:45
  165.2 30.1 %collective-permute-start.22 = (bf16[128,3712]{0,1:T(8,128)(2,1)S(1)}, bf16[128,3712]{0,1:T(8,128)(2,1)S(1)}, u32[]{:S(2)}, u32[]{:S(2)}) collective-permute-start(bf16[128,3712]{0,1:T(8,128)(2,1)S(1)} %pad_maximum_fusion.25), channel_id=1, source_target_pairs={{0,4},{1,5},{2,6},{3,7},{4,0},{5,1},{6,2},{7,3},{8,12},{9,13},{10,... | collective-permute-start | bytes 2850824 | tf_op jit(solution)/shard_map/ppermute | solution.py:39
  168.3 27.0 %collective-permute-start.23 = (bf16[128,3712]{0,1:T(8,128)(2,1)S(1)}, bf16[128,3712]{0,1:T(8,128)(2,1)S(1)}, u32[]{:S(2)}, u32[]{:S(2)}) collective-permute-start(bf16[128,3712]{0,1:T(8,128)(2,1)S(1)} %pad_maximum_fusion.25), channel_id=1, source_target_pairs={{4,8},{5,9},{6,10},{7,11},{8,4},{9,5},{10,6},{11,7},{20,24},{21,25... | collective-permute-start | bytes 2850824 | tf_op jit(solution)/shard_map/ppermute | solution.py:39
  196.5 28.2 %collective-permute-start.27 = (bf16[128,3712]{0,1:T(8,128)(2,1)S(1)}, bf16[128,3712]{0,1:T(8,128)(2,1)S(1)}, u32[]{:S(2)}, u32[]{:S(2)}) collective-permute-start(bf16[128,3712]{0,1:T(8,128)(2,1)S(1)} %collective-permute-done.22), channel_id=1, source_target_pairs={{4,8},{5,9},{6,10},{7,11},{8,4},{9,5},{10,6},{11,7},{20,24},{21,25... | collective-permute-start | bytes 2850824 | tf_op jit(solution)/shard_map/ppermute | solution.py:39
  197.2 27.5 %collective-permute-start.28 = (bf16[128,3712]{0,1:T(8,128)(2,1)S(1)}, bf16[128,3712]{0,1:T(8,128)(2,1)S(1)}, u32[]{:S(2)}, u32[]{:S(2)}) collective-permute-start(bf16[128,3712]{0,1:T(8,128)(2,1)S(1)} %collective-permute-done.23), channel_id=1, source_target_pairs={{4,0},{5,1},{6,2},{7,3},{8,12},{9,13},{10,14},{11,15},{20,16},{21,... | collective-permute-start | bytes 2850824 | tf_op jit(solution)/shard_map/ppermute | solution.py:39
  227.0 27.3 %collective-permute-start.32 = (bf16[128,3712]{0,1:T(8,128)(2,1)S(1)}, bf16[128,3712]{0,1:T(8,128)(2,1)S(1)}, u32[]{:S(2)}, u32[]{:S(2)}) collective-permute-start(bf16[128,3712]{0,1:T(8,128)(2,1)S(1)} %collective-permute-done.27), channel_id=1, source_target_pairs={{4,0},{5,1},{6,2},{7,3},{8,12},{9,13},{10,14},{11,15},{20,16},{21,... | collective-permute-start | bytes 2850824 | tf_op jit(solution)/shard_map/ppermute | solution.py:39
  228.4 25.9 %collective-permute-start.33 = (bf16[128,3712]{0,1:T(8,128)(2,1)}, bf16[128,3712]{0,1:T(8,128)(2,1)}, u32[]{:S(2)}, u32[]{:S(2)}) collective-permute-start(bf16[128,3712]{0,1:T(8,128)(2,1)} %collective-permute-done.12), channel_id=1, source_target_pairs={{4,8},{5,9},{6,10},{7,11},{8,4},{9,5},{10,6},{11,7},{20,24},{21,25... | collective-permute-start | bytes 2850824 | tf_op jit(solution)/shard_map/ppermute | solution.py:39
  257.3 25.9 %collective-permute-start.37 = (bf16[128,3712]{0,1:T(8,128)(2,1)}, bf16[128,3712]{0,1:T(8,128)(2,1)}, u32[]{:S(2)}, u32[]{:S(2)}) collective-permute-start(bf16[128,3712]{0,1:T(8,128)(2,1)} %collective-permute-done.33), channel_id=1, source_target_pairs={{4,0},{5,1},{6,2},{7,3},{8,12},{9,13},{10,14},{11,15},{20,16},{21,... | collective-permute-start | bytes 2850824 | tf_op jit(solution)/shard_map/ppermute | solution.py:39
  322.8 27.0 %collective-permute-start.45 = (bf16[80,3584]{1,0:T(8,128)(2,1)S(1)}, bf16[80,3584]{1,0:T(8,128)(2,1)S(1)}, u32[]{:S(2)}, u32[]{:S(2)}) collective-permute-start(bf16[80,3584]{1,0:T(8,128)(2,1)S(1)} %copy-done.60), channel_id=1, source_target_pairs={{0,2},{1,3},{2,0},{3,1},{4,6},{5,7},{6,4},{7,5},{8,10},{9,11},{10,... | collective-permute-start | bytes 1720328 | tf_op jit(solution)/shard_map/ppermute | solution.py:45
  323.1 26.7 %collective-permute-start.46 = (bf16[80,3584]{1,0:T(8,128)(2,1)S(1)}, bf16[80,3584]{1,0:T(8,128)(2,1)S(1)}, u32[]{:S(2)}, u32[]{:S(2)}) collective-permute-start(bf16[80,3584]{1,0:T(8,128)(2,1)S(1)} %copy-done.59), channel_id=1, source_target_pairs={{0,3},{1,2},{2,1},{3,0},{4,7},{5,6},{6,5},{7,4},{8,11},{9,10},{10,... | collective-permute-start | bytes 1720328 | tf_op jit(solution)/shard_map/ppermute | solution.py:45
  363.6 28.6 %collective-permute-start.51 = (bf16[80,3712]{1,0:T(8,128)(2,1)S(1)}, bf16[80,3712]{1,0:T(8,128)(2,1)S(1)}, u32[]{:S(2)}, u32[]{:S(2)}) collective-permute-start(bf16[80,3712]{1,0:T(8,128)(2,1)S(1)} %copy-done.45), channel_id=1, source_target_pairs={{0,2},{1,3},{2,0},{3,1},{4,6},{5,7},{6,4},{7,5},{8,10},{9,11},{10,... | collective-permute-start | bytes 1781768 | tf_op jit(solution)/shard_map/ppermute | solution.py:45
  364.6 27.5 %collective-permute-start.52 = (bf16[80,3712]{1,0:T(8,128)(2,1)S(1)}, bf16[80,3712]{1,0:T(8,128)(2,1)S(1)}, u32[]{:S(2)}, u32[]{:S(2)}) collective-permute-start(bf16[80,3712]{1,0:T(8,128)(2,1)S(1)} %copy-done.44), channel_id=1, source_target_pairs={{0,3},{1,2},{2,1},{3,0},{4,7},{5,6},{6,5},{7,4},{8,11},{9,10},{10,... | collective-permute-start | bytes 1781768 | tf_op jit(solution)/shard_map/ppermute | solution.py:45
  400.9 27.9 %collective-permute-start.58 = (bf16[80,3712]{1,0:T(8,128)(2,1)S(1)}, bf16[80,3712]{1,0:T(8,128)(2,1)S(1)}, u32[]{:S(2)}, u32[]{:S(2)}) collective-permute-start(bf16[80,3712]{1,0:T(8,128)(2,1)S(1)} %get-tuple-element.356), channel_id=1, source_target_pairs={{0,2},{1,3},{2,0},{3,1},{4,6},{5,7},{6,4},{7,5},{8,10},{9,11},{10,... | collective-permute-start | bytes 1781768 | tf_op jit(solution)/shard_map/ppermute | solution.py:45
  402.4 26.4 %collective-permute-start.59 = (bf16[80,3712]{1,0:T(8,128)(2,1)S(1)}, bf16[80,3712]{1,0:T(8,128)(2,1)S(1)}, u32[]{:S(2)}, u32[]{:S(2)}) collective-permute-start(bf16[80,3712]{1,0:T(8,128)(2,1)S(1)} %get-tuple-element.357), channel_id=1, source_target_pairs={{0,3},{1,2},{2,1},{3,0},{4,7},{5,6},{6,5},{7,4},{8,11},{9,10},{10,... | collective-permute-start | bytes 1781768 | tf_op jit(solution)/shard_map/ppermute | solution.py:45
  411.3 26.1 %collective-permute-start.56 = (bf16[128,3712]{0,1:T(8,128)(2,1)S(1)}, bf16[128,3712]{0,1:T(8,128)(2,1)S(1)}, u32[]{:S(2)}, u32[]{:S(2)}) collective-permute-start(bf16[128,3712]{0,1:T(8,128)(2,1)S(1)} %fusion.25), channel_id=1, source_target_pairs={{0,4},{1,5},{2,6},{3,7},{12,8},{13,9},{14,10},{15,11},{16,20},{17,... | collective-permute-start | bytes 2850824 | tf_op jit(solution)/shard_map/ppermute | solution.py:39
  444.9 27.9 %collective-permute-start.66 = (bf16[80,3712]{1,0:T(8,128)(2,1)S(1)}, bf16[80,3712]{1,0:T(8,128)(2,1)S(1)}, u32[]{:S(2)}, u32[]{:S(2)}) collective-permute-start(bf16[80,3712]{1,0:T(8,128)(2,1)S(1)} %get-tuple-element.374), channel_id=1, source_target_pairs={{0,2},{1,3},{2,0},{3,1},{4,6},{5,7},{6,4},{7,5},{8,10},{9,11},{10,... | collective-permute-start | bytes 1781768 | tf_op jit(solution)/shard_map/ppermute | solution.py:45
  446.3 26.6 %collective-permute-start.63 = (bf16[128,3712]{0,1:T(8,128)(2,1)S(1)}, bf16[128,3712]{0,1:T(8,128)(2,1)S(1)}, u32[]{:S(2)}, u32[]{:S(2)}) collective-permute-start(bf16[128,3712]{0,1:T(8,128)(2,1)S(1)} %add_convert_fusion.1), channel_id=1, source_target_pairs={{4,8},{5,9},{6,10},{7,11},{8,4},{9,5},{10,6},{11,7},{20,24},{21,25... | collective-permute-start | bytes 2850824 | tf_op jit(solution)/shard_map/ppermute | solution.py:39
  447.0 26.7 %collective-permute-start.64 = (bf16[128,3712]{0,1:T(8,128)(2,1)S(1)}, bf16[128,3712]{0,1:T(8,128)(2,1)S(1)}, u32[]{:S(2)}, u32[]{:S(2)}) collective-permute-start(bf16[128,3712]{0,1:T(8,128)(2,1)S(1)} %fusion.24), channel_id=1, source_target_pairs={{0,4},{1,5},{2,6},{3,7},{12,8},{13,9},{14,10},{15,11},{16,20},{17,... | collective-permute-start | bytes 2850824 | tf_op jit(solution)/shard_map/ppermute | solution.py:39
  478.8 32.8 %collective-permute-start.71 = (bf16[128,3712]{0,1:T(8,128)(2,1)}, bf16[128,3712]{0,1:T(8,128)(2,1)}, u32[]{:S(2)}, u32[]{:S(2)}) collective-permute-start(bf16[128,3712]{0,1:T(8,128)(2,1)} %add_convert_fusion), channel_id=1, source_target_pairs={{4,8},{5,9},{6,10},{7,11},{8,4},{9,5},{10,6},{11,7},{20,24},{21,25... | collective-permute-start | bytes 2850824 | tf_op jit(solution)/shard_map/ppermute | solution.py:39
  480.5 31.2 %collective-permute-start.72 = (bf16[128,3712]{0,1:T(8,128)(2,1)}, bf16[128,3712]{0,1:T(8,128)(2,1)}, u32[]{:S(2)}, u32[]{:S(2)}) collective-permute-start(bf16[128,3712]{0,1:T(8,128)(2,1)} %fusion.12), channel_id=1, source_target_pairs={{0,4},{1,5},{2,6},{3,7},{4,0},{5,1},{6,2},{7,3},{8,12},{9,13},{10,... | collective-permute-start | bytes 2850824 | tf_op jit(solution)/shard_map/ppermute | solution.py:39
  485.3 26.4 %collective-permute-start.74 = (bf16[80,3712]{1,0:T(8,128)(2,1)}, bf16[80,3712]{1,0:T(8,128)(2,1)S(1)}, u32[]{:S(2)}, u32[]{:S(2)}) collective-permute-start(bf16[80,3712]{1,0:T(8,128)(2,1)} %get-tuple-element.388), channel_id=1, source_target_pairs={{0,2},{1,3},{2,0},{3,1},{4,6},{5,7},{6,4},{7,5},{8,10},{9,11},{10,... | collective-permute-start | bytes 1781768 | tf_op jit(solution)/shard_map/ppermute | solution.py:45
  (168 other events, 1868.7 us)
